TPU v7x, 32 devices: a whole 2x2x4 slice. The times are simulated.
32 devices in a mesh: region: 16 (over z, y, x), band: 2 (over core).
Axes of the slice: x: 2, y: 2, z: 4, core: 2. Of those that a mesh axis runs over, the one named last changes fastest.
Arguments:
- emission: bfloat16 [16384, 192], P(('region', 'band')), may hold values from 0.099609375 to 10
- path_sends: int32 [32, 32, 64], P(('region', 'band')), may hold values from -1 to 511, as said below
- tile_slots: int32 [256, 512], P(('region', 'band')), may hold values from -1 to 2047, as said below
- geometry: bfloat16 [256, 256, 512], P(('region', 'band')), may hold values from 0.00049972534 to 0.0099487305
- absorption: bfloat16 [256, 8, 512], P(('region', 'band')), may hold values from 0.099609375 to 1
- hour_period: int32 [24], replicated, may hold values from 0 to 2
- dwellings: int32 [65536], P(('region', 'band')), may hold values from 1 to 8
- addr_sends: int32 [32, 32, 16], P(('region', 'band')), may hold values from -1 to 2047, as said below
- addr_building: int32 [32, 32, 16], P(('region', 'band')), may hold values from 0 to 2047
Outputs:
- receiver_level: float32 [65536], P(('region', 'band'))
- building_level: float32 [65536], P(('region', 'band'))
- exposure: float32 [65536, 192], P(('region', 'band'))
Inputs may be any that keep to these rules, and one draw needn't show every extreme that they name: path_sends[s, d, c] is a segment of device s or -1; the live entries of each list come first; some destination gets 64 live entries from every source. tile_slots[t, p] names a received slot s * 64 + c of the tile's device whose entry path_sends[s, d, c] is live, or is -1; live entries of a tile come first, at least 256 of them, and some tile of every device has all 512 live; a slot may feed several paths. addr_sends[s, d, c] is a receiver of device s or -1; live entries of each list come first; each receiver is named at most once over all lists; some destination gets 16 live entries from every source.
All inputs are finite; a program needn't handle non-finite values.
Results may differ from a plain program's by a relative error of at most 0.00034.
Values may be sent and summed in bfloat16 or wider, within the bound.
No kernel may reach another device: no remote copies, remote signals or barrier semaphores. Data moves between devices by JAX's collectives and lax.ppermute only.
A program may use at most 64 MiB of HBM per device.

v0:
```python
import math

import jax
import jax.numpy as jnp
from jax import lax
from jax.sharding import PartitionSpec as P

HOURS = 24
BLD_DEV = 2048


A_WEIGHTING_DB = [-26.2, -16.1, -8.6, -3.2, 0.0, 1.2, 1.0, -1.1]


def hour_weights(hour_period):
    a_weight = jnp.power(10.0, jnp.array(A_WEIGHTING_DB, jnp.float32) / 10.0)
    period_gain = jnp.array([1.0, 10.0**0.5, 10.0], jnp.float32)
    matches = hour_period[:, None] == jnp.arange(3, dtype=jnp.int32)[None, :]
    per_hour = jnp.sum(jnp.where(matches, period_gain[None, :], jnp.float32(0.0)), axis=1)
    return (a_weight[:, None] * per_hour[None, :] / HOURS).reshape(-1)


def one_hot_rows(index, extent, kind):
    return (index[:, None] == jnp.arange(extent, dtype=jnp.int32)[None, :]).astype(kind)


def local(
    emission,
    path_sends,
    tile_slots,
    geometry,
    absorption,
    hour_period,
    dwellings,
    addr_sends,
    addr_building,
):
    weights = hour_weights(hour_period)
    width = emission.shape[1]
    seg_count = emission.shape[0]
    send_list = path_sends[0]
    flat_list = send_list.reshape(-1)
    block_rows = math.gcd(flat_list.shape[0], 512)

    def pick_rows(index):
        table = one_hot_rows(index, seg_count, jnp.bfloat16)
        return jnp.dot(table, emission, preferred_element_type=jnp.float32).astype(jnp.bfloat16)

    outgoing = lax.map(pick_rows, flat_list.reshape(-1, block_rows)).reshape(
        send_list.shape + (width,)
    )
    arrived = lax.all_to_all(outgoing, ("region", "band"), split_axis=0, concat_axis=0, tiled=True)
    received = arrived.reshape(-1, width)
    slot_count = received.shape[0]

    def tile_work(items):
        slots, tile_geometry, tile_absorption = items
        table = one_hot_rows(slots, slot_count, jnp.bfloat16)
        gathered = jnp.dot(table, received, preferred_element_type=jnp.float32).astype(jnp.bfloat16)
        factor = jnp.repeat(jnp.swapaxes(tile_absorption, 0, 1), HOURS, axis=1)
        mixed_rows = (factor.astype(jnp.float32) * gathered.astype(jnp.float32)).astype(
            jnp.bfloat16
        )
        return jnp.dot(tile_geometry, mixed_rows, preferred_element_type=jnp.float32)

    exposure = lax.map(tile_work, (tile_slots, geometry, absorption))
    flat_rows = exposure.reshape(-1, width)
    levels = jnp.log10(jnp.dot(flat_rows, weights, precision=lax.Precision.HIGHEST))
    address_list = addr_sends[0]
    recv_count = flat_rows.shape[0]
    select = one_hot_rows(address_list.reshape(-1), recv_count, jnp.float32)
    dwell_weight = jnp.dot(
        select, dwellings.astype(jnp.float32), precision=lax.Precision.HIGHEST
    ).reshape(address_list.shape)
    level_at = jnp.dot(select, levels, precision=lax.Precision.HIGHEST).reshape(address_list.shape)
    weighted_out = dwell_weight * level_at
    weighted_in, dwell_in = (
        lax.all_to_all(weighted_out, ("region", "band"), split_axis=0, concat_axis=0, tiled=True),
        lax.all_to_all(dwell_weight, ("region", "band"), split_axis=0, concat_axis=0, tiled=True),
    )
    building = addr_building[0].reshape(-1)
    owner_table = (jnp.arange(BLD_DEV, dtype=jnp.int32)[:, None] == building[None, :]).astype(
        jnp.float32
    )
    numerator = jnp.dot(owner_table, weighted_in.reshape(-1), precision=lax.Precision.HIGHEST)
    denominator = jnp.dot(owner_table, dwell_in.reshape(-1), precision=lax.Precision.HIGHEST)
    return (levels, numerator / jnp.maximum(denominator, jnp.float32(1.0)), flat_rows)


def solution(mesh):
    in_specs = (
        P(("region", "band"), None),
        P(("region", "band"), None, None),
        P(("region", "band"), None),
        P(("region", "band"), None, None),
        P(("region", "band"), None, None),
        P(),
        P(("region", "band")),
        P(("region", "band"), None, None),
        P(("region", "band"), None, None),
    )
    out_specs = (P(("region", "band")), P(("region", "band")), P(("region", "band"), None))
    return jax.shard_map(local, mesh=mesh, in_specs=in_specs, out_specs=out_specs, check_vma=False)
```

profile of v0, /device:TPU:0, one launch (start us, length us, event | category | flops | bytes accessed | tf_op | source)
XLA Modules:
  0.0 126.5 jit_solution(6517004737073508879)
XLA Ops:
  2.2 2.0 %fusion.15 = f32[1,512]{1,0:T(1,128)S(1)} fusion(f32[2048,1]{0,1:T(1,128)S(1)} %bitcast.70, s32[512]{0:T(512)S(1)} %eq.80), kind=kOutput, calls=%fused_computation.22 | convolution fusion | flops 13631488 | bytes 12288 | tf_op jit(solution)/shard_map/dot_general | solution.py:72
  4.9 7.3 %all-to-all-start.2 = ((f32[32,1,16]{2,1,0:T(1,128)}), f32[32,1,16]{2,1,0:T(1,128)S(1)}, u32[]{:S(2)}, u32[]{:S(2)}) async-start(f32[32,1,16]{2,1,0:T(1,128)} %bitcast.17), calls=%async_computation.2 | async-start | bytes 32768 | tf_op jit(solution)/shard_map/all_to_all | solution.py:79
  13.0 5.7 %while.20 = (s32[]{:T(128)}, bf16[4,512,192]{1,2,0:T(8,128)(2,1)S(1)}, s32[4,512]{1,0:T(4,128)S(1)}, bf16[512,192]{0,1:T(8,128)(2,1)}, s32[]{:T(128)}) while((s32[]{:T(128)}, bf16[4,512,192]{1,2,0:T(8,128)(2,1)S(1)}, s32[4,512]{1,0:T(4,128)S(1)}, bf16[512,192]{0,1:T(8,128)(2,1)}, s32[]{:T(128)}) %tuple.35), condition=%wide.region_1.2_spmd, body=%wide.region_0.1_spmd.sunk | while | flops 101023744 | bytes 399429 | solution.py:49
  13.0 1.4 %fusion.37 = bf16[4,512,192]{1,2,0:T(8,128)(2,1)S(1)} fusion(bf16[4,512,192]{1,2,0:T(8,128)(2,1)S(1)} %get-tuple-element.147, s32[]{:T(128)} %get-tuple-element.146, bf16[512,192]{0,1:T(8,128)(2,1)} %get-tuple-element.154, s32[512]{0:T(512)S(1)} %bitcast.64), kind=kOutput, calls=%fused_computation.2.clone.1 | convolution fusion | flops 101023744 | bytes 395268 | tf_op jit(solution)/shard_map/while/body/eval_jaxpr/dot_general | solution.py:47
  14.4 1.4 %fusion.37 = bf16[4,512,192]{1,2,0:T(8,128)(2,1)S(1)} fusion(bf16[4,512,192]{1,2,0:T(8,128)(2,1)S(1)} %get-tuple-element.147, s32[]{:T(128)} %get-tuple-element.146, bf16[512,192]{0,1:T(8,128)(2,1)} %get-tuple-element.154, s32[512]{0:T(512)S(1)} %bitcast.64), kind=kOutput, calls=%fused_computation.2.clone.1 | convolution fusion | flops 101023744 | bytes 395268 | tf_op jit(solution)/shard_map/while/body/eval_jaxpr/dot_general | solution.py:47
  15.9 1.4 %fusion.37 = bf16[4,512,192]{1,2,0:T(8,128)(2,1)S(1)} fusion(bf16[4,512,192]{1,2,0:T(8,128)(2,1)S(1)} %get-tuple-element.147, s32[]{:T(128)} %get-tuple-element.146, bf16[512,192]{0,1:T(8,128)(2,1)} %get-tuple-element.154, s32[512]{0:T(512)S(1)} %bitcast.64), kind=kOutput, calls=%fused_computation.2.clone.1 | convolution fusion | flops 101023744 | bytes 395268 | tf_op jit(solution)/shard_map/while/body/eval_jaxpr/dot_general | solution.py:47
  17.3 1.4 %fusion.37 = bf16[4,512,192]{1,2,0:T(8,128)(2,1)S(1)} fusion(bf16[4,512,192]{1,2,0:T(8,128)(2,1)S(1)} %get-tuple-element.147, s32[]{:T(128)} %get-tuple-element.146, bf16[512,192]{0,1:T(8,128)(2,1)} %get-tuple-element.154, s32[512]{0:T(512)S(1)} %bitcast.64), kind=kOutput, calls=%fused_computation.2.clone.1 | convolution fusion | flops 101023744 | bytes 395268 | tf_op jit(solution)/shard_map/while/body/eval_jaxpr/dot_general | solution.py:47
  20.0 6.0 %all-to-all-start = ((bf16[32,64,192]{2,1,0:T(8,128)(2,1)}), bf16[32,64,192]{2,1,0:T(8,128)(2,1)}, u32[]{:S(2)}, u32[]{:S(2)}) async-start(bf16[32,64,192]{2,1,0:T(8,128)(2,1)} %bitcast.8), calls=%async_computation | async-start | bytes 2097152 | tf_op jit(solution)/shard_map/all_to_all | solution.py:52
  27.7 24.5 %all-to-all-done = bf16[32,64,192]{2,1,0:T(8,128)(2,1)} async-done(((bf16[32,64,192]{2,1,0:T(8,128)(2,1)}), bf16[32,64,192]{2,1,0:T(8,128)(2,1)}, u32[]{:S(2)}, u32[]{:S(2)}) %all-to-all-start) | async-done | bytes 786464 | tf_op jit(solution)/shard_map/all_to_all | solution.py:52
  52.2 55.2 %while.21 = (s32[]{:T(128)}, f32[8,256,192]{1,0,2:T(8,128)S(1)}, bf16[8,256,512]{2,1,0:T(8,128)(2,1)}, bf16[8,8,512]{2,1,0:T(8,128)(2,1)}, s32[8,512]{1,0:T(8,12...) while((s32[]{:T(128)}, f32[8,256,192]{1,0,2:T(8,128)S(1)}, bf16[8,256,512]{2,1,0:T(8,128)(2,1)}, ...), condition=%wide.region_3.4_spmd, body=%wide.region_2.3_spmd.sunk | while | flops 454430720 | bytes 3127905 | solution.py:66
  53.7 2.6 %fusion.40 = f32[1,256,192]{1,2,0:T(8,128)S(1)} fusion(f32[512,192]{0,1:T(8,128)S(1)} %bitcast.60, bf16[2048,192]{1,0:T(8,128)(2,1)} %get-tuple-element.177, s32[512]{0:T(512)S(1)} %bitcast.65, bf16[8,256,512]{2,1,0:T(8,128)(2,1)} %get-tuple-element.174, s32[]{:T(128)} %get-tuple-element.164), kind=kOutput, calls=%fused_computation.14.clone.1 | convolution fusion | flops 454426624 | bytes 1903104 | tf_op jit(solution)/shard_map/while/body/eval_jaxpr/dot_general | solution.py:64
  56.5 2.6 %dynamic_update_slice.12 = f32[8,256,192]{1,0,2:T(8,128)S(1)} dynamic-update-slice(f32[8,256,192]{1,0,2:T(8,128)S(1)} %get-tuple-element.165, f32[1,256,192]{1,0,2:T(1,128)S(1)} %copy.37, s32[]{:T(128)} %get-tuple-element.164, s32[]{:T(128)} %constant.21.clone.1..sunk, s32[]{:T(128)} %constant.21.clone.1..sunk) | dynamic-update-slice | bytes 393220 | tf_op jit(solution)/shard_map/while/body/jit(dynamic_update_index_in_dim)/dynamic_update_slice | solution.py:66
  60.6 2.6 %fusion.40 = f32[1,256,192]{1,2,0:T(8,128)S(1)} fusion(f32[512,192]{0,1:T(8,128)S(1)} %bitcast.60, bf16[2048,192]{1,0:T(8,128)(2,1)} %get-tuple-element.177, s32[512]{0:T(512)S(1)} %bitcast.65, bf16[8,256,512]{2,1,0:T(8,128)(2,1)} %get-tuple-element.174, s32[]{:T(128)} %get-tuple-element.164), kind=kOutput, calls=%fused_computation.14.clone.1 | convolution fusion | flops 454426624 | bytes 1903104 | tf_op jit(solution)/shard_map/while/body/eval_jaxpr/dot_general | solution.py:64
  63.4 2.6 %dynamic_update_slice.12 = f32[8,256,192]{1,0,2:T(8,128)S(1)} dynamic-update-slice(f32[8,256,192]{1,0,2:T(8,128)S(1)} %get-tuple-element.165, f32[1,256,192]{1,0,2:T(1,128)S(1)} %copy.37, s32[]{:T(128)} %get-tuple-element.164, s32[]{:T(128)} %constant.21.clone.1..sunk, s32[]{:T(128)} %constant.21.clone.1..sunk) | dynamic-update-slice | bytes 393220 | tf_op jit(solution)/shard_map/while/body/jit(dynamic_update_index_in_dim)/dynamic_update_slice | solution.py:66
  67.5 2.6 %fusion.40 = f32[1,256,192]{1,2,0:T(8,128)S(1)} fusion(f32[512,192]{0,1:T(8,128)S(1)} %bitcast.60, bf16[2048,192]{1,0:T(8,128)(2,1)} %get-tuple-element.177, s32[512]{0:T(512)S(1)} %bitcast.65, bf16[8,256,512]{2,1,0:T(8,128)(2,1)} %get-tuple-element.174, s32[]{:T(128)} %get-tuple-element.164), kind=kOutput, calls=%fused_computation.14.clone.1 | convolution fusion | flops 454426624 | bytes 1903104 | tf_op jit(solution)/shard_map/while/body/eval_jaxpr/dot_general | solution.py:64
  70.3 2.6 %dynamic_update_slice.12 = f32[8,256,192]{1,0,2:T(8,128)S(1)} dynamic-update-slice(f32[8,256,192]{1,0,2:T(8,128)S(1)} %get-tuple-element.165, f32[1,256,192]{1,0,2:T(1,128)S(1)} %copy.37, s32[]{:T(128)} %get-tuple-element.164, s32[]{:T(128)} %constant.21.clone.1..sunk, s32[]{:T(128)} %constant.21.clone.1..sunk) | dynamic-update-slice | bytes 393220 | tf_op jit(solution)/shard_map/while/body/jit(dynamic_update_index_in_dim)/dynamic_update_slice | solution.py:66
  74.4 2.6 %fusion.40 = f32[1,256,192]{1,2,0:T(8,128)S(1)} fusion(f32[512,192]{0,1:T(8,128)S(1)} %bitcast.60, bf16[2048,192]{1,0:T(8,128)(2,1)} %get-tuple-element.177, s32[512]{0:T(512)S(1)} %bitcast.65, bf16[8,256,512]{2,1,0:T(8,128)(2,1)} %get-tuple-element.174, s32[]{:T(128)} %get-tuple-element.164), kind=kOutput, calls=%fused_computation.14.clone.1 | convolution fusion | flops 454426624 | bytes 1903104 | tf_op jit(solution)/shard_map/while/body/eval_jaxpr/dot_general | solution.py:64
  77.2 2.6 %dynamic_update_slice.12 = f32[8,256,192]{1,0,2:T(8,128)S(1)} dynamic-update-slice(f32[8,256,192]{1,0,2:T(8,128)S(1)} %get-tuple-element.165, f32[1,256,192]{1,0,2:T(1,128)S(1)} %copy.37, s32[]{:T(128)} %get-tuple-element.164, s32[]{:T(128)} %constant.21.clone.1..sunk, s32[]{:T(128)} %constant.21.clone.1..sunk) | dynamic-update-slice | bytes 393220 | tf_op jit(solution)/shard_map/while/body/jit(dynamic_update_index_in_dim)/dynamic_update_slice | solution.py:66
  81.3 2.6 %fusion.40 = f32[1,256,192]{1,2,0:T(8,128)S(1)} fusion(f32[512,192]{0,1:T(8,128)S(1)} %bitcast.60, bf16[2048,192]{1,0:T(8,128)(2,1)} %get-tuple-element.177, s32[512]{0:T(512)S(1)} %bitcast.65, bf16[8,256,512]{2,1,0:T(8,128)(2,1)} %get-tuple-element.174, s32[]{:T(128)} %get-tuple-element.164), kind=kOutput, calls=%fused_computation.14.clone.1 | convolution fusion | flops 454426624 | bytes 1903104 | tf_op jit(solution)/shard_map/while/body/eval_jaxpr/dot_general | solution.py:64
  84.1 2.6 %dynamic_update_slice.12 = f32[8,256,192]{1,0,2:T(8,128)S(1)} dynamic-update-slice(f32[8,256,192]{1,0,2:T(8,128)S(1)} %get-tuple-element.165, f32[1,256,192]{1,0,2:T(1,128)S(1)} %copy.37, s32[]{:T(128)} %get-tuple-element.164, s32[]{:T(128)} %constant.21.clone.1..sunk, s32[]{:T(128)} %constant.21.clone.1..sunk) | dynamic-update-slice | bytes 393220 | tf_op jit(solution)/shard_map/while/body/jit(dynamic_update_index_in_dim)/dynamic_update_slice | solution.py:66
  88.2 2.6 %fusion.40 = f32[1,256,192]{1,2,0:T(8,128)S(1)} fusion(f32[512,192]{0,1:T(8,128)S(1)} %bitcast.60, bf16[2048,192]{1,0:T(8,128)(2,1)} %get-tuple-element.177, s32[512]{0:T(512)S(1)} %bitcast.65, bf16[8,256,512]{2,1,0:T(8,128)(2,1)} %get-tuple-element.174, s32[]{:T(128)} %get-tuple-element.164), kind=kOutput, calls=%fused_computation.14.clone.1 | convolution fusion | flops 454426624 | bytes 1903104 | tf_op jit(solution)/shard_map/while/body/eval_jaxpr/dot_general | solution.py:64
  91.0 2.6 %dynamic_update_slice.12 = f32[8,256,192]{1,0,2:T(8,128)S(1)} dynamic-update-slice(f32[8,256,192]{1,0,2:T(8,128)S(1)} %get-tuple-element.165, f32[1,256,192]{1,0,2:T(1,128)S(1)} %copy.37, s32[]{:T(128)} %get-tuple-element.164, s32[]{:T(128)} %constant.21.clone.1..sunk, s32[]{:T(128)} %constant.21.clone.1..sunk) | dynamic-update-slice | bytes 393220 | tf_op jit(solution)/shard_map/while/body/jit(dynamic_update_index_in_dim)/dynamic_update_slice | solution.py:66
  95.1 2.6 %fusion.40 = f32[1,256,192]{1,2,0:T(8,128)S(1)} fusion(f32[512,192]{0,1:T(8,128)S(1)} %bitcast.60, bf16[2048,192]{1,0:T(8,128)(2,1)} %get-tuple-element.177, s32[512]{0:T(512)S(1)} %bitcast.65, bf16[8,256,512]{2,1,0:T(8,128)(2,1)} %get-tuple-element.174, s32[]{:T(128)} %get-tuple-element.164), kind=kOutput, calls=%fused_computation.14.clone.1 | convolution fusion | flops 454426624 | bytes 1903104 | tf_op jit(solution)/shard_map/while/body/eval_jaxpr/dot_general | solution.py:64
  97.9 2.6 %dynamic_update_slice.12 = f32[8,256,192]{1,0,2:T(8,128)S(1)} dynamic-update-slice(f32[8,256,192]{1,0,2:T(8,128)S(1)} %get-tuple-element.165, f32[1,256,192]{1,0,2:T(1,128)S(1)} %copy.37, s32[]{:T(128)} %get-tuple-element.164, s32[]{:T(128)} %constant.21.clone.1..sunk, s32[]{:T(128)} %constant.21.clone.1..sunk) | dynamic-update-slice | bytes 393220 | tf_op jit(solution)/shard_map/while/body/jit(dynamic_update_index_in_dim)/dynamic_update_slice | solution.py:66
  102.0 2.6 %fusion.40 = f32[1,256,192]{1,2,0:T(8,128)S(1)} fusion(f32[512,192]{0,1:T(8,128)S(1)} %bitcast.60, bf16[2048,192]{1,0:T(8,128)(2,1)} %get-tuple-element.177, s32[512]{0:T(512)S(1)} %bitcast.65, bf16[8,256,512]{2,1,0:T(8,128)(2,1)} %get-tuple-element.174, s32[]{:T(128)} %get-tuple-element.164), kind=kOutput, calls=%fused_computation.14.clone.1 | convolution fusion | flops 454426624 | bytes 1903104 | tf_op jit(solution)/shard_map/while/body/eval_jaxpr/dot_general | solution.py:64
  104.8 2.6 %dynamic_update_slice.12 = f32[8,256,192]{1,0,2:T(8,128)S(1)} dynamic-update-slice(f32[8,256,192]{1,0,2:T(8,128)S(1)} %get-tuple-element.165, f32[1,256,192]{1,0,2:T(1,128)S(1)} %copy.37, s32[]{:T(128)} %get-tuple-element.164, s32[]{:T(128)} %constant.21.clone.1..sunk, s32[]{:T(128)} %constant.21.clone.1..sunk) | dynamic-update-slice | bytes 393220 | tf_op jit(solution)/shard_map/while/body/jit(dynamic_update_index_in_dim)/dynamic_update_slice | solution.py:66
  109.0 2.0 %fusion.14 = f32[1,512]{1,0:T(1,128)S(1)} fusion(f32[2048,1]{0,1:T(1,128)S(1)} %bitcast.69, s32[512]{0:T(512)S(1)} %eq.80), kind=kOutput, calls=%fused_computation.21 | convolution fusion | flops 13631488 | bytes 12288 | tf_op jit(solution)/shard_map/dot_general | solution.py:75
  111.0 1.3 %mul.45 = f32[32,1,16]{2,0,1:T(8,128)} multiply(f32[32,1,16]{2,0,1:T(8,128)} %reshape.81, f32[32,1,16]{2,0,1:T(8,128)S(1)} %reshape.82) | non-fusion elementwise | flops 512 | bytes 6144 | tf_op jit(solution)/shard_map/mul | solution.py:76
  112.4 3.6 %all-to-all-start.1 = ((f32[32,1,16]{2,1,0:T(1,128)}), f32[32,1,16]{2,1,0:T(1,128)S(1)}, u32[]{:S(2)}, u32[]{:S(2)}) async-start(f32[32,1,16]{2,1,0:T(1,128)} %bitcast.15), calls=%async_computation.1 | async-start | bytes 32768 | tf_op jit(solution)/shard_map/all_to_all | solution.py:78
  116.0 1.9 %fusion.16 = f32[1,2048]{1,0:T(1,128)S(1)} fusion(f32[512,1]{0,1:T(1,128)S(1)} %reshape.94, s32[512]{0:T(512)S(1)} %eq.77), kind=kOutput, calls=%fused_computation.24 | convolution fusion | flops 13631488 | bytes 12288 | tf_op jit(solution)/shard_map/dot_general | solution.py:86
  118.0 5.2 %all-to-all-done.1 = f32[32,1,16]{2,1,0:T(1,128)S(1)} async-done(((f32[32,1,16]{2,1,0:T(1,128)}), f32[32,1,16]{2,1,0:T(1,128)S(1)}, u32[]{:S(2)}, u32[]{:S(2)}) %all-to-all-start.1) | async-done | bytes 2080 | tf_op jit(solution)/shard_map/all_to_all | solution.py:78
  123.9 1.9 %fusion.17 = f32[1,2048]{1,0:T(1,128)S(1)} fusion(f32[512,1]{0,1:T(1,128)S(1)} %reshape.92, s32[512]{0:T(512)S(1)} %eq.77), kind=kOutput, calls=%fused_computation.25 | convolution fusion | flops 13631488 | bytes 12288 | tf_op jit(solution)/shard_map/dot_general | solution.py:85
  (72 shorter events, 22.5 us)
Async XLA Ops:
  4.9 15.1 %all-to-all-start.2 = ((f32[32,1,16]{2,1,0:T(1,128)}), f32[32,1,16]{2,1,0:T(1,128)S(1)}, u32[]{:S(2)}, u32[]{:S(2)}) async-start(f32[32,1,16]{2,1,0:T(1,128)} %bitcast.17), calls=%async_computation.2 | async-start | bytes 32768 | tf_op jit(solution)/shard_map/all_to_all | solution.py:79
  18.7 7.3 %copy-start.4 = (s32[24]{0:T(128)S(1)}, s32[24]{0:T(128)}, u32[]{:S(2)}) copy-start(s32[24]{0:T(128)} %param.20) | copy-start | bytes 292
  18.7 7.3 %copy-start.5 = (f32[3]{0:T(128)S(1)}, f32[3]{0:T(128)}, u32[]{:S(2)}) copy-start(f32[3]{0:T(128)} %constant.45.clone) | copy-start | bytes 40
  18.7 7.4 %copy-start.3 = (f32[8]{0:T(128)S(1)}, f32[8]{0:T(128)}, u32[]{:S(2)}) copy-start(f32[8]{0:T(128)} %constant.53) | copy-start | bytes 100
  18.7 7.6 %copy-start.1 = (s32[1,32,16]{1,2,0:T(8,128)S(1)}, s32[1,32,16]{1,2,0:T(8,128)}, u32[]{:S(2)}) copy-start(s32[1,32,16]{1,2,0:T(8,128)} %param.23) | copy-start | bytes 6148
  20.0 32.2 %all-to-all-start = ((bf16[32,64,192]{2,1,0:T(8,128)(2,1)}), bf16[32,64,192]{2,1,0:T(8,128)(2,1)}, u32[]{:S(2)}, u32[]{:S(2)}) async-start(bf16[32,64,192]{2,1,0:T(8,128)(2,1)} %bitcast.8), calls=%async_computation | async-start | bytes 2097152 | tf_op jit(solution)/shard_map/all_to_all | solution.py:52
  108.0 17.9 %copy-start = (f32[24,8,8,256]{3,1,2,0:T(8,128)}, f32[24,8,8,256]{3,1,2,0:T(8,128)S(1)}, u32[]{:S(2)}) copy-start(f32[24,8,8,256]{3,1,2,0:T(8,128)S(1)} %copy.35) | copy-start | bytes 4718596
  108.9 17.5 %copy-start.2 = (f32[2048]{0:T(1024)}, f32[2048]{0:T(1024)S(1)}, u32[]{:S(2)}) copy-start(f32[2048]{0:T(1024)S(1)} %log_multiply_fusion) | copy-start | bytes 24580
  112.4 10.8 %all-to-all-start.1 = ((f32[32,1,16]{2,1,0:T(1,128)}), f32[32,1,16]{2,1,0:T(1,128)S(1)}, u32[]{:S(2)}, u32[]{:S(2)}) async-start(f32[32,1,16]{2,1,0:T(1,128)} %bitcast.15), calls=%async_computation.1 | async-start | bytes 32768 | tf_op jit(solution)/shard_map/all_to_all | solution.py:78
where the time goes:
time: 128 us; the launch traced here: 126 us
  matrix products  35.3 us (28%)
  local copies, waits for them, and re-layouts  33.6 us (26%)
  waiting for transfers between devices  29.7 us (23%)
  starting transfers between devices  16.9 us (13%)
  other arithmetic  9.82 us (8%)
    all_to_all x1, waiting for transfers between devices, local(): lax.all_to_all(outgoing, ('region', 'band'), split_axis=0, concat_axis=0,...  24.5 us
    dynamic_update_slice x16, local copies, waits for them, and re-layouts, local(): exposure = lax.map(tile_work, (tile_slots, geometry, absorption))  22.2 us
    dot_general x8, matrix products, tile_work(): jnp.dot(tile_geometry, mixed_rows, preferred_element_type=jnp.float32)  20.9 us
    all_to_all x1, starting transfers between devices, local(): lax.all_to_all(dwell_weight, ('region', 'band'), split_axis=0, concat_axi...  7.3 us
    all_to_all x1, starting transfers between devices, local(): lax.all_to_all(outgoing, ('region', 'band'), split_axis=0, concat_axis=0,...  5.96 us
    dynamic_slice x8, local copies, waits for them, and re-layouts, local(): exposure = lax.map(tile_work, (tile_slots, geometry, absorption))  5.83 us
    convert_element_type x8, other arithmetic, tile_work(): factor.astype(jnp.float32) * gathered.astype(jnp.float32)  5.62 us
    dot_general x4, matrix products, pick_rows(): jnp.dot(table, emission, preferred_element_type=jnp.float32)  5.54 us
  transfers between devices with their start and end apart: 3, of which 2 were waited for; matrix products, arithmetic and copies ran while one was open for 9% of the time, Pallas kernels for 0%

commit v1 on v0

v1 whole, which is shorter than its diff:
```python
import functools

import jax
import jax.numpy as jnp
from jax import lax
from jax.experimental import pallas as pl
from jax.experimental.pallas import tpu as pltpu
from jax.sharding import PartitionSpec as P

HOURS = 24
BANDS = 8
BLD_DEV = 2048
LANES = 128
HALF = LANES // 2
GROUP = 256
AXES = ("plane", "cell", "band")

A_WEIGHTING_DB = [-26.2, -16.1, -8.6, -3.2, 0.0, 1.2, 1.0, -1.1]
GAIN = [1.0, 10.0**0.5, 10.0]
LOG10_E = 0.4342944819032518

QUAD = 4
CHUNKS = ((0, 2), (2, 8))

NT = (((1,), (1,)), ((), ()))
VMEM = pl.BlockSpec(memory_space=pltpu.VMEM)
HBM = pl.BlockSpec(memory_space=pltpu.HBM)


def params(chips):
    return pltpu.CompilerParams(vmem_limit_bytes=min(16 * max(chips // 16, 1), 48) * 1024 * 1024)


def bf(x):
    return x.astype(jnp.bfloat16)


def f32(x):
    return x.astype(jnp.float32)


def three_parts(x):
    hi = f32(bf(x))
    rest = x - hi
    mid = f32(bf(rest))
    return hi, mid, rest - mid


def dot(a, b, dims=(((1,), (0,)), ((), ()))):
    return lax.dot_general(a, b, dims, preferred_element_type=jnp.float32)


def one_hot_columns(index, extent):
    rows = lax.broadcasted_iota(jnp.int32, (extent, index.shape[1]), 0)
    return bf(jnp.where(rows == index, jnp.float32(1.0), jnp.float32(0.0)))


def one_hot_groups(index):
    step = 16
    shape = (step, index.shape[1])
    rows = lax.broadcasted_iota(jnp.int32, shape, 0).astype(jnp.int16)
    wanted = jnp.broadcast_to(index, shape).astype(jnp.int16)
    one, zero = jnp.ones(shape, jnp.bfloat16), jnp.zeros(shape, jnp.bfloat16)
    return jnp.concatenate(
        [jnp.where(wanted == rows + jnp.int16(start), one, zero) for start in range(0, GROUP, step)], axis=0
    )


def merge(low, high):
    lane = lax.broadcasted_iota(jnp.int32, low.shape, 1)
    return jnp.where(lane < HALF, low, high)


def hour_gains(period_row):
    gain = jnp.where(period_row == 0, GAIN[0], jnp.where(period_row == 1, GAIN[1], jnp.where(period_row == 2, GAIN[2], 0.0)))
    shape = (HOURS, HOURS)
    same = lax.broadcasted_iota(jnp.int32, shape, 0) == lax.broadcasted_iota(jnp.int32, shape, 1)
    return jnp.sum(jnp.where(same, jnp.broadcast_to(gain, shape), 0.0), axis=1, keepdims=True)


def band_sums(emission, gains):
    sums = []
    for b in range(BANDS):
        rows = f32(emission[b * HOURS : (b + 1) * HOURS, :])
        factor = 10.0 ** (A_WEIGHTING_DB[b] / 10.0) / HOURS
        sums.append(jnp.sum(rows * (gains * factor), axis=0, keepdims=True))
    total = jnp.concatenate(sums, axis=0)
    high = f32(bf(total))
    return bf(jnp.concatenate([high, total - high], axis=0))


def chunk_rows(i):
    first, last = CHUNKS[i]
    if i == 0:
        return 0, last * HOURS + 2 * BANDS
    return first * HOURS + 2 * BANDS, (last - first) * HOURS


def extend_order(emission, sums):
    cut = CHUNKS[0][1] * HOURS
    return jnp.concatenate([emission[:cut], sums, emission[cut:]], axis=0)


def lists_of(list_ref, step, swapped):
    plane = lax.axis_index("plane") ^ step
    band = lax.axis_index("band")
    order = [q ^ 1 if swapped else q for q in range(QUAD)]
    return jnp.concatenate([list_ref[pl.ds(2 * (plane * QUAD + q) + band, 1), :] for q in order], axis=1)


def own_kernel(period_hbm, emission_hbm, list_hbm, out_ref, period_ref, emission_ref, list_ref, sems):
    pairs = ((list_hbm, list_ref), (period_hbm, period_ref), (emission_hbm, emission_ref))
    copies = [pltpu.make_async_copy(src, dst, sems.at[i]) for i, (src, dst) in enumerate(pairs)]
    for copy in copies:
        copy.start()
    for copy in copies:
        copy.wait()
    emission = emission_ref[...]
    rows = extend_order(emission, band_sums(emission, hour_gains(period_ref[...])))
    for step in range(out_ref.shape[0]):
        found = bf(dot(rows, one_hot_columns(lists_of(list_ref, step, False), rows.shape[1])))
        for pair in range(QUAD // 2):
            out_ref[step, pair] = found[:, pair * LANES : (pair + 1) * LANES]


def other_kernel(period_ref, emission_ref, list_ref, own_ref, *refs):
    planes = own_ref.shape[0]
    a_refs, (b_hbm, b_ref, sems) = refs[:planes], refs[planes:]
    emission = emission_ref[...]
    rows = extend_order(emission, band_sums(emission, hour_gains(period_ref[...])))
    (start_a, count_a), (start_b, count_b) = chunk_rows(0), chunk_rows(1)
    copies = []
    for step in range(planes):
        found = bf(dot(rows, one_hot_columns(lists_of(list_ref, step, True), rows.shape[1])))
        for pair in range(QUAD // 2):
            other = found[:, pair * LANES : (pair + 1) * LANES]
            own = own_ref[step, pair]
            for odd, block in ((0, merge(own, other)), (1, merge(other, own))):
                q = 2 * pair + odd
                a_refs[step][q] = block[start_a : start_a + count_a]
                b_ref[q, step] = block[start_b : start_b + count_b]
        copy = pltpu.make_async_copy(b_ref.at[:, step], b_hbm.at[:, step], sems.at[step])
        copy.start()
        copies.append(copy)
    for copy in copies:
        copy.wait()


def make_sends(hour_period, emission_t, other_t, sends, other_sends, chips):
    width, segs = emission_t.shape
    total = width + 2 * BANDS
    planes = chips // QUAD
    period = hour_period.reshape(1, HOURS)
    operands = [period, emission_t, sends]
    own = pl.pallas_call(
        own_kernel,
        in_specs=[HBM] * 3,
        out_specs=VMEM,
        out_shape=jax.ShapeDtypeStruct((planes, QUAD // 2, total, LANES), jnp.bfloat16),
        scratch_shapes=[pltpu.VMEM(x.shape, x.dtype) for x in operands] + [pltpu.SemaphoreType.DMA((3,))],
        compiler_params=params(chips),
        name="own_rows",
    )(*operands)
    outs = pl.pallas_call(
        other_kernel,
        in_specs=[VMEM] * 4,
        out_specs=[VMEM] * planes + [HBM],
        out_shape=[jax.ShapeDtypeStruct((QUAD, chunk_rows(0)[1], LANES), jnp.bfloat16)] * planes
        + [jax.ShapeDtypeStruct((QUAD, planes, chunk_rows(1)[1], LANES), jnp.bfloat16)],
        scratch_shapes=[
            pltpu.VMEM((QUAD, planes, chunk_rows(1)[1], LANES), jnp.bfloat16),
            pltpu.SemaphoreType.DMA((planes,)),
        ],
        compiler_params=params(chips),
        name="send_rows",
    )(period, other_t, other_sends, own)
    return outs[:planes], outs[planes]


def regroup_kernel(planes, *refs):
    b_ref = refs[1]
    a_refs, a_hbm = refs[2 : planes + 2], refs[planes + 2]
    b_outs, sems = refs[planes + 3 : -1], refs[-1]
    copies = [pltpu.make_async_copy(ref, a_hbm.at[:, j], sems.at[j]) for j, ref in enumerate(a_refs)]
    for copy in copies:
        copy.start()
    for j, out in enumerate(b_outs, 1):
        for q in range(QUAD):
            out[q] = b_ref[q, j]
    for copy in copies:
        copy.wait()


def regroup(after, blocks_a, block_b, chips):
    planes = len(blocks_a)
    outs = pl.pallas_call(
        functools.partial(regroup_kernel, planes),
        in_specs=[VMEM] * (2 + planes),
        out_specs=[HBM] + [VMEM] * (planes - 1),
        out_shape=[jax.ShapeDtypeStruct((QUAD, planes) + blocks_a[0].shape[1:], jnp.bfloat16)]
        + [jax.ShapeDtypeStruct((QUAD,) + block_b.shape[2:], jnp.bfloat16)] * (planes - 1),
        scratch_shapes=[pltpu.SemaphoreType.DMA((planes,))],
        compiler_params=params(chips),
        name="regroup",
    )(after, block_b, *blocks_a)
    return outs[0], outs[1:]


def along_planes(blocks):
    planes = len(blocks) + 1
    return [lax.ppermute(block, "plane", [(p, p ^ j) for p in range(planes)]) for j, block in enumerate(blocks, 1)]


def among_cells(array):
    return lax.all_to_all(array, "cell", split_axis=0, concat_axis=0, tiled=True)


def exchange(blocks_a, block_b, chips, after):
    near_b = among_cells(block_b)
    held_a = [blocks_a[0]] + along_planes(blocks_a[1:])
    grouped_a, grouped_b = regroup(after, held_a, near_b, chips)
    return among_cells(grouped_a), [near_b] + along_planes(grouped_b)


def slot_places(slots):
    half = (lax.axis_index("band") ^ (lax.axis_index("cell") & 1)) * HALF
    return slots ^ (lax.axis_index("plane") * (QUAD * LANES) + half)


def blocks_of_first(ref):
    return [ref.at[q, j] for j in range(ref.shape[1]) for q in range(QUAD)]


def blocks_of_second(refs):
    near, far = refs[0], refs[1:]
    return [near.at[q, 0] for q in range(QUAD)] + [ref.at[q] for ref in far for q in range(QUAD)]


def stack_groups(blocks, start, count, table_ref, first, rows):
    per_group = GROUP // LANES
    for c, block in enumerate(blocks):
        g, j = divmod(c, per_group)
        table_ref[pl.ds(g * rows + first, count), j * LANES : (j + 1) * LANES] = block[start : start + count, :]


def index_kernel(after_ref, slots_ref, dwell_ref, addr_ref, building_ref, places_out, dwell_out, addr_out, building_out):
    places_out[...] = slot_places(slots_ref[...])
    dwell_out[...] = f32(dwell_ref[...])
    for ref, out in ((addr_ref, addr_out), (building_ref, building_out)):
        out[...] = jnp.concatenate([ref[c : c + 1, :] for c in range(ref.shape[0])], axis=1)


def make_index(after, tile_slots, dwellings, addr_t, building_t, chips):
    dwell = dwellings.reshape(-1, LANES)
    row = jax.ShapeDtypeStruct((1, addr_t.size), jnp.int32)
    return pl.pallas_call(
        index_kernel,
        in_specs=[HBM] + [VMEM] * 4,
        out_specs=[VMEM] * 4,
        out_shape=[
            jax.ShapeDtypeStruct(tile_slots.shape, jnp.int32),
            jax.ShapeDtypeStruct(dwell.shape, jnp.float32),
            row,
            row,
        ],
        compiler_params=params(chips),
        name="index_rows",
    )(after, tile_slots, dwell, addr_t, building_t)


def gather_columns(table, rows, places):
    found = dot(table, one_hot_groups(places & (GROUP - 1)))
    group = places >> (GROUP.bit_length() - 1)
    out = jnp.zeros((rows, places.shape[1]), jnp.float32)
    for g in range(table.shape[0] // rows):
        out = jnp.where(group == g, found[g * rows : (g + 1) * rows], out)
    return out


def level_kernel(devices, recv_ref, places_ref, absorption_ref, geometry_ref, dwell_ref, addr_ref, *refs):
    level_ref, pay_hbm, table, pay_ref, sem = refs
    blocks = blocks_of_first(recv_ref)
    tiles, recv_tile, paths = geometry_ref.shape
    rows = 2 * BANDS
    stack_groups(blocks, blocks[0].shape[0] - rows, rows, table, 0, rows)
    places = places_ref[...]
    per_tile = recv_tile // LANES
    zeros = jnp.zeros((5, paths), jnp.float32)
    for t in range(tiles):
        sums = gather_columns(table[...], rows, places[t : t + 1, :])
        path = jnp.sum(f32(absorption_ref[t]) * (sums[:BANDS] + sums[BANDS:]), axis=0, keepdims=True)
        lhs = bf(jnp.concatenate([*three_parts(path), zeros], axis=0))
        energy = jnp.sum(dot(lhs, geometry_ref[t], NT), axis=0, keepdims=True)
        level = jnp.log(energy) * LOG10_E
        for j in range(per_tile):
            level_ref[t * per_tile + j : t * per_tile + j + 1, :] = level[:, j * LANES : (j + 1) * LANES]

    addr = addr_ref[...]
    cap = addr.shape[1] // devices
    level_rows = level_ref.shape[0]
    parts = [*three_parts(level_ref[...]), dwell_ref[...]]
    found = dot(bf(jnp.concatenate(parts, axis=0)), one_hot_columns(addr & (LANES - 1), LANES))
    row = lax.broadcasted_iota(jnp.int32, (level_rows, addr.shape[1]), 0)
    hit = row == (addr >> (LANES.bit_length() - 1))

    def pick(i):
        part = found[i * level_rows : (i + 1) * level_rows]
        return jnp.sum(jnp.where(hit, part, 0.0), axis=0, keepdims=True)

    dwelt = pick(3)
    weighted = dwelt * ((pick(0) + pick(1)) + pick(2))
    lines = [value[:, c * devices : (c + 1) * devices] for value in (weighted, dwelt) for c in range(cap)]
    square = jnp.concatenate(lines + [jnp.zeros((LANES - 2 * cap, devices), jnp.float32)], axis=0)
    if devices < LANES:
        square = jnp.concatenate([square, jnp.zeros((LANES, LANES - devices), jnp.float32)], axis=1)
    turned = square.T
    for d in range(devices):
        pay_ref[d] = turned[d : d + 1, :]
    copy = pltpu.make_async_copy(pay_ref, pay_hbm, sem)
    copy.start()
    copy.wait()


def make_levels(recv, chips, places, absorption, geometry, dwell, addr):
    tiles, recv_tile, paths = geometry.shape
    devices = 2 * chips
    operands = [recv, places, absorption, geometry, dwell, addr]
    return pl.pallas_call(
        functools.partial(level_kernel, devices),
        in_specs=[VMEM] * len(operands),
        out_specs=[VMEM, HBM],
        out_shape=[
            jax.ShapeDtypeStruct(dwell.shape, jnp.float32),
            jax.ShapeDtypeStruct((devices, 1, LANES), jnp.float32),
        ],
        scratch_shapes=[
            pltpu.VMEM((chips * LANES // GROUP * 2 * BANDS, GROUP), jnp.bfloat16),
            pltpu.VMEM((devices, 1, LANES), jnp.float32),
            pltpu.SemaphoreType.DMA,
        ],
        compiler_params=params(chips),
        name="levels",
    )(*operands)


def exposure_kernel(planes, *refs):
    places_ref, absorption_ref, geometry_ref, out_hbm, done_ref, table, out_ref, sems = refs[1 + planes :]
    done_ref[...] = jnp.zeros_like(done_ref)
    tiles, recv_tile, paths = geometry_ref.shape
    rows = out_ref.shape[0]
    for (first, last), blocks in zip(CHUNKS, (blocks_of_first(refs[0]), blocks_of_second(refs[1 : 1 + planes]))):
        stack_groups(blocks, 0, (last - first) * HOURS, table, first * HOURS, rows)
    places = places_ref[...]
    copies = []
    for t in range(tiles):
        gathered = gather_columns(table[...], rows, places[t : t + 1, :])
        absorption = f32(absorption_ref[t])
        mixed = jnp.concatenate(
            [absorption[b : b + 1] * gathered[b * HOURS : (b + 1) * HOURS] for b in range(BANDS)], axis=0
        )
        columns = slice(t * recv_tile, (t + 1) * recv_tile)
        out_ref[:, columns] = dot(bf(mixed), geometry_ref[t], NT)
        copy = pltpu.make_async_copy(out_ref.at[:, columns], out_hbm.at[:, columns], sems.at[t])
        copy.start()
        copies.append(copy)
    for copy in copies:
        copy.wait()


def make_exposure(moved, chips, places, absorption, geometry):
    tiles, recv_tile, paths = geometry.shape
    shape = (BANDS * HOURS, tiles * recv_tile)
    operands = [moved[0], *moved[1], places, absorption, geometry]
    return pl.pallas_call(
        functools.partial(exposure_kernel, chips // QUAD),
        in_specs=[VMEM] * len(operands),
        out_specs=[HBM, VMEM],
        out_shape=[jax.ShapeDtypeStruct(shape, jnp.float32), jax.ShapeDtypeStruct((8, LANES), jnp.float32)],
        scratch_shapes=[
            pltpu.VMEM((chips * LANES // GROUP * shape[0], GROUP), jnp.bfloat16),
            pltpu.VMEM(shape, jnp.float32),
            pltpu.SemaphoreType.DMA((tiles,)),
        ],
        compiler_params=params(chips),
        name="exposure",
    )(*operands)


def building_kernel(after_ref, arrived_ref, building_ref, out_ref):
    devices = arrived_ref.shape[0]
    building = building_ref[...]
    cap = building.shape[1] // devices
    square = jnp.concatenate([arrived_ref[s] for s in range(devices)], axis=0)
    if devices < LANES:
        square = jnp.concatenate([square, jnp.zeros((LANES - devices, LANES), jnp.float32)], axis=0)
    turned = square.T

    def line(ref, first):
        return jnp.concatenate([ref[first + c : first + c + 1, :devices] for c in range(cap)], axis=1)

    weighted, dwelt = line(turned, 0), line(turned, cap)
    rows = out_ref.shape[0]
    row = lax.broadcasted_iota(jnp.int32, (rows, building.shape[1]), 0)
    hit = row == (building >> (LANES.bit_length() - 1))
    parts = [jnp.where(hit, value, 0.0) for value in three_parts(weighted) + (dwelt,)]
    table = one_hot_columns(building & (LANES - 1), LANES)
    sums = dot(bf(jnp.concatenate(parts, axis=0)), table, NT)
    numer = (sums[:rows] + sums[rows : 2 * rows]) + sums[2 * rows : 3 * rows]
    out_ref[...] = numer / jnp.maximum(sums[3 * rows :], 1.0)


def make_buildings(after, arrived, building, chips):
    return pl.pallas_call(
        building_kernel,
        in_specs=[VMEM] * 3,
        out_specs=VMEM,
        out_shape=jax.ShapeDtypeStruct((BLD_DEV // LANES, LANES), jnp.float32),
        compiler_params=params(chips),
        name="buildings",
    )(after, arrived, building)


def local(
    emission,
    path_sends,
    tile_slots,
    geometry,
    absorption,
    hour_period,
    dwellings,
    addr_sends,
    addr_building,
    chips,
):
    swap = [(0, 1), (1, 0)]
    emission_t = emission.T
    sends = path_sends[0]
    other_t = lax.ppermute(emission_t, "band", swap)
    other_sends = lax.ppermute(sends, "band", swap)
    blocks_a, block_b = make_sends(hour_period, emission_t, other_t, sends, other_sends, chips)
    places, dwell, addr, building = make_index(
        blocks_a[0], tile_slots, dwellings, addr_sends[0].T, addr_building[0].T, chips
    )
    moved = exchange(blocks_a, block_b, chips, places)
    levels, pay = make_levels(moved[0], chips, places, absorption, geometry, dwell, addr)
    arrived = lax.all_to_all(pay, AXES, split_axis=0, concat_axis=0, tiled=True)
    exposure_t, done = make_exposure(moved, chips, places, absorption, geometry)
    buildings = make_buildings(done, arrived, building, chips)
    return (levels.reshape(-1), buildings.reshape(-1), exposure_t.T)


def solution(mesh):
    chips = mesh.shape["region"]
    cells = jax.sharding.Mesh(mesh.devices.reshape(chips // QUAD, QUAD, mesh.shape["band"]), AXES)
    in_specs = (
        P(AXES, None),
        P(AXES, None, None),
        P(AXES, None),
        P(AXES, None, None),
        P(AXES, None, None),
        P(),
        P(AXES),
        P(AXES, None, None),
        P(AXES, None, None),
    )
    out_specs = (P(AXES), P(AXES), P(AXES, None))
    body = functools.partial(local, chips=chips)
    return jax.shard_map(body, mesh=cells, in_specs=in_specs, out_specs=out_specs, check_vma=False)
```

time: 128 us -> 46.7 us (0.36)
  matrix products: 35.3 us -> 0 us
  local copies, waits for them, and re-layouts: 33.6 us -> 2.36 us
  waiting for transfers between devices: 29.7 us -> 8.55 us
  Pallas kernels: 0 us -> 12.7 us
  other arithmetic: 9.82 us -> 0 us
  starting transfers between devices: 16.9 us -> 21.9 us
    dot_general x17 -> x0, matrix products: 35.3 us -> none  [the longest x8 20.9 us: tile_work(): jnp.dot(tile_geometry, mixed_rows, preferred_element_type=jnp.float32)]
    all_to_all x3, waiting for transfers between devices: 29.7 us -> 1.13 us  [the longest x2 0.98 us: among_cells(): lax.all_to_all(array, 'cell', split_axis=0, concat_axis=0, tiled=True)]
    dynamic_update_slice x16 -> x0, local copies, waits for them, and re-layouts: 22.2 us -> none  [local(): exposure = lax.map(tile_work, (tile_slots, geometry, absorption))]
    pallas_call x0 -> x7, Pallas kernels: none -> 12.7 us  [the longest x1 5.33 us: make_exposure(): pl.pallas_call(functools.partial(exposure_kernel, chips // QUAD), in_spec...]
    ppermute x0 -> x8, starting transfers between devices: none -> 9.37 us  [the longest x6 8.77 us: along_planes(): lax.ppermute(block, 'plane', [(p, p ^ j) for p in range(planes)])]
    ppermute x0 -> x8, waiting for transfers between devices: none -> 7.42 us  [the longest x6 7.41 us: along_planes(): lax.ppermute(block, 'plane', [(p, p ^ j) for p in range(planes)])]
    convert_element_type x9 -> x0, other arithmetic: 6.32 us -> none  [the longest x8 5.62 us: tile_work(): factor.astype(jnp.float32) * gathered.astype(jnp.float32)]
    dynamic_slice x12 -> x0, local copies, waits for them, and re-layouts: 5.86 us -> none  [the longest x8 5.83 us: local(): exposure = lax.map(tile_work, (tile_slots, geometry, absorption))]
  transfers between devices with their start and end apart: 3 -> 11, of which waited for: 2 -> 5; matrix products, arithmetic and copies ran while one was open for 9% -> 0% of each run, Pallas kernels for 0% -> 20%
where the time goes in v1:
time: 46.7 us; the launch traced here: 46.4 us
  starting transfers between devices  21.9 us (47%)
  Pallas kernels  12.7 us (27%)
  waiting for transfers between devices  8.55 us (18%)
  local copies, waits for them, and re-layouts  2.36 us (5%)
  between operations  0.77 us (2%)
    all_to_all x2, starting transfers between devices, among_cells(): lax.all_to_all(array, 'cell', split_axis=0, concat_axis=0, tiled=True)  9.34 us
    ppermute x6, starting transfers between devices, along_planes(): lax.ppermute(block, 'plane', [(p, p ^ j) for p in range(planes)])  8.77 us
    ppermute x6, waiting for transfers between devices, along_planes(): lax.ppermute(block, 'plane', [(p, p ^ j) for p in range(planes)])  7.41 us
    pallas_call x1, Pallas kernels, make_exposure(): pl.pallas_call(functools.partial(exposure_kernel, chips // QUAD), in_spec...  5.33 us
    all_to_all x1, starting transfers between devices, local(): arrived = lax.all_to_all(pay, AXES, split_axis=0, concat_axis=0, tiled=True)  3.24 us
    pallas_call x1, Pallas kernels, make_levels(): pl.pallas_call(functools.partial(level_kernel, devices), in_specs=[VMEM]...  2.79 us
    unnamed x20, local copies, waits for them, and re-layouts  2.36 us
    pallas_call x1, Pallas kernels, regroup(): pl.pallas_call(functools.partial(regroup_kernel, planes), in_specs=[VMEM]...  1.45 us
  transfers between devices with their start and end apart: 11, of which 5 were waited for; matrix products, arithmetic and copies ran while one was open for 0% of the time, Pallas kernels for 20%

profile of v1, /device:TPU:0, one launch (start us, length us, event | category | flops | bytes accessed | tf_op | source)
XLA Modules:
  0.0 46.4 jit_solution(13370600841556939298)
XLA Ops:
  0.7 0.5 %collective-permute-start = (bf16[192,512]{1,0:T(8,128)(2,1)}, bf16[192,512]{1,0:T(8,128)(2,1)S(1)}, u32[]{:S(2)}, u32[]{:S(2)}) collective-permute-start(bf16[192,512]{1,0:T(8,128)(2,1)} %bitcast.13), channel_id=1, source_target_pairs={{0,1},{1,0},{2,3},{3,2},{4,5},{5,4},{6,7},{7,6},{8,9},{9,8},{10,11... | collective-permute-start | bytes 589832 | tf_op jit(solution)/shard_map/ppermute | solution.py:438
  1.2 0.1 collective-permute-start.1
  1.3 1.0 %copy-done.2 = bf16[512,192]{0,1:T(8,128)(2,1)S(1)} copy-done((bf16[512,192]{0,1:T(8,128)(2,1)S(1)}, bf16[512,192]{0,1:T(8,128)(2,1)}, u32[]{:S(2)}) %copy-start.2) | copy-done | bytes 196632
  2.2 0.7 %copy-done.3 = s32[1,32,64]{2,1,0:T(8,128)S(1)} copy-done((s32[1,32,64]{2,1,0:T(8,128)S(1)}, s32[1,32,64]{2,1,0:T(8,128)}, u32[]{:S(2)}) %copy-start.3) | copy-done | bytes 8216
  2.9 0.7 %copy-done.8 = s32[24]{0:T(128)S(1)} copy-done((s32[24]{0:T(128)S(1)}, s32[24]{0:T(128)}, u32[]{:S(2)}) %copy-start.8) | copy-done | bytes 120
  3.6 0.9 %own_rows.1.own_ref = bf16[4,2,208,128]{3,2,1,0:T(8,128)(2,1)S(1)} custom-call(s32[1,24]{1,0:T(1,128)S(1)} %bitcast.20, bf16[192,512]{1,0:T(8,128)(2,1)S(1)} %bitcast.14, s32[32,64]{1,0:T(8,128)S(1)} %bitcast.16), custom_call_target="tpu_custom_call" | custom-call | tf_op jit(solution)/shard_map/own_rows/pallas_call | solution.py:155
  4.5 0.0 collective-permute-done.1.list_ref
  4.5 0.0 collective-permute-done.emission_ref
  4.5 1.3 %send_rows.1 = (bf16[4,64,128]{2,1,0:T(8,128)(2,1)S(1)}, bf16[4,64,128]{2,1,0:T(8,128)(2,1)S(1)}, bf16[4,64,128]{2,1,0:T(8,128)(2,1)S(1)}, bf16[4,64,128]{2,1,0:T(8,128)(2,1)S(1)}, bf16[4,4,144,128]{3,2,1,0:T(8,128)(2,1)}) custom-call(s32[1,24]{1,0:T(1,128)S(1)} %bitcast.21, bf16[192,512]{1,0:T(8,128)(2,1)S(1)} %collective-permute-done.emission_ref, ...), custom_call_target="tpu_custom_call" | custom-call | tf_op jit(solution)/shard_map/send_rows/pallas_call | solution.py:164
  5.8 5.2 %all-to-all-start = ((bf16[4,4,144,128]{3,2,1,0:T(8,128)(2,1)}), bf16[4,4,144,128]{3,2,1,0:T(8,128)(2,1)S(1)}, u32[]{:S(2)}, u32[]{:S(2)}) async-start(bf16[4,4,144,128]{3,2,1,0:T(8,128)(2,1)} %get-tuple-element.22), calls=%async_computation | async-start | bytes 1179648 | tf_op jit(solution)/shard_map/all_to_all | solution.py:215
  11.0 1.6 %collective-permute-start.2 = (bf16[4,64,128]{2,1,0:T(8,128)(2,1)S(1)}, bf16[4,64,128]{2,1,0:T(8,128)(2,1)S(1)}, u32[]{:S(2)}, u32[]{:S(2)}) collective-permute-start(bf16[4,64,128]{2,1,0:T(8,128)(2,1)S(1)} %get-tuple-element.23), channel_id=1, source_target_pairs={{0,8},{8,0},{16,24},{24,16},{1,9},{9,1},{17,25},{25,17},{2,10},{10... | collective-permute-start | bytes 196616 | tf_op jit(solution)/shard_map/ppermute | solution.py:211
  12.6 2.6 %collective-permute-start.3 = (bf16[4,64,128]{2,1,0:T(8,128)(2,1)S(1)}, bf16[4,64,128]{2,1,0:T(8,128)(2,1)S(1)}, u32[]{:S(2)}, u32[]{:S(2)}) collective-permute-start(bf16[4,64,128]{2,1,0:T(8,128)(2,1)S(1)} %get-tuple-element.24), channel_id=1, source_target_pairs={{0,16},{8,24},{16,0},{24,8},{1,17},{9,25},{17,1},{25,9},{2,18},{10... | collective-permute-start | bytes 196616 | tf_op jit(solution)/shard_map/ppermute | solution.py:211
  15.1 0.2 collective-permute-start.4
  15.4 0.1 index_rows.1
  15.5 0.0 collective-permute-done.2.refs_3_
  15.5 4.4 %collective-permute-done.3.refs_4_ = bf16[4,64,128]{2,1,0:T(8,128)(2,1)S(1)} collective-permute-done((bf16[4,64,128]{2,1,0:T(8,128)(2,1)S(1)}, bf16[4,64,128]{2,1,0:T(8,128)(2,1)S(1)}, u32[]{:S(2)}, u32[]{:S(2)}) %collective-permute-start.3) | collective-permute-done | bytes 65568 | tf_op jit(solution)/shard_map/ppermute | solution.py:211
  19.8 1.4 %collective-permute-done.4.refs_5_ = bf16[4,64,128]{2,1,0:T(8,128)(2,1)S(1)} collective-permute-done((bf16[4,64,128]{2,1,0:T(8,128)(2,1)S(1)}, bf16[4,64,128]{2,1,0:T(8,128)(2,1)S(1)}, u32[]{:S(2)}, u32[]{:S(2)}) %collective-permute-start.4) | collective-permute-done | bytes 65568 | tf_op jit(solution)/shard_map/ppermute | solution.py:211
  21.2 0.0 all-to-all-done.refs_1_
  21.2 1.5 %regroup.1 = (bf16[4,4,64,128]{3,2,1,0:T(8,128)(2,1)}, bf16[4,144,128]{2,1,0:T(8,128)(2,1)}, bf16[4,144,128]{2,1,0:T(8,128)(2,1)}, bf16[4,144,128]{2,1,0:T(8,128)(2,1)S(1)}) custom-call(s32[8,512]{1,0:T(8,128)S(1)} %get-tuple-element.21.refs_0_.places_ref.refs_5_, bf16[4,4,144,128]{3,2,1,0:T(8,128)(2,1)S(1)} %all-to-all-done.refs_1_, ...), custom_call_target="tpu_custom_call" | custom-call | tf_op jit(solution)/shard_map/regroup/pallas_call | solution.py:196
  22.7 4.2 %all-to-all-start.1 = ((bf16[4,4,64,128]{3,2,1,0:T(8,128)(2,1)}), bf16[4,4,64,128]{3,2,1,0:T(8,128)(2,1)S(1)}, u32[]{:S(2)}, u32[]{:S(2)}) async-start(bf16[4,4,64,128]{3,2,1,0:T(8,128)(2,1)} %get-tuple-element.26), calls=%async_computation.1 | async-start | bytes 524288 | tf_op jit(solution)/shard_map/all_to_all | solution.py:215
  26.9 0.0 collective-permute-start.5
  26.9 2.1 %collective-permute-start.6 = (bf16[4,144,128]{2,1,0:T(8,128)(2,1)}, bf16[4,144,128]{2,1,0:T(8,128)(2,1)S(1)}, u32[]{:S(2)}, u32[]{:S(2)}) collective-permute-start(bf16[4,144,128]{2,1,0:T(8,128)(2,1)} %get-tuple-element.31), channel_id=1, source_target_pairs={{0,16},{8,24},{16,0},{24,8},{1,17},{9,25},{17,1},{25,9},{2,18},{10... | collective-permute-start | bytes 442376 | tf_op jit(solution)/shard_map/ppermute | solution.py:211
  29.0 2.2 %collective-permute-start.7 = (bf16[4,144,128]{2,1,0:T(8,128)(2,1)}, bf16[4,144,128]{2,1,0:T(8,128)(2,1)S(1)}, u32[]{:S(2)}, u32[]{:S(2)}) collective-permute-start(bf16[4,144,128]{2,1,0:T(8,128)(2,1)} %copy-done.9), channel_id=1, source_target_pairs={{0,24},{8,16},{16,8},{24,0},{1,25},{9,17},{17,9},{25,1},{2,26},{10... | collective-permute-start | bytes 442376 | tf_op jit(solution)/shard_map/ppermute | solution.py:211
  31.3 1.0 %all-to-all-done.1.recv_ref.refs_0_ = bf16[4,4,64,128]{3,2,1,0:T(8,128)(2,1)S(1)} async-done(((bf16[4,4,64,128]{3,2,1,0:T(8,128)(2,1)}), bf16[4,4,64,128]{3,2,1,0:T(8,128)(2,1)S(1)}, u32[]{:S(2)}, u32[]{:S(2)}) %all-to-all-start.1) | async-done | bytes 262176 | tf_op jit(solution)/shard_map/all_to_all | solution.py:215
  32.3 2.8 %levels.1 = (f32[16,128]{1,0:T(8,128)}, f32[32,1,128]{2,1,0:T(1,128)}) custom-call(bf16[4,4,64,128]{3,2,1,0:T(8,128)(2,1)S(1)} %all-to-all-done.1.recv_ref.refs_0_, s32[8,512]{1,0:T(8,128)S(1)} %get-tuple-element.21.refs_0_.places_ref.refs_5_, bf16[8,8,512]{2,1,0:T(8,128)(2,1)S(1)} %copy-done.1, bf16[8,256,512]{2,1,0:T(8,128)(2,1)S(1)} %copy-done, ...), custom_call_target="tpu_custom_call" | custom-call | tf_op jit(solution)/shard_map/levels/pallas_call | solution.py:328
  35.1 3.2 %all-to-all-start.2 = ((f32[32,1,128]{2,1,0:T(1,128)}), f32[32,1,128]{2,1,0:T(1,128)S(1)}, u32[]{:S(2)}, u32[]{:S(2)}) async-start(f32[32,1,128]{2,1,0:T(1,128)} %get-tuple-element.34), calls=%async_computation.2 | async-start | bytes 32768 | tf_op jit(solution)/shard_map/all_to_all | solution.py:446
  38.3 0.0 collective-permute-done.5.refs_2_
  38.3 1.6 %collective-permute-done.6.refs_3_ = bf16[4,144,128]{2,1,0:T(8,128)(2,1)S(1)} collective-permute-done((bf16[4,144,128]{2,1,0:T(8,128)(2,1)}, bf16[4,144,128]{2,1,0:T(8,128)(2,1)S(1)}, u32[]{:S(2)}, u32[]{:S(2)}) %collective-permute-start.6) | collective-permute-done | bytes 147488 | tf_op jit(solution)/shard_map/ppermute | solution.py:211
  40.0 0.0 collective-permute-done.7.refs_4_
  40.0 5.3 %exposure.1 = (f32[192,2048]{1,0:T(8,128)}, f32[8,128]{1,0:T(8,128)S(1)}) custom-call(bf16[4,4,64,128]{3,2,1,0:T(8,128)(2,1)S(1)} %all-to-all-done.1.recv_ref.refs_0_, bf16[4,4,144,128]{3,2,1,0:T(8,128)(2,1)S(1)} %all-to-all-done.refs_1_, bf16[4,144,128]{2,1,0:T(8,128)(2,1)S(1)} %collective-permute-done.5.refs_2_, ...), custom_call_target="tpu_custom_call" | custom-call | tf_op jit(solution)/shard_map/exposure/pallas_call | solution.py:374
  45.3 0.1 all-to-all-done.2.arrived_ref
  45.4 0.9 %buildings.1 = f32[16,128]{1,0:T(8,128)} custom-call(f32[8,128]{1,0:T(8,128)S(1)} %get-tuple-element.33.after_ref, f32[32,1,128]{2,1,0:T(1,128)S(1)} %all-to-all-done.2.arrived_ref, s32[1,512]{1,0:T(1,128)S(1)} %get-tuple-element.35.building_ref), custom_call_target="tpu_custom_call" | custom-call | tf_op jit(solution)/shard_map/buildings/pallas_call | solution.py:413
  (17 shorter events, 0.0 us)
Async XLA Ops:
  0.6 31.6 %copy-start = (bf16[8,256,512]{2,1,0:T(8,128)(2,1)S(1)}, bf16[8,256,512]{2,1,0:T(8,128)(2,1)}, u32[]{:S(2)}) copy-start(bf16[8,256,512]{2,1,0:T(8,128)(2,1)} %refs_7_.1) | copy-start | bytes 6291460
  0.6 31.6 %copy-start.1 = (bf16[8,8,512]{2,1,0:T(8,128)(2,1)S(1)}, bf16[8,8,512]{2,1,0:T(8,128)(2,1)}, u32[]{:S(2)}) copy-start(bf16[8,8,512]{2,1,0:T(8,128)(2,1)} %refs_6_.1) | copy-start | bytes 196612
  0.7 3.8 %collective-permute-start = (bf16[192,512]{1,0:T(8,128)(2,1)}, bf16[192,512]{1,0:T(8,128)(2,1)S(1)}, u32[]{:S(2)}, u32[]{:S(2)}) collective-permute-start(bf16[192,512]{1,0:T(8,128)(2,1)} %bitcast.13), channel_id=1, source_target_pairs={{0,1},{1,0},{2,3},{3,2},{4,5},{5,4},{6,7},{7,6},{8,9},{9,8},{10,11... | collective-permute-start | bytes 589832 | tf_op jit(solution)/shard_map/ppermute | solution.py:438
  1.2 3.3 %collective-permute-start.1 = (s32[32,64]{1,0:T(8,128)}, s32[32,64]{1,0:T(8,128)S(1)}, u32[]{:S(2)}, u32[]{:S(2)}) collective-permute-start(s32[32,64]{1,0:T(8,128)} %bitcast.15), channel_id=1, source_target_pairs={{0,1},{1,0},{2,3},{3,2},{4,5},{5,4},{6,7},{7,6},{8,9},{9,8},{10,11... | collective-permute-start | bytes 24584 | tf_op jit(solution)/shard_map/ppermute | solution.py:439
  1.2 1.0 %copy-start.2 = (bf16[512,192]{0,1:T(8,128)(2,1)S(1)}, bf16[512,192]{0,1:T(8,128)(2,1)}, u32[]{:S(2)}) copy-start(bf16[512,192]{0,1:T(8,128)(2,1)} %param.9) | copy-start | bytes 589828
  2.2 0.7 %copy-start.3 = (s32[1,32,64]{2,1,0:T(8,128)S(1)}, s32[1,32,64]{2,1,0:T(8,128)}, u32[]{:S(2)}) copy-start(s32[1,32,64]{2,1,0:T(8,128)} %param.10) | copy-start | bytes 24580
  2.9 0.7 %copy-start.8 = (s32[24]{0:T(128)S(1)}, s32[24]{0:T(128)}, u32[]{:S(2)}) copy-start(s32[24]{0:T(128)} %param.14) | copy-start | bytes 292
  3.6 11.8 %copy-start.4 = (s32[8,512]{1,0:T(8,128)S(1)}, s32[8,512]{1,0:T(8,128)}, u32[]{:S(2)}) copy-start(s32[8,512]{1,0:T(8,128)} %slots_ref.1) | copy-start | bytes 49156
  3.6 11.8 %copy-start.5 = (s32[2048]{0:T(1024)S(1)}, s32[2048]{0:T(1024)}, u32[]{:S(2)}) copy-start(s32[2048]{0:T(1024)} %param.15) | copy-start | bytes 24580
  3.6 11.8 %copy-start.6 = (s32[1,32,16]{1,2,0:T(8,128)S(1)}, s32[1,32,16]{1,2,0:T(8,128)}, u32[]{:S(2)}) copy-start(s32[1,32,16]{1,2,0:T(8,128)} %param.16) | copy-start | bytes 6148
  3.6 11.8 %copy-start.7 = (s32[1,32,16]{1,2,0:T(8,128)S(1)}, s32[1,32,16]{1,2,0:T(8,128)}, u32[]{:S(2)}) copy-start(s32[1,32,16]{1,2,0:T(8,128)} %param.17) | copy-start | bytes 6148
  5.8 15.4 %all-to-all-start = ((bf16[4,4,144,128]{3,2,1,0:T(8,128)(2,1)}), bf16[4,4,144,128]{3,2,1,0:T(8,128)(2,1)S(1)}, u32[]{:S(2)}, u32[]{:S(2)}) async-start(bf16[4,4,144,128]{3,2,1,0:T(8,128)(2,1)} %get-tuple-element.22), calls=%async_computation | async-start | bytes 1179648 | tf_op jit(solution)/shard_map/all_to_all | solution.py:215
  11.0 4.5 %collective-permute-start.2 = (bf16[4,64,128]{2,1,0:T(8,128)(2,1)S(1)}, bf16[4,64,128]{2,1,0:T(8,128)(2,1)S(1)}, u32[]{:S(2)}, u32[]{:S(2)}) collective-permute-start(bf16[4,64,128]{2,1,0:T(8,128)(2,1)S(1)} %get-tuple-element.23), channel_id=1, source_target_pairs={{0,8},{8,0},{16,24},{24,16},{1,9},{9,1},{17,25},{25,17},{2,10},{10... | collective-permute-start | bytes 196616 | tf_op jit(solution)/shard_map/ppermute | solution.py:211
  12.6 7.3 %collective-permute-start.3 = (bf16[4,64,128]{2,1,0:T(8,128)(2,1)S(1)}, bf16[4,64,128]{2,1,0:T(8,128)(2,1)S(1)}, u32[]{:S(2)}, u32[]{:S(2)}) collective-permute-start(bf16[4,64,128]{2,1,0:T(8,128)(2,1)S(1)} %get-tuple-element.24), channel_id=1, source_target_pairs={{0,16},{8,24},{16,0},{24,8},{1,17},{9,25},{17,1},{25,9},{2,18},{10... | collective-permute-start | bytes 196616 | tf_op jit(solution)/shard_map/ppermute | solution.py:211
  15.1 6.1 %collective-permute-start.4 = (bf16[4,64,128]{2,1,0:T(8,128)(2,1)S(1)}, bf16[4,64,128]{2,1,0:T(8,128)(2,1)S(1)}, u32[]{:S(2)}, u32[]{:S(2)}) collective-permute-start(bf16[4,64,128]{2,1,0:T(8,128)(2,1)S(1)} %get-tuple-element.25), channel_id=1, source_target_pairs={{0,24},{8,16},{16,8},{24,0},{1,25},{9,17},{17,9},{25,1},{2,26},{10... | collective-permute-start | bytes 196616 | tf_op jit(solution)/shard_map/ppermute | solution.py:211
  22.7 4.2 %copy-start.9 = (bf16[4,144,128]{2,1,0:T(8,128)(2,1)}, bf16[4,144,128]{2,1,0:T(8,128)(2,1)S(1)}, u32[]{:S(2)}) copy-start(bf16[4,144,128]{2,1,0:T(8,128)(2,1)S(1)} %get-tuple-element.32) | copy-start | bytes 442372
  22.7 9.5 %all-to-all-start.1 = ((bf16[4,4,64,128]{3,2,1,0:T(8,128)(2,1)}), bf16[4,4,64,128]{3,2,1,0:T(8,128)(2,1)S(1)}, u32[]{:S(2)}, u32[]{:S(2)}) async-start(bf16[4,4,64,128]{3,2,1,0:T(8,128)(2,1)} %get-tuple-element.26), calls=%async_computation.1 | async-start | bytes 524288 | tf_op jit(solution)/shard_map/all_to_all | solution.py:215
  26.9 11.4 %collective-permute-start.5 = (bf16[4,144,128]{2,1,0:T(8,128)(2,1)}, bf16[4,144,128]{2,1,0:T(8,128)(2,1)S(1)}, u32[]{:S(2)}, u32[]{:S(2)}) collective-permute-start(bf16[4,144,128]{2,1,0:T(8,128)(2,1)} %get-tuple-element.30), channel_id=1, source_target_pairs={{0,8},{8,0},{16,24},{24,16},{1,9},{9,1},{17,25},{25,17},{2,10},{10... | collective-permute-start | bytes 442376 | tf_op jit(solution)/shard_map/ppermute | solution.py:211
  26.9 13.1 %collective-permute-start.6 = (bf16[4,144,128]{2,1,0:T(8,128)(2,1)}, bf16[4,144,128]{2,1,0:T(8,128)(2,1)S(1)}, u32[]{:S(2)}, u32[]{:S(2)}) collective-permute-start(bf16[4,144,128]{2,1,0:T(8,128)(2,1)} %get-tuple-element.31), channel_id=1, source_target_pairs={{0,16},{8,24},{16,0},{24,8},{1,17},{9,25},{17,1},{25,9},{2,18},{10... | collective-permute-start | bytes 442376 | tf_op jit(solution)/shard_map/ppermute | solution.py:211
  29.0 10.9 %collective-permute-start.7 = (bf16[4,144,128]{2,1,0:T(8,128)(2,1)}, bf16[4,144,128]{2,1,0:T(8,128)(2,1)S(1)}, u32[]{:S(2)}, u32[]{:S(2)}) collective-permute-start(bf16[4,144,128]{2,1,0:T(8,128)(2,1)} %copy-done.9), channel_id=1, source_target_pairs={{0,24},{8,16},{16,8},{24,0},{1,25},{9,17},{17,9},{25,1},{2,26},{10... | collective-permute-start | bytes 442376 | tf_op jit(solution)/shard_map/ppermute | solution.py:211
  35.1 10.4 %all-to-all-start.2 = ((f32[32,1,128]{2,1,0:T(1,128)}), f32[32,1,128]{2,1,0:T(1,128)S(1)}, u32[]{:S(2)}, u32[]{:S(2)}) async-start(f32[32,1,128]{2,1,0:T(1,128)} %get-tuple-element.34), calls=%async_computation.2 | async-start | bytes 32768 | tf_op jit(solution)/shard_map/all_to_all | solution.py:446

commit v2 on v1

--- a/solution.py
+++ b/solution.py
@@ -101,8 +101,18 @@
     return jnp.concatenate([emission[:cut], sums, emission[cut:]], axis=0)
 
 
+def turned_step(step):
+    low, high = step & 1, (step >> 1) & 1
+    return (step & ~3) | (((low ^ high) << 1) | high)
+
+
+def turned_back(step):
+    low, high = step & 1, (step >> 1) & 1
+    return (step & ~3) | ((low << 1) | (low ^ high))
+
+
 def lists_of(list_ref, step, swapped):
-    plane = lax.axis_index("plane") ^ step
+    plane = lax.axis_index("plane") ^ jnp.where(lax.axis_index("band") == 0, step, turned_step(step))
     band = lax.axis_index("band")
     order = [q ^ 1 if swapped else q for q in range(QUAD)]
     return jnp.concatenate([list_ref[pl.ds(2 * (plane * QUAD + q) + band, 1), :] for q in order], axis=1)
@@ -208,7 +218,11 @@
 
 def along_planes(blocks):
     planes = len(blocks) + 1
-    return [lax.ppermute(block, "plane", [(p, p ^ j) for p in range(planes)]) for j, block in enumerate(blocks, 1)]
+
+    def pairs(step):
+        return [(2 * p + core, 2 * (p ^ own) + core) for core, own in enumerate((step, turned_step(step))) for p in range(planes)]
+
+    return [lax.ppermute(block, ("plane", "band"), pairs(step)) for step, block in enumerate(blocks, 1)]
 
 
 def among_cells(array):
@@ -224,7 +238,10 @@
 
 def slot_places(slots):
     half = (lax.axis_index("band") ^ (lax.axis_index("cell") & 1)) * HALF
-    return slots ^ (lax.axis_index("plane") * (QUAD * LANES) + half)
+    shift = (QUAD * LANES).bit_length() - 1
+    place = slots ^ ((lax.axis_index("plane") << shift) + half)
+    turned = (turned_back(place >> shift) << shift) | (place & (QUAD * LANES - 1))
+    return jnp.where(lax.axis_index("band") == 0, place, turned)
 
 
 def blocks_of_first(ref):
@@ -278,7 +295,7 @@
 
 
 def level_kernel(devices, recv_ref, places_ref, absorption_ref, geometry_ref, dwell_ref, addr_ref, *refs):
-    level_ref, pay_hbm, table, pay_ref, sem = refs
+    level_ref, pay_ref, table = refs
     blocks = blocks_of_first(recv_ref)
     tiles, recv_tile, paths = geometry_ref.shape
     rows = 2 * BANDS
@@ -316,9 +333,6 @@
     turned = square.T
     for d in range(devices):
         pay_ref[d] = turned[d : d + 1, :]
-    copy = pltpu.make_async_copy(pay_ref, pay_hbm, sem)
-    copy.start()
-    copy.wait()
 
 
 def make_levels(recv, chips, places, absorption, geometry, dwell, addr):
@@ -328,16 +342,12 @@
     return pl.pallas_call(
         functools.partial(level_kernel, devices),
         in_specs=[VMEM] * len(operands),
-        out_specs=[VMEM, HBM],
+        out_specs=[VMEM] * 2,
         out_shape=[
             jax.ShapeDtypeStruct(dwell.shape, jnp.float32),
             jax.ShapeDtypeStruct((devices, 1, LANES), jnp.float32),
         ],
-        scratch_shapes=[
-            pltpu.VMEM((chips * LANES // GROUP * 2 * BANDS, GROUP), jnp.bfloat16),
-            pltpu.VMEM((devices, 1, LANES), jnp.float32),
-            pltpu.SemaphoreType.DMA,
-        ],
+        scratch_shapes=[pltpu.VMEM((chips * LANES // GROUP * 2 * BANDS, GROUP), jnp.bfloat16)],
         compiler_params=params(chips),
         name="levels",
     )(*operands)

time: 46.7 us -> 46.1 us (0.987)
  Pallas kernels: 12.7 us -> 12.1 us
    pallas_call x1, Pallas kernels: 2.79 us -> 2.19 us  [make_levels(): pl.pallas_call(functools.partial(level_kernel, devices), in_specs=[VMEM]...]
  transfers between devices with their start and end apart: 11 -> 11, of which waited for: 5 -> 6; matrix products, arithmetic and copies ran while one was open for 0% -> 0% of each run, Pallas kernels for 20% -> 18%
where the time goes in v2:
time: 46.1 us; the launch traced here: 45.8 us
  starting transfers between devices  22 us (48%)
  Pallas kernels  12.1 us (26%)
  waiting for transfers between devices  8.49 us (18%)
  local copies, waits for them, and re-layouts  2.36 us (5%)
  between operations  0.76 us (2%)
    all_to_all x2, starting transfers between devices, among_cells(): lax.all_to_all(array, 'cell', split_axis=0, concat_axis=0, tiled=True)  9.38 us
    ppermute x6, starting transfers between devices, along_planes(): lax.ppermute(block, ('plane', 'band'), pairs(step))  8.8 us
    ppermute x6, waiting for transfers between devices, along_planes(): lax.ppermute(block, ('plane', 'band'), pairs(step))  7.04 us
    pallas_call x1, Pallas kernels, make_exposure(): pl.pallas_call(functools.partial(exposure_kernel, chips // QUAD), in_spec...  5.32 us
    all_to_all x1, starting transfers between devices, local(): arrived = lax.all_to_all(pay, AXES, split_axis=0, concat_axis=0, tiled=True)  3.22 us
    unnamed x20, local copies, waits for them, and re-layouts  2.36 us
    pallas_call x1, Pallas kernels, make_levels(): pl.pallas_call(functools.partial(level_kernel, devices), in_specs=[VMEM]...  2.19 us
    pallas_call x1, Pallas kernels, regroup(): pl.pallas_call(functools.partial(regroup_kernel, planes), in_specs=[VMEM]...  1.45 us
  transfers between devices with their start and end apart: 11, of which 6 were waited for; matrix products, arithmetic and copies ran while one was open for 0% of the time, Pallas kernels for 18%

profile of v2, /device:TPU:0, one launch (start us, length us, event | category | flops | bytes accessed | tf_op | source)
XLA Modules:
  0.0 45.8 jit_solution(2589076678060396772)
XLA Ops:
  0.7 0.5 %collective-permute-start = (bf16[192,512]{1,0:T(8,128)(2,1)}, bf16[192,512]{1,0:T(8,128)(2,1)S(1)}, u32[]{:S(2)}, u32[]{:S(2)}) collective-permute-start(bf16[192,512]{1,0:T(8,128)(2,1)} %bitcast.13), channel_id=1, source_target_pairs={{0,1},{1,0},{2,3},{3,2},{4,5},{5,4},{6,7},{7,6},{8,9},{9,8},{10,11... | collective-permute-start | bytes 589832 | tf_op jit(solution)/shard_map/ppermute | solution.py:448
  1.2 0.1 collective-permute-start.1
  1.3 1.0 %copy-done.2 = bf16[512,192]{0,1:T(8,128)(2,1)S(1)} copy-done((bf16[512,192]{0,1:T(8,128)(2,1)S(1)}, bf16[512,192]{0,1:T(8,128)(2,1)}, u32[]{:S(2)}) %copy-start.2) | copy-done | bytes 196632
  2.2 0.7 %copy-done.3 = s32[1,32,64]{2,1,0:T(8,128)S(1)} copy-done((s32[1,32,64]{2,1,0:T(8,128)S(1)}, s32[1,32,64]{2,1,0:T(8,128)}, u32[]{:S(2)}) %copy-start.3) | copy-done | bytes 8216
  2.9 0.7 %copy-done.8 = s32[24]{0:T(128)S(1)} copy-done((s32[24]{0:T(128)S(1)}, s32[24]{0:T(128)}, u32[]{:S(2)}) %copy-start.8) | copy-done | bytes 120
  3.6 0.9 %own_rows.1.own_ref = bf16[4,2,208,128]{3,2,1,0:T(8,128)(2,1)S(1)} custom-call(s32[1,24]{1,0:T(1,128)S(1)} %bitcast.20, bf16[192,512]{1,0:T(8,128)(2,1)S(1)} %bitcast.14, s32[32,64]{1,0:T(8,128)S(1)} %bitcast.16), custom_call_target="tpu_custom_call" | custom-call | tf_op jit(solution)/shard_map/own_rows/pallas_call | solution.py:165
  4.5 0.0 collective-permute-done.1.list_ref
  4.5 0.0 collective-permute-done.emission_ref
  4.5 1.3 %send_rows.1 = (bf16[4,64,128]{2,1,0:T(8,128)(2,1)S(1)}, bf16[4,64,128]{2,1,0:T(8,128)(2,1)S(1)}, bf16[4,64,128]{2,1,0:T(8,128)(2,1)S(1)}, bf16[4,64,128]{2,1,0:T(8,128)(2,1)S(1)}, bf16[4,4,144,128]{3,2,1,0:T(8,128)(2,1)}) custom-call(s32[1,24]{1,0:T(1,128)S(1)} %bitcast.21, bf16[192,512]{1,0:T(8,128)(2,1)S(1)} %collective-permute-done.emission_ref, ...), custom_call_target="tpu_custom_call" | custom-call | tf_op jit(solution)/shard_map/send_rows/pallas_call | solution.py:174
  5.8 5.2 %all-to-all-start = ((bf16[4,4,144,128]{3,2,1,0:T(8,128)(2,1)}), bf16[4,4,144,128]{3,2,1,0:T(8,128)(2,1)S(1)}, u32[]{:S(2)}, u32[]{:S(2)}) async-start(bf16[4,4,144,128]{3,2,1,0:T(8,128)(2,1)} %get-tuple-element.22), calls=%async_computation | async-start | bytes 1179648 | tf_op jit(solution)/shard_map/all_to_all | solution.py:229
  11.0 1.6 %collective-permute-start.2 = (bf16[4,64,128]{2,1,0:T(8,128)(2,1)S(1)}, bf16[4,64,128]{2,1,0:T(8,128)(2,1)S(1)}, u32[]{:S(2)}, u32[]{:S(2)}) collective-permute-start(bf16[4,64,128]{2,1,0:T(8,128)(2,1)S(1)} %get-tuple-element.23), channel_id=1, source_target_pairs={{0,8},{8,0},{16,24},{24,16},{1,17},{9,25},{17,1},{25,9},{2,10},{10... | collective-permute-start | bytes 196616 | tf_op jit(solution)/shard_map/ppermute | solution.py:225
  12.6 2.6 %collective-permute-start.3 = (bf16[4,64,128]{2,1,0:T(8,128)(2,1)S(1)}, bf16[4,64,128]{2,1,0:T(8,128)(2,1)S(1)}, u32[]{:S(2)}, u32[]{:S(2)}) collective-permute-start(bf16[4,64,128]{2,1,0:T(8,128)(2,1)S(1)} %get-tuple-element.24), channel_id=1, source_target_pairs={{0,16},{8,24},{16,0},{24,8},{1,25},{9,17},{17,9},{25,1},{2,18},{10... | collective-permute-start | bytes 196616 | tf_op jit(solution)/shard_map/ppermute | solution.py:225
  15.2 0.2 collective-permute-start.4
  15.4 0.1 index_rows.1
  15.5 0.2 collective-permute-done.2.refs_3_
  15.7 3.9 %collective-permute-done.3.refs_4_ = bf16[4,64,128]{2,1,0:T(8,128)(2,1)S(1)} collective-permute-done((bf16[4,64,128]{2,1,0:T(8,128)(2,1)S(1)}, bf16[4,64,128]{2,1,0:T(8,128)(2,1)S(1)}, u32[]{:S(2)}, u32[]{:S(2)}) %collective-permute-start.3) | collective-permute-done | bytes 65568 | tf_op jit(solution)/shard_map/ppermute | solution.py:225
  19.6 1.7 %collective-permute-done.4.refs_5_ = bf16[4,64,128]{2,1,0:T(8,128)(2,1)S(1)} collective-permute-done((bf16[4,64,128]{2,1,0:T(8,128)(2,1)S(1)}, bf16[4,64,128]{2,1,0:T(8,128)(2,1)S(1)}, u32[]{:S(2)}, u32[]{:S(2)}) %collective-permute-start.4) | collective-permute-done | bytes 65568 | tf_op jit(solution)/shard_map/ppermute | solution.py:225
  21.2 0.0 all-to-all-done.refs_1_
  21.2 1.5 %regroup.1 = (bf16[4,4,64,128]{3,2,1,0:T(8,128)(2,1)}, bf16[4,144,128]{2,1,0:T(8,128)(2,1)}, bf16[4,144,128]{2,1,0:T(8,128)(2,1)}, bf16[4,144,128]{2,1,0:T(8,128)(2,1)S(1)}) custom-call(s32[8,512]{1,0:T(8,128)S(1)} %get-tuple-element.21.refs_0_.places_ref.refs_5_, bf16[4,4,144,128]{3,2,1,0:T(8,128)(2,1)S(1)} %all-to-all-done.refs_1_, ...), custom_call_target="tpu_custom_call" | custom-call | tf_op jit(solution)/shard_map/regroup/pallas_call | solution.py:206
  22.7 4.2 %all-to-all-start.1 = ((bf16[4,4,64,128]{3,2,1,0:T(8,128)(2,1)}), bf16[4,4,64,128]{3,2,1,0:T(8,128)(2,1)S(1)}, u32[]{:S(2)}, u32[]{:S(2)}) async-start(bf16[4,4,64,128]{3,2,1,0:T(8,128)(2,1)} %get-tuple-element.26), calls=%async_computation.1 | async-start | bytes 524288 | tf_op jit(solution)/shard_map/all_to_all | solution.py:229
  26.9 0.0 collective-permute-start.5
  26.9 2.1 %collective-permute-start.6 = (bf16[4,144,128]{2,1,0:T(8,128)(2,1)}, bf16[4,144,128]{2,1,0:T(8,128)(2,1)S(1)}, u32[]{:S(2)}, u32[]{:S(2)}) collective-permute-start(bf16[4,144,128]{2,1,0:T(8,128)(2,1)} %get-tuple-element.31), channel_id=1, source_target_pairs={{0,16},{8,24},{16,0},{24,8},{1,25},{9,17},{17,9},{25,1},{2,18},{10... | collective-permute-start | bytes 442376 | tf_op jit(solution)/shard_map/ppermute | solution.py:225
  29.0 2.3 %collective-permute-start.7 = (bf16[4,144,128]{2,1,0:T(8,128)(2,1)}, bf16[4,144,128]{2,1,0:T(8,128)(2,1)S(1)}, u32[]{:S(2)}, u32[]{:S(2)}) collective-permute-start(bf16[4,144,128]{2,1,0:T(8,128)(2,1)} %copy-done.9), channel_id=1, source_target_pairs={{0,24},{8,16},{16,8},{24,0},{1,9},{9,1},{17,25},{25,17},{2,26},{10... | collective-permute-start | bytes 442376 | tf_op jit(solution)/shard_map/ppermute | solution.py:225
  31.3 0.9 %all-to-all-done.1.recv_ref.refs_0_ = bf16[4,4,64,128]{3,2,1,0:T(8,128)(2,1)S(1)} async-done(((bf16[4,4,64,128]{3,2,1,0:T(8,128)(2,1)}), bf16[4,4,64,128]{3,2,1,0:T(8,128)(2,1)S(1)}, u32[]{:S(2)}, u32[]{:S(2)}) %all-to-all-start.1) | async-done | bytes 262176 | tf_op jit(solution)/shard_map/all_to_all | solution.py:229
  32.3 2.2 %levels.1 = (f32[16,128]{1,0:T(8,128)}, f32[32,1,128]{2,1,0:T(1,128)}) custom-call(bf16[4,4,64,128]{3,2,1,0:T(8,128)(2,1)S(1)} %all-to-all-done.1.recv_ref.refs_0_, s32[8,512]{1,0:T(8,128)S(1)} %get-tuple-element.21.refs_0_.places_ref.refs_5_, bf16[8,8,512]{2,1,0:T(8,128)(2,1)S(1)} %copy-done.1, bf16[8,256,512]{2,1,0:T(8,128)(2,1)S(1)} %copy-done, ...), custom_call_target="tpu_custom_call" | custom-call | tf_op jit(solution)/shard_map/levels/pallas_call | solution.py:342
  34.5 3.2 %all-to-all-start.2 = ((f32[32,1,128]{2,1,0:T(1,128)}), f32[32,1,128]{2,1,0:T(1,128)S(1)}, u32[]{:S(2)}, u32[]{:S(2)}) async-start(f32[32,1,128]{2,1,0:T(1,128)} %get-tuple-element.34), calls=%async_computation.2 | async-start | bytes 32768 | tf_op jit(solution)/shard_map/all_to_all | solution.py:456
  37.7 0.0 collective-permute-done.5.refs_2_
  37.7 0.0 collective-permute-done.6.refs_3_
  37.7 1.3 %collective-permute-done.7.refs_4_ = bf16[4,144,128]{2,1,0:T(8,128)(2,1)S(1)} collective-permute-done((bf16[4,144,128]{2,1,0:T(8,128)(2,1)}, bf16[4,144,128]{2,1,0:T(8,128)(2,1)S(1)}, u32[]{:S(2)}, u32[]{:S(2)}) %collective-permute-start.7) | collective-permute-done | bytes 147488 | tf_op jit(solution)/shard_map/ppermute | solution.py:225
  39.0 5.3 %exposure.1 = (f32[192,2048]{1,0:T(8,128)}, f32[8,128]{1,0:T(8,128)S(1)}) custom-call(bf16[4,4,64,128]{3,2,1,0:T(8,128)(2,1)S(1)} %all-to-all-done.1.recv_ref.refs_0_, bf16[4,4,144,128]{3,2,1,0:T(8,128)(2,1)S(1)} %all-to-all-done.refs_1_, bf16[4,144,128]{2,1,0:T(8,128)(2,1)S(1)} %collective-permute-done.5.refs_2_, ...), custom_call_target="tpu_custom_call" | custom-call | tf_op jit(solution)/shard_map/exposure/pallas_call | solution.py:384
  44.3 0.5 %all-to-all-done.2.arrived_ref = f32[32,1,128]{2,1,0:T(1,128)S(1)} async-done(((f32[32,1,128]{2,1,0:T(1,128)}), f32[32,1,128]{2,1,0:T(1,128)S(1)}, u32[]{:S(2)}, u32[]{:S(2)}) %all-to-all-start.2) | async-done | bytes 16416 | tf_op jit(solution)/shard_map/all_to_all | solution.py:456
  44.8 0.9 %buildings.1 = f32[16,128]{1,0:T(8,128)} custom-call(f32[8,128]{1,0:T(8,128)S(1)} %get-tuple-element.33.after_ref, f32[32,1,128]{2,1,0:T(1,128)S(1)} %all-to-all-done.2.arrived_ref, s32[1,512]{1,0:T(1,128)S(1)} %get-tuple-element.35.building_ref), custom_call_target="tpu_custom_call" | custom-call | tf_op jit(solution)/shard_map/buildings/pallas_call | solution.py:423
  (17 shorter events, 0.0 us)
Async XLA Ops:
  0.6 31.6 %copy-start = (bf16[8,256,512]{2,1,0:T(8,128)(2,1)S(1)}, bf16[8,256,512]{2,1,0:T(8,128)(2,1)}, u32[]{:S(2)}) copy-start(bf16[8,256,512]{2,1,0:T(8,128)(2,1)} %refs_7_.1) | copy-start | bytes 6291460
  0.6 31.6 %copy-start.1 = (bf16[8,8,512]{2,1,0:T(8,128)(2,1)S(1)}, bf16[8,8,512]{2,1,0:T(8,128)(2,1)}, u32[]{:S(2)}) copy-start(bf16[8,8,512]{2,1,0:T(8,128)(2,1)} %refs_6_.1) | copy-start | bytes 196612
  0.7 3.8 %collective-permute-start = (bf16[192,512]{1,0:T(8,128)(2,1)}, bf16[192,512]{1,0:T(8,128)(2,1)S(1)}, u32[]{:S(2)}, u32[]{:S(2)}) collective-permute-start(bf16[192,512]{1,0:T(8,128)(2,1)} %bitcast.13), channel_id=1, source_target_pairs={{0,1},{1,0},{2,3},{3,2},{4,5},{5,4},{6,7},{7,6},{8,9},{9,8},{10,11... | collective-permute-start | bytes 589832 | tf_op jit(solution)/shard_map/ppermute | solution.py:448
  1.2 3.3 %collective-permute-start.1 = (s32[32,64]{1,0:T(8,128)}, s32[32,64]{1,0:T(8,128)S(1)}, u32[]{:S(2)}, u32[]{:S(2)}) collective-permute-start(s32[32,64]{1,0:T(8,128)} %bitcast.15), channel_id=1, source_target_pairs={{0,1},{1,0},{2,3},{3,2},{4,5},{5,4},{6,7},{7,6},{8,9},{9,8},{10,11... | collective-permute-start | bytes 24584 | tf_op jit(solution)/shard_map/ppermute | solution.py:449
  1.2 1.0 %copy-start.2 = (bf16[512,192]{0,1:T(8,128)(2,1)S(1)}, bf16[512,192]{0,1:T(8,128)(2,1)}, u32[]{:S(2)}) copy-start(bf16[512,192]{0,1:T(8,128)(2,1)} %param.9) | copy-start | bytes 589828
  2.2 0.7 %copy-start.3 = (s32[1,32,64]{2,1,0:T(8,128)S(1)}, s32[1,32,64]{2,1,0:T(8,128)}, u32[]{:S(2)}) copy-start(s32[1,32,64]{2,1,0:T(8,128)} %param.10) | copy-start | bytes 24580
  2.9 0.7 %copy-start.8 = (s32[24]{0:T(128)S(1)}, s32[24]{0:T(128)}, u32[]{:S(2)}) copy-start(s32[24]{0:T(128)} %param.14) | copy-start | bytes 292
  3.6 11.8 %copy-start.4 = (s32[8,512]{1,0:T(8,128)S(1)}, s32[8,512]{1,0:T(8,128)}, u32[]{:S(2)}) copy-start(s32[8,512]{1,0:T(8,128)} %slots_ref.1) | copy-start | bytes 49156
  3.6 11.8 %copy-start.5 = (s32[2048]{0:T(1024)S(1)}, s32[2048]{0:T(1024)}, u32[]{:S(2)}) copy-start(s32[2048]{0:T(1024)} %param.15) | copy-start | bytes 24580
  3.6 11.8 %copy-start.6 = (s32[1,32,16]{1,2,0:T(8,128)S(1)}, s32[1,32,16]{1,2,0:T(8,128)}, u32[]{:S(2)}) copy-start(s32[1,32,16]{1,2,0:T(8,128)} %param.16) | copy-start | bytes 6148
  3.6 11.8 %copy-start.7 = (s32[1,32,16]{1,2,0:T(8,128)S(1)}, s32[1,32,16]{1,2,0:T(8,128)}, u32[]{:S(2)}) copy-start(s32[1,32,16]{1,2,0:T(8,128)} %param.17) | copy-start | bytes 6148
  5.8 15.4 %all-to-all-start = ((bf16[4,4,144,128]{3,2,1,0:T(8,128)(2,1)}), bf16[4,4,144,128]{3,2,1,0:T(8,128)(2,1)S(1)}, u32[]{:S(2)}, u32[]{:S(2)}) async-start(bf16[4,4,144,128]{3,2,1,0:T(8,128)(2,1)} %get-tuple-element.22), calls=%async_computation | async-start | bytes 1179648 | tf_op jit(solution)/shard_map/all_to_all | solution.py:229
  11.0 4.7 %collective-permute-start.2 = (bf16[4,64,128]{2,1,0:T(8,128)(2,1)S(1)}, bf16[4,64,128]{2,1,0:T(8,128)(2,1)S(1)}, u32[]{:S(2)}, u32[]{:S(2)}) collective-permute-start(bf16[4,64,128]{2,1,0:T(8,128)(2,1)S(1)} %get-tuple-element.23), channel_id=1, source_target_pairs={{0,8},{8,0},{16,24},{24,16},{1,17},{9,25},{17,1},{25,9},{2,10},{10... | collective-permute-start | bytes 196616 | tf_op jit(solution)/shard_map/ppermute | solution.py:225
  12.6 7.0 %collective-permute-start.3 = (bf16[4,64,128]{2,1,0:T(8,128)(2,1)S(1)}, bf16[4,64,128]{2,1,0:T(8,128)(2,1)S(1)}, u32[]{:S(2)}, u32[]{:S(2)}) collective-permute-start(bf16[4,64,128]{2,1,0:T(8,128)(2,1)S(1)} %get-tuple-element.24), channel_id=1, source_target_pairs={{0,16},{8,24},{16,0},{24,8},{1,25},{9,17},{17,9},{25,1},{2,18},{10... | collective-permute-start | bytes 196616 | tf_op jit(solution)/shard_map/ppermute | solution.py:225
  15.2 6.1 %collective-permute-start.4 = (bf16[4,64,128]{2,1,0:T(8,128)(2,1)S(1)}, bf16[4,64,128]{2,1,0:T(8,128)(2,1)S(1)}, u32[]{:S(2)}, u32[]{:S(2)}) collective-permute-start(bf16[4,64,128]{2,1,0:T(8,128)(2,1)S(1)} %get-tuple-element.25), channel_id=1, source_target_pairs={{0,24},{8,16},{16,8},{24,0},{1,9},{9,1},{17,25},{25,17},{2,26},{10... | collective-permute-start | bytes 196616 | tf_op jit(solution)/shard_map/ppermute | solution.py:225
  22.7 4.2 %copy-start.9 = (bf16[4,144,128]{2,1,0:T(8,128)(2,1)}, bf16[4,144,128]{2,1,0:T(8,128)(2,1)S(1)}, u32[]{:S(2)}) copy-start(bf16[4,144,128]{2,1,0:T(8,128)(2,1)S(1)} %get-tuple-element.32) | copy-start | bytes 442372
  22.7 9.6 %all-to-all-start.1 = ((bf16[4,4,64,128]{3,2,1,0:T(8,128)(2,1)}), bf16[4,4,64,128]{3,2,1,0:T(8,128)(2,1)S(1)}, u32[]{:S(2)}, u32[]{:S(2)}) async-start(bf16[4,4,64,128]{3,2,1,0:T(8,128)(2,1)} %get-tuple-element.26), calls=%async_computation.1 | async-start | bytes 524288 | tf_op jit(solution)/shard_map/all_to_all | solution.py:229
  26.9 10.8 %collective-permute-start.5 = (bf16[4,144,128]{2,1,0:T(8,128)(2,1)}, bf16[4,144,128]{2,1,0:T(8,128)(2,1)S(1)}, u32[]{:S(2)}, u32[]{:S(2)}) collective-permute-start(bf16[4,144,128]{2,1,0:T(8,128)(2,1)} %get-tuple-element.30), channel_id=1, source_target_pairs={{0,8},{8,0},{16,24},{24,16},{1,17},{9,25},{17,1},{25,9},{2,10},{10... | collective-permute-start | bytes 442376 | tf_op jit(solution)/shard_map/ppermute | solution.py:225
  26.9 10.8 %collective-permute-start.6 = (bf16[4,144,128]{2,1,0:T(8,128)(2,1)}, bf16[4,144,128]{2,1,0:T(8,128)(2,1)S(1)}, u32[]{:S(2)}, u32[]{:S(2)}) collective-permute-start(bf16[4,144,128]{2,1,0:T(8,128)(2,1)} %get-tuple-element.31), channel_id=1, source_target_pairs={{0,16},{8,24},{16,0},{24,8},{1,25},{9,17},{17,9},{25,1},{2,18},{10... | collective-permute-start | bytes 442376 | tf_op jit(solution)/shard_map/ppermute | solution.py:225
  29.0 10.0 %collective-permute-start.7 = (bf16[4,144,128]{2,1,0:T(8,128)(2,1)}, bf16[4,144,128]{2,1,0:T(8,128)(2,1)S(1)}, u32[]{:S(2)}, u32[]{:S(2)}) collective-permute-start(bf16[4,144,128]{2,1,0:T(8,128)(2,1)} %copy-done.9), channel_id=1, source_target_pairs={{0,24},{8,16},{16,8},{24,0},{1,9},{9,1},{17,25},{25,17},{2,26},{10... | collective-permute-start | bytes 442376 | tf_op jit(solution)/shard_map/ppermute | solution.py:225
  34.5 10.4 %all-to-all-start.2 = ((f32[32,1,128]{2,1,0:T(1,128)}), f32[32,1,128]{2,1,0:T(1,128)S(1)}, u32[]{:S(2)}, u32[]{:S(2)}) async-start(f32[32,1,128]{2,1,0:T(1,128)} %get-tuple-element.34), calls=%async_computation.2 | async-start | bytes 32768 | tf_op jit(solution)/shard_map/all_to_all | solution.py:456

commit v3 on v2

--- a/solution.py
+++ b/solution.py
@@ -96,11 +96,6 @@
     return first * HOURS + 2 * BANDS, (last - first) * HOURS
 
 
-def extend_order(emission, sums):
-    cut = CHUNKS[0][1] * HOURS
-    return jnp.concatenate([emission[:cut], sums, emission[cut:]], axis=0)
-
-
 def turned_step(step):
     low, high = step & 1, (step >> 1) & 1
     return (step & ~3) | (((low ^ high) << 1) | high)
@@ -118,15 +113,14 @@
     return jnp.concatenate([list_ref[pl.ds(2 * (plane * QUAD + q) + band, 1), :] for q in order], axis=1)
 
 
-def own_kernel(period_hbm, emission_hbm, list_hbm, out_ref, period_ref, emission_ref, list_ref, sems):
-    pairs = ((list_hbm, list_ref), (period_hbm, period_ref), (emission_hbm, emission_ref))
+def own_kernel(emission_hbm, list_hbm, out_ref, emission_ref, list_ref, sems):
+    pairs = ((list_hbm, list_ref), (emission_hbm, emission_ref))
     copies = [pltpu.make_async_copy(src, dst, sems.at[i]) for i, (src, dst) in enumerate(pairs)]
     for copy in copies:
         copy.start()
     for copy in copies:
         copy.wait()
-    emission = emission_ref[...]
-    rows = extend_order(emission, band_sums(emission, hour_gains(period_ref[...])))
+    rows = emission_ref[...]
     for step in range(out_ref.shape[0]):
         found = bf(dot(rows, one_hot_columns(lists_of(list_ref, step, False), rows.shape[1])))
         for pair in range(QUAD // 2):
@@ -136,9 +130,9 @@
 def other_kernel(period_ref, emission_ref, list_ref, own_ref, *refs):
     planes = own_ref.shape[0]
     a_refs, (b_hbm, b_ref, sems) = refs[:planes], refs[planes:]
-    emission = emission_ref[...]
-    rows = extend_order(emission, band_sums(emission, hour_gains(period_ref[...])))
-    (start_a, count_a), (start_b, count_b) = chunk_rows(0), chunk_rows(1)
+    rows = emission_ref[...]
+    gains = hour_gains(period_ref[...])
+    cut = CHUNKS[0][1] * HOURS
     copies = []
     for step in range(planes):
         found = bf(dot(rows, one_hot_columns(lists_of(list_ref, step, True), rows.shape[1])))
@@ -147,8 +141,8 @@
             own = own_ref[step, pair]
             for odd, block in ((0, merge(own, other)), (1, merge(other, own))):
                 q = 2 * pair + odd
-                a_refs[step][q] = block[start_a : start_a + count_a]
-                b_ref[q, step] = block[start_b : start_b + count_b]
+                a_refs[step][q] = jnp.concatenate([block[:cut], band_sums(block, gains)], axis=0)
+                b_ref[q, step] = block[cut:]
         copy = pltpu.make_async_copy(b_ref.at[:, step], b_hbm.at[:, step], sems.at[step])
         copy.start()
         copies.append(copy)
@@ -156,18 +150,16 @@
         copy.wait()
 
 
-def make_sends(hour_period, emission_t, other_t, sends, other_sends, chips):
+def make_sends(period, emission_t, other_t, sends, other_sends, chips):
     width, segs = emission_t.shape
-    total = width + 2 * BANDS
     planes = chips // QUAD
-    period = hour_period.reshape(1, HOURS)
-    operands = [period, emission_t, sends]
+    operands = [emission_t, sends]
     own = pl.pallas_call(
         own_kernel,
-        in_specs=[HBM] * 3,
+        in_specs=[HBM] * 2,
         out_specs=VMEM,
-        out_shape=jax.ShapeDtypeStruct((planes, QUAD // 2, total, LANES), jnp.bfloat16),
-        scratch_shapes=[pltpu.VMEM(x.shape, x.dtype) for x in operands] + [pltpu.SemaphoreType.DMA((3,))],
+        out_shape=jax.ShapeDtypeStruct((planes, QUAD // 2, width, LANES), jnp.bfloat16),
+        scratch_shapes=[pltpu.VMEM(x.shape, x.dtype) for x in operands] + [pltpu.SemaphoreType.DMA((2,))],
         compiler_params=params(chips),
         name="own_rows",
     )(*operands)
@@ -447,7 +439,8 @@
     sends = path_sends[0]
     other_t = lax.ppermute(emission_t, "band", swap)
     other_sends = lax.ppermute(sends, "band", swap)
-    blocks_a, block_b = make_sends(hour_period, emission_t, other_t, sends, other_sends, chips)
+    period = lax.ppermute(hour_period.reshape(1, HOURS), "band", swap)
+    blocks_a, block_b = make_sends(period, emission_t, other_t, sends, other_sends, chips)
     places, dwell, addr, building = make_index(
         blocks_a[0], tile_slots, dwellings, addr_sends[0].T, addr_building[0].T, chips
     )

time: 46.1 us -> 46.1 us (level)
  local copies, waits for them, and re-layouts: 2.36 us -> 1.67 us
    unnamed x20 -> x18, local copies, waits for them, and re-layouts: 2.36 us -> 1.67 us
  transfers between devices with their start and end apart: 11 -> 12, of which waited for: 6 -> 6; matrix products, arithmetic and copies ran while one was open for 0% -> 0% of each run, Pallas kernels for 18% -> 18%
where the time goes in v3:
time: 46.1 us; the launch traced here: 45.6 us
  starting transfers between devices  22.4 us (49%)
  Pallas kernels  12.2 us (26%)
  waiting for transfers between devices  8.54 us (19%)
  local copies, waits for them, and re-layouts  1.67 us (4%)
  between operations  0.76 us (2%)
    all_to_all x2, starting transfers between devices, among_cells(): lax.all_to_all(array, 'cell', split_axis=0, concat_axis=0, tiled=True)  8.98 us
    ppermute x6, starting transfers between devices, along_planes(): lax.ppermute(block, ('plane', 'band'), pairs(step))  8.77 us
    ppermute x6, waiting for transfers between devices, along_planes(): lax.ppermute(block, ('plane', 'band'), pairs(step))  7.29 us
    pallas_call x1, Pallas kernels, make_exposure(): pl.pallas_call(functools.partial(exposure_kernel, chips // QUAD), in_spec...  5.32 us
    all_to_all x1, starting transfers between devices, local(): arrived = lax.all_to_all(pay, AXES, split_axis=0, concat_axis=0, tiled=True)  3.64 us
    pallas_call x1, Pallas kernels, make_levels(): pl.pallas_call(functools.partial(level_kernel, devices), in_specs=[VMEM]...  2.19 us
    unnamed x18, local copies, waits for them, and re-layouts  1.67 us
    pallas_call x1, Pallas kernels, make_sends(): pl.pallas_call(other_kernel, in_specs=[VMEM] * 4, out_specs=[VMEM] * plan...  1.5 us
  transfers between devices with their start and end apart: 12, of which 6 were waited for; matrix products, arithmetic and copies ran while one was open for 0% of the time, Pallas kernels for 18%

profile of v3, /device:TPU:0, one launch (start us, length us, event | category | flops | bytes accessed | tf_op | source)
XLA Modules:
  0.0 45.6 jit_solution(11240972896469679916)
XLA Ops:
  0.7 0.5 %collective-permute-start.1 = (bf16[192,512]{1,0:T(8,128)(2,1)}, bf16[192,512]{1,0:T(8,128)(2,1)S(1)}, u32[]{:S(2)}, u32[]{:S(2)}) collective-permute-start(bf16[192,512]{1,0:T(8,128)(2,1)} %bitcast.13), channel_id=1, source_target_pairs={{0,1},{1,0},{2,3},{3,2},{4,5},{5,4},{6,7},{7,6},{8,9},{9,8},{10,11... | collective-permute-start | bytes 589832 | tf_op jit(solution)/shard_map/ppermute | solution.py:440
  1.2 0.1 collective-permute-start.2
  1.2 0.4 collective-permute-start
  1.7 0.9 %copy-done.2 = bf16[512,192]{0,1:T(8,128)(2,1)S(1)} copy-done((bf16[512,192]{0,1:T(8,128)(2,1)S(1)}, bf16[512,192]{0,1:T(8,128)(2,1)}, u32[]{:S(2)}) %copy-start.2) | copy-done | bytes 196632
  2.6 0.7 %copy-done.3 = s32[1,32,64]{2,1,0:T(8,128)S(1)} copy-done((s32[1,32,64]{2,1,0:T(8,128)S(1)}, s32[1,32,64]{2,1,0:T(8,128)}, u32[]{:S(2)}) %copy-start.3) | copy-done | bytes 8216
  3.3 0.8 %own_rows.1.own_ref = bf16[4,2,192,128]{3,2,1,0:T(8,128)(2,1)S(1)} custom-call(bf16[192,512]{1,0:T(8,128)(2,1)S(1)} %bitcast.14, s32[32,64]{1,0:T(8,128)S(1)} %bitcast.16), custom_call_target="tpu_custom_call" | custom-call | tf_op jit(solution)/shard_map/own_rows/pallas_call | solution.py:157
  4.1 0.0 collective-permute-done.period_ref
  4.1 0.0 collective-permute-done.2.list_ref
  4.1 0.0 collective-permute-done.1.emission_ref
  4.1 1.5 %send_rows.1 = (bf16[4,64,128]{2,1,0:T(8,128)(2,1)S(1)}, bf16[4,64,128]{2,1,0:T(8,128)(2,1)S(1)}, bf16[4,64,128]{2,1,0:T(8,128)(2,1)S(1)}, bf16[4,64,128]{2,1,0:T(8,128)(2,1)S(1)}, bf16[4,4,144,128]{3,2,1,0:T(8,128)(2,1)}) custom-call(s32[1,24]{1,0:T(1,128)S(1)} %collective-permute-done.period_ref, bf16[192,512]{1,0:T(8,128)(2,1)S(1)} %collective-permute-done.1.emission_ref, ...), custom_call_target="tpu_custom_call" | custom-call | tf_op jit(solution)/shard_map/send_rows/pallas_call | solution.py:166
  5.6 4.8 %all-to-all-start = ((bf16[4,4,144,128]{3,2,1,0:T(8,128)(2,1)}), bf16[4,4,144,128]{3,2,1,0:T(8,128)(2,1)S(1)}, u32[]{:S(2)}, u32[]{:S(2)}) async-start(bf16[4,4,144,128]{3,2,1,0:T(8,128)(2,1)} %get-tuple-element.22), calls=%async_computation | async-start | bytes 1179648 | tf_op jit(solution)/shard_map/all_to_all | solution.py:221
  10.4 1.6 %collective-permute-start.3 = (bf16[4,64,128]{2,1,0:T(8,128)(2,1)S(1)}, bf16[4,64,128]{2,1,0:T(8,128)(2,1)S(1)}, u32[]{:S(2)}, u32[]{:S(2)}) collective-permute-start(bf16[4,64,128]{2,1,0:T(8,128)(2,1)S(1)} %get-tuple-element.23), channel_id=1, source_target_pairs={{0,8},{8,0},{16,24},{24,16},{1,17},{9,25},{17,1},{25,9},{2,10},{10... | collective-permute-start | bytes 196616 | tf_op jit(solution)/shard_map/ppermute | solution.py:217
  12.0 2.6 %collective-permute-start.4 = (bf16[4,64,128]{2,1,0:T(8,128)(2,1)S(1)}, bf16[4,64,128]{2,1,0:T(8,128)(2,1)S(1)}, u32[]{:S(2)}, u32[]{:S(2)}) collective-permute-start(bf16[4,64,128]{2,1,0:T(8,128)(2,1)S(1)} %get-tuple-element.24), channel_id=1, source_target_pairs={{0,16},{8,24},{16,0},{24,8},{1,25},{9,17},{17,9},{25,1},{2,18},{10... | collective-permute-start | bytes 196616 | tf_op jit(solution)/shard_map/ppermute | solution.py:217
  14.6 0.2 collective-permute-start.5
  14.8 0.1 index_rows.1
  14.9 0.5 %collective-permute-done.3.refs_3_ = bf16[4,64,128]{2,1,0:T(8,128)(2,1)S(1)} collective-permute-done((bf16[4,64,128]{2,1,0:T(8,128)(2,1)S(1)}, bf16[4,64,128]{2,1,0:T(8,128)(2,1)S(1)}, u32[]{:S(2)}, u32[]{:S(2)}) %collective-permute-start.3) | collective-permute-done | bytes 65568 | tf_op jit(solution)/shard_map/ppermute | solution.py:217
  15.4 3.7 %collective-permute-done.4.refs_4_ = bf16[4,64,128]{2,1,0:T(8,128)(2,1)S(1)} collective-permute-done((bf16[4,64,128]{2,1,0:T(8,128)(2,1)S(1)}, bf16[4,64,128]{2,1,0:T(8,128)(2,1)S(1)}, u32[]{:S(2)}, u32[]{:S(2)}) %collective-permute-start.4) | collective-permute-done | bytes 65568 | tf_op jit(solution)/shard_map/ppermute | solution.py:217
  19.1 1.6 %collective-permute-done.5.refs_5_ = bf16[4,64,128]{2,1,0:T(8,128)(2,1)S(1)} collective-permute-done((bf16[4,64,128]{2,1,0:T(8,128)(2,1)S(1)}, bf16[4,64,128]{2,1,0:T(8,128)(2,1)S(1)}, u32[]{:S(2)}, u32[]{:S(2)}) %collective-permute-start.5) | collective-permute-done | bytes 65568 | tf_op jit(solution)/shard_map/ppermute | solution.py:217
  20.7 0.0 all-to-all-done.refs_1_
  20.7 1.5 %regroup.1 = (bf16[4,4,64,128]{3,2,1,0:T(8,128)(2,1)}, bf16[4,144,128]{2,1,0:T(8,128)(2,1)}, bf16[4,144,128]{2,1,0:T(8,128)(2,1)}, bf16[4,144,128]{2,1,0:T(8,128)(2,1)S(1)}) custom-call(s32[8,512]{1,0:T(8,128)S(1)} %get-tuple-element.21.refs_0_.places_ref.refs_5_, bf16[4,4,144,128]{3,2,1,0:T(8,128)(2,1)S(1)} %all-to-all-done.refs_1_, ...), custom_call_target="tpu_custom_call" | custom-call | tf_op jit(solution)/shard_map/regroup/pallas_call | solution.py:198
  22.2 4.2 %all-to-all-start.1 = ((bf16[4,4,64,128]{3,2,1,0:T(8,128)(2,1)}), bf16[4,4,64,128]{3,2,1,0:T(8,128)(2,1)S(1)}, u32[]{:S(2)}, u32[]{:S(2)}) async-start(bf16[4,4,64,128]{3,2,1,0:T(8,128)(2,1)} %get-tuple-element.26), calls=%async_computation.1 | async-start | bytes 524288 | tf_op jit(solution)/shard_map/all_to_all | solution.py:221
  26.4 0.0 collective-permute-start.6
  26.4 2.6 %collective-permute-start.7 = (bf16[4,144,128]{2,1,0:T(8,128)(2,1)}, bf16[4,144,128]{2,1,0:T(8,128)(2,1)S(1)}, u32[]{:S(2)}, u32[]{:S(2)}) collective-permute-start(bf16[4,144,128]{2,1,0:T(8,128)(2,1)} %get-tuple-element.31), channel_id=1, source_target_pairs={{0,16},{8,24},{16,0},{24,8},{1,25},{9,17},{17,9},{25,1},{2,18},{10... | collective-permute-start | bytes 442376 | tf_op jit(solution)/shard_map/ppermute | solution.py:217
  28.9 1.8 %collective-permute-start.8 = (bf16[4,144,128]{2,1,0:T(8,128)(2,1)}, bf16[4,144,128]{2,1,0:T(8,128)(2,1)S(1)}, u32[]{:S(2)}, u32[]{:S(2)}) collective-permute-start(bf16[4,144,128]{2,1,0:T(8,128)(2,1)} %copy-done.8), channel_id=1, source_target_pairs={{0,24},{8,16},{16,8},{24,0},{1,9},{9,1},{17,25},{25,17},{2,26},{10... | collective-permute-start | bytes 442376 | tf_op jit(solution)/shard_map/ppermute | solution.py:217
  30.7 1.0 %all-to-all-done.1.recv_ref.refs_0_ = bf16[4,4,64,128]{3,2,1,0:T(8,128)(2,1)S(1)} async-done(((bf16[4,4,64,128]{3,2,1,0:T(8,128)(2,1)}), bf16[4,4,64,128]{3,2,1,0:T(8,128)(2,1)S(1)}, u32[]{:S(2)}, u32[]{:S(2)}) %all-to-all-start.1) | async-done | bytes 262176 | tf_op jit(solution)/shard_map/all_to_all | solution.py:221
  31.7 2.2 %levels.1 = (f32[16,128]{1,0:T(8,128)}, f32[32,1,128]{2,1,0:T(1,128)}) custom-call(bf16[4,4,64,128]{3,2,1,0:T(8,128)(2,1)S(1)} %all-to-all-done.1.recv_ref.refs_0_, s32[8,512]{1,0:T(8,128)S(1)} %get-tuple-element.21.refs_0_.places_ref.refs_5_, bf16[8,8,512]{2,1,0:T(8,128)(2,1)S(1)} %copy-done.1, bf16[8,256,512]{2,1,0:T(8,128)(2,1)S(1)} %copy-done, ...), custom_call_target="tpu_custom_call" | custom-call | tf_op jit(solution)/shard_map/levels/pallas_call | solution.py:334
  33.9 3.6 %all-to-all-start.2 = ((f32[32,1,128]{2,1,0:T(1,128)}), f32[32,1,128]{2,1,0:T(1,128)S(1)}, u32[]{:S(2)}, u32[]{:S(2)}) async-start(f32[32,1,128]{2,1,0:T(1,128)} %get-tuple-element.34), calls=%async_computation.2 | async-start | bytes 32768 | tf_op jit(solution)/shard_map/all_to_all | solution.py:449
  37.6 1.5 %collective-permute-done.7.refs_3_ = bf16[4,144,128]{2,1,0:T(8,128)(2,1)S(1)} collective-permute-done((bf16[4,144,128]{2,1,0:T(8,128)(2,1)}, bf16[4,144,128]{2,1,0:T(8,128)(2,1)S(1)}, u32[]{:S(2)}, u32[]{:S(2)}) %collective-permute-start.7) | collective-permute-done | bytes 147488 | tf_op jit(solution)/shard_map/ppermute | solution.py:217
  39.1 0.0 collective-permute-done.8.refs_4_
  39.1 5.3 %exposure.1 = (f32[192,2048]{1,0:T(8,128)}, f32[8,128]{1,0:T(8,128)S(1)}) custom-call(bf16[4,4,64,128]{3,2,1,0:T(8,128)(2,1)S(1)} %all-to-all-done.1.recv_ref.refs_0_, bf16[4,4,144,128]{3,2,1,0:T(8,128)(2,1)S(1)} %all-to-all-done.refs_1_, bf16[4,144,128]{2,1,0:T(8,128)(2,1)S(1)} %collective-permute-done.6.refs_2_, ...), custom_call_target="tpu_custom_call" | custom-call | tf_op jit(solution)/shard_map/exposure/pallas_call | solution.py:376
  44.4 0.3 all-to-all-done.2.arrived_ref
  44.7 0.9 %buildings.1 = f32[16,128]{1,0:T(8,128)} custom-call(f32[8,128]{1,0:T(8,128)S(1)} %get-tuple-element.33.after_ref, f32[32,1,128]{2,1,0:T(1,128)S(1)} %all-to-all-done.2.arrived_ref, s32[1,512]{1,0:T(1,128)S(1)} %get-tuple-element.35.building_ref), custom_call_target="tpu_custom_call" | custom-call | tf_op jit(solution)/shard_map/buildings/pallas_call | solution.py:415
  (17 shorter events, 0.0 us)
Async XLA Ops:
  0.6 31.1 %copy-start = (bf16[8,256,512]{2,1,0:T(8,128)(2,1)S(1)}, bf16[8,256,512]{2,1,0:T(8,128)(2,1)}, u32[]{:S(2)}) copy-start(bf16[8,256,512]{2,1,0:T(8,128)(2,1)} %refs_7_.1) | copy-start | bytes 6291460
  0.6 31.1 %copy-start.1 = (bf16[8,8,512]{2,1,0:T(8,128)(2,1)S(1)}, bf16[8,8,512]{2,1,0:T(8,128)(2,1)}, u32[]{:S(2)}) copy-start(bf16[8,8,512]{2,1,0:T(8,128)(2,1)} %refs_6_.1) | copy-start | bytes 196612
  0.7 3.5 %collective-permute-start.1 = (bf16[192,512]{1,0:T(8,128)(2,1)}, bf16[192,512]{1,0:T(8,128)(2,1)S(1)}, u32[]{:S(2)}, u32[]{:S(2)}) collective-permute-start(bf16[192,512]{1,0:T(8,128)(2,1)} %bitcast.13), channel_id=1, source_target_pairs={{0,1},{1,0},{2,3},{3,2},{4,5},{5,4},{6,7},{7,6},{8,9},{9,8},{10,11... | collective-permute-start | bytes 589832 | tf_op jit(solution)/shard_map/ppermute | solution.py:440
  1.2 3.0 %collective-permute-start.2 = (s32[32,64]{1,0:T(8,128)}, s32[32,64]{1,0:T(8,128)S(1)}, u32[]{:S(2)}, u32[]{:S(2)}) collective-permute-start(s32[32,64]{1,0:T(8,128)} %bitcast.15), channel_id=1, source_target_pairs={{0,1},{1,0},{2,3},{3,2},{4,5},{5,4},{6,7},{7,6},{8,9},{9,8},{10,11... | collective-permute-start | bytes 24584 | tf_op jit(solution)/shard_map/ppermute | solution.py:441
  1.2 2.9 %collective-permute-start = (s32[1,24]{1,0:T(1,128)}, s32[1,24]{1,0:T(1,128)S(1)}, u32[]{:S(2)}, u32[]{:S(2)}) collective-permute-start(s32[1,24]{1,0:T(1,128)} %bitcast.23), channel_id=1, source_target_pairs={{0,1},{1,0},{2,3},{3,2},{4,5},{5,4},{6,7},{7,6},{8,9},{9,8},{10,11... | collective-permute-start | bytes 296 | tf_op jit(solution)/shard_map/ppermute | solution.py:442
  1.7 0.9 %copy-start.2 = (bf16[512,192]{0,1:T(8,128)(2,1)S(1)}, bf16[512,192]{0,1:T(8,128)(2,1)}, u32[]{:S(2)}) copy-start(bf16[512,192]{0,1:T(8,128)(2,1)} %param.9) | copy-start | bytes 589828
  2.6 0.7 %copy-start.3 = (s32[1,32,64]{2,1,0:T(8,128)S(1)}, s32[1,32,64]{2,1,0:T(8,128)}, u32[]{:S(2)}) copy-start(s32[1,32,64]{2,1,0:T(8,128)} %param.10) | copy-start | bytes 24580
  3.3 11.5 %copy-start.4 = (s32[8,512]{1,0:T(8,128)S(1)}, s32[8,512]{1,0:T(8,128)}, u32[]{:S(2)}) copy-start(s32[8,512]{1,0:T(8,128)} %slots_ref.1) | copy-start | bytes 49156
  3.3 11.5 %copy-start.5 = (s32[2048]{0:T(1024)S(1)}, s32[2048]{0:T(1024)}, u32[]{:S(2)}) copy-start(s32[2048]{0:T(1024)} %param.15) | copy-start | bytes 24580
  3.3 11.5 %copy-start.6 = (s32[1,32,16]{1,2,0:T(8,128)S(1)}, s32[1,32,16]{1,2,0:T(8,128)}, u32[]{:S(2)}) copy-start(s32[1,32,16]{1,2,0:T(8,128)} %param.16) | copy-start | bytes 6148
  3.3 11.5 %copy-start.7 = (s32[1,32,16]{1,2,0:T(8,128)S(1)}, s32[1,32,16]{1,2,0:T(8,128)}, u32[]{:S(2)}) copy-start(s32[1,32,16]{1,2,0:T(8,128)} %param.17) | copy-start | bytes 6148
  5.6 15.1 %all-to-all-start = ((bf16[4,4,144,128]{3,2,1,0:T(8,128)(2,1)}), bf16[4,4,144,128]{3,2,1,0:T(8,128)(2,1)S(1)}, u32[]{:S(2)}, u32[]{:S(2)}) async-start(bf16[4,4,144,128]{3,2,1,0:T(8,128)(2,1)} %get-tuple-element.22), calls=%async_computation | async-start | bytes 1179648 | tf_op jit(solution)/shard_map/all_to_all | solution.py:221
  10.4 5.0 %collective-permute-start.3 = (bf16[4,64,128]{2,1,0:T(8,128)(2,1)S(1)}, bf16[4,64,128]{2,1,0:T(8,128)(2,1)S(1)}, u32[]{:S(2)}, u32[]{:S(2)}) collective-permute-start(bf16[4,64,128]{2,1,0:T(8,128)(2,1)S(1)} %get-tuple-element.23), channel_id=1, source_target_pairs={{0,8},{8,0},{16,24},{24,16},{1,17},{9,25},{17,1},{25,9},{2,10},{10... | collective-permute-start | bytes 196616 | tf_op jit(solution)/shard_map/ppermute | solution.py:217
  12.0 7.1 %collective-permute-start.4 = (bf16[4,64,128]{2,1,0:T(8,128)(2,1)S(1)}, bf16[4,64,128]{2,1,0:T(8,128)(2,1)S(1)}, u32[]{:S(2)}, u32[]{:S(2)}) collective-permute-start(bf16[4,64,128]{2,1,0:T(8,128)(2,1)S(1)} %get-tuple-element.24), channel_id=1, source_target_pairs={{0,16},{8,24},{16,0},{24,8},{1,25},{9,17},{17,9},{25,1},{2,18},{10... | collective-permute-start | bytes 196616 | tf_op jit(solution)/shard_map/ppermute | solution.py:217
  14.6 6.1 %collective-permute-start.5 = (bf16[4,64,128]{2,1,0:T(8,128)(2,1)S(1)}, bf16[4,64,128]{2,1,0:T(8,128)(2,1)S(1)}, u32[]{:S(2)}, u32[]{:S(2)}) collective-permute-start(bf16[4,64,128]{2,1,0:T(8,128)(2,1)S(1)} %get-tuple-element.25), channel_id=1, source_target_pairs={{0,24},{8,16},{16,8},{24,0},{1,9},{9,1},{17,25},{25,17},{2,26},{10... | collective-permute-start | bytes 196616 | tf_op jit(solution)/shard_map/ppermute | solution.py:217
  22.2 4.2 %copy-start.8 = (bf16[4,144,128]{2,1,0:T(8,128)(2,1)}, bf16[4,144,128]{2,1,0:T(8,128)(2,1)S(1)}, u32[]{:S(2)}) copy-start(bf16[4,144,128]{2,1,0:T(8,128)(2,1)S(1)} %get-tuple-element.32) | copy-start | bytes 442372
  22.2 9.6 %all-to-all-start.1 = ((bf16[4,4,64,128]{3,2,1,0:T(8,128)(2,1)}), bf16[4,4,64,128]{3,2,1,0:T(8,128)(2,1)S(1)}, u32[]{:S(2)}, u32[]{:S(2)}) async-start(bf16[4,4,64,128]{3,2,1,0:T(8,128)(2,1)} %get-tuple-element.26), calls=%async_computation.1 | async-start | bytes 524288 | tf_op jit(solution)/shard_map/all_to_all | solution.py:221
  26.4 11.2 %collective-permute-start.6 = (bf16[4,144,128]{2,1,0:T(8,128)(2,1)}, bf16[4,144,128]{2,1,0:T(8,128)(2,1)S(1)}, u32[]{:S(2)}, u32[]{:S(2)}) collective-permute-start(bf16[4,144,128]{2,1,0:T(8,128)(2,1)} %get-tuple-element.30), channel_id=1, source_target_pairs={{0,8},{8,0},{16,24},{24,16},{1,17},{9,25},{17,1},{25,9},{2,10},{10... | collective-permute-start | bytes 442376 | tf_op jit(solution)/shard_map/ppermute | solution.py:217
  26.4 12.7 %collective-permute-start.7 = (bf16[4,144,128]{2,1,0:T(8,128)(2,1)}, bf16[4,144,128]{2,1,0:T(8,128)(2,1)S(1)}, u32[]{:S(2)}, u32[]{:S(2)}) collective-permute-start(bf16[4,144,128]{2,1,0:T(8,128)(2,1)} %get-tuple-element.31), channel_id=1, source_target_pairs={{0,16},{8,24},{16,0},{24,8},{1,25},{9,17},{17,9},{25,1},{2,18},{10... | collective-permute-start | bytes 442376 | tf_op jit(solution)/shard_map/ppermute | solution.py:217
  28.9 10.2 %collective-permute-start.8 = (bf16[4,144,128]{2,1,0:T(8,128)(2,1)}, bf16[4,144,128]{2,1,0:T(8,128)(2,1)S(1)}, u32[]{:S(2)}, u32[]{:S(2)}) collective-permute-start(bf16[4,144,128]{2,1,0:T(8,128)(2,1)} %copy-done.8), channel_id=1, source_target_pairs={{0,24},{8,16},{16,8},{24,0},{1,9},{9,1},{17,25},{25,17},{2,26},{10... | collective-permute-start | bytes 442376 | tf_op jit(solution)/shard_map/ppermute | solution.py:217
  33.9 10.8 %all-to-all-start.2 = ((f32[32,1,128]{2,1,0:T(1,128)}), f32[32,1,128]{2,1,0:T(1,128)S(1)}, u32[]{:S(2)}, u32[]{:S(2)}) async-start(f32[32,1,128]{2,1,0:T(1,128)} %get-tuple-element.34), calls=%async_computation.2 | async-start | bytes 32768 | tf_op jit(solution)/shard_map/all_to_all | solution.py:449

commit v4 on v2

--- a/solution.py
+++ b/solution.py
@@ -112,7 +112,7 @@
 
 
 def lists_of(list_ref, step, swapped):
-    plane = lax.axis_index("plane") ^ jnp.where(lax.axis_index("band") == 0, step, turned_step(step))
+    plane = lax.axis_index("plane") ^ jnp.where(lax.axis_index("band") == 0, turned_step(step), turned_back(step))
     band = lax.axis_index("band")
     order = [q ^ 1 if swapped else q for q in range(QUAD)]
     return jnp.concatenate([list_ref[pl.ds(2 * (plane * QUAD + q) + band, 1), :] for q in order], axis=1)
@@ -188,17 +188,31 @@
 
 
 def regroup_kernel(planes, *refs):
-    b_ref = refs[1]
-    a_refs, a_hbm = refs[2 : planes + 2], refs[planes + 2]
-    b_outs, sems = refs[planes + 3 : -1], refs[-1]
-    copies = [pltpu.make_async_copy(ref, a_hbm.at[:, j], sems.at[j]) for j, ref in enumerate(a_refs)]
-    for copy in copies:
-        copy.start()
+    b_ref, a_refs = refs[1], refs[2 : planes + 2]
+    a_outs, b_outs = refs[planes + 2 : planes + 2 + QUAD], refs[planes + 2 + QUAD :]
+    cell = lax.axis_index("cell")
+    for i, out in enumerate(a_outs):
+        for j, ref in enumerate(a_refs):
+            out[j] = ref[cell ^ i]
     for j, out in enumerate(b_outs, 1):
         for q in range(QUAD):
             out[q] = b_ref[q, j]
-    for copy in copies:
-        copy.wait()
+
+
+def last_kernel(after_ref, b_ref, out_ref):
+    for q in range(QUAD):
+        out_ref[q] = b_ref[q, b_ref.shape[1] - 1]
+
+
+def last_blocks(after, block_b, chips):
+    return pl.pallas_call(
+        last_kernel,
+        in_specs=[VMEM] * 2,
+        out_specs=VMEM,
+        out_shape=jax.ShapeDtypeStruct((QUAD,) + block_b.shape[2:], jnp.bfloat16),
+        compiler_params=params(chips),
+        name="last_blocks",
+    )(after, block_b)
 
 
 def regroup(after, blocks_a, block_b, chips):
@@ -206,46 +220,50 @@
     outs = pl.pallas_call(
         functools.partial(regroup_kernel, planes),
         in_specs=[VMEM] * (2 + planes),
-        out_specs=[HBM] + [VMEM] * (planes - 1),
-        out_shape=[jax.ShapeDtypeStruct((QUAD, planes) + blocks_a[0].shape[1:], jnp.bfloat16)]
-        + [jax.ShapeDtypeStruct((QUAD,) + block_b.shape[2:], jnp.bfloat16)] * (planes - 1),
-        scratch_shapes=[pltpu.SemaphoreType.DMA((planes,))],
+        out_specs=[VMEM] * (QUAD + planes - 2),
+        out_shape=[jax.ShapeDtypeStruct((planes,) + blocks_a[0].shape[1:], jnp.bfloat16)] * QUAD
+        + [jax.ShapeDtypeStruct((QUAD,) + block_b.shape[2:], jnp.bfloat16)] * (planes - 2),
         compiler_params=params(chips),
         name="regroup",
     )(after, block_b, *blocks_a)
-    return outs[0], outs[1:]
-
-
-def along_planes(blocks):
-    planes = len(blocks) + 1
-
-    def pairs(step):
-        return [(2 * p + core, 2 * (p ^ own) + core) for core, own in enumerate((step, turned_step(step))) for p in range(planes)]
-
-    return [lax.ppermute(block, ("plane", "band"), pairs(step)) for step, block in enumerate(blocks, 1)]
+    return outs[:QUAD], outs[QUAD:]
+
+
+def along_plane(block, step, planes):
+    pairs = [
+        (2 * p + core, 2 * (p ^ own) + core)
+        for core, own in enumerate((turned_step(step), turned_back(step)))
+        for p in range(planes)
+    ]
+    return lax.ppermute(block, ("plane", "band"), pairs)
 
 
 def among_cells(array):
     return lax.all_to_all(array, "cell", split_axis=0, concat_axis=0, tiled=True)
 
 
+def to_cells(blocks):
+    return [blocks[0]] + [
+        lax.ppermute(blocks[i], "cell", [(q, q ^ i) for q in range(QUAD)]) for i in range(1, QUAD)
+    ]
+
+
 def exchange(blocks_a, block_b, chips, after):
+    planes = len(blocks_a)
     near_b = among_cells(block_b)
-    held_a = [blocks_a[0]] + along_planes(blocks_a[1:])
+    held_a = [blocks_a[0]] + [along_plane(blocks_a[step], step, planes) for step in range(1, planes)]
     grouped_a, grouped_b = regroup(after, held_a, near_b, chips)
-    return among_cells(grouped_a), [near_b] + along_planes(grouped_b)
+    far_b = [along_plane(block, step, planes) for step, block in enumerate(grouped_b, 1)]
+    return to_cells(grouped_a), [near_b] + far_b
 
 
 def slot_places(slots):
     half = (lax.axis_index("band") ^ (lax.axis_index("cell") & 1)) * HALF
     shift = (QUAD * LANES).bit_length() - 1
     place = slots ^ ((lax.axis_index("plane") << shift) + half)
-    turned = (turned_back(place >> shift) << shift) | (place & (QUAD * LANES - 1))
-    return jnp.where(lax.axis_index("band") == 0, place, turned)
-
-
-def blocks_of_first(ref):
-    return [ref.at[q, j] for j in range(ref.shape[1]) for q in range(QUAD)]
+    step = place >> shift
+    step = jnp.where(lax.axis_index("band") == 0, turned_back(step), turned_step(step))
+    return (step << shift) | (place & (QUAD * LANES - 1))
 
 
 def blocks_of_second(refs):
@@ -258,6 +276,17 @@
     for c, block in enumerate(blocks):
         g, j = divmod(c, per_group)
         table_ref[pl.ds(g * rows + first, count), j * LANES : (j + 1) * LANES] = block[start : start + count, :]
+
+
+def stack_steps(arrays, start, count, table_ref, first, rows):
+    cell = lax.axis_index("cell")
+    per_group = GROUP // LANES
+    for i, array in enumerate(arrays):
+        for j in range(array.shape[0]):
+            place = j * QUAD + (cell ^ i)
+            row = pl.multiple_of((place // per_group) * rows + first, 2 * BANDS)
+            lane = pl.multiple_of((place % per_group) * LANES, LANES)
+            table_ref[pl.ds(row, count), pl.ds(lane, LANES)] = array[j, start : start + count, :]
 
 
 def index_kernel(after_ref, slots_ref, dwell_ref, addr_ref, building_ref, places_out, dwell_out, addr_out, building_out):
@@ -294,12 +323,12 @@
     return out
 
 
-def level_kernel(devices, recv_ref, places_ref, absorption_ref, geometry_ref, dwell_ref, addr_ref, *refs):
-    level_ref, pay_ref, table = refs
-    blocks = blocks_of_first(recv_ref)
+def level_kernel(devices, *refs):
+    places_ref, absorption_ref, geometry_ref, dwell_ref, addr_ref, level_ref, pay_ref, done_ref, table = refs[QUAD:]
+    done_ref[...] = jnp.zeros_like(done_ref)
     tiles, recv_tile, paths = geometry_ref.shape
     rows = 2 * BANDS
-    stack_groups(blocks, blocks[0].shape[0] - rows, rows, table, 0, rows)
+    stack_steps(refs[:QUAD], refs[0].shape[1] - rows, rows, table, 0, rows)
     places = places_ref[...]
     per_tile = recv_tile // LANES
     zeros = jnp.zeros((5, paths), jnp.float32)
@@ -338,14 +367,15 @@
 def make_levels(recv, chips, places, absorption, geometry, dwell, addr):
     tiles, recv_tile, paths = geometry.shape
     devices = 2 * chips
-    operands = [recv, places, absorption, geometry, dwell, addr]
+    operands = [*recv, places, absorption, geometry, dwell, addr]
     return pl.pallas_call(
         functools.partial(level_kernel, devices),
         in_specs=[VMEM] * len(operands),
-        out_specs=[VMEM] * 2,
+        out_specs=[VMEM] * 3,
         out_shape=[
             jax.ShapeDtypeStruct(dwell.shape, jnp.float32),
             jax.ShapeDtypeStruct((devices, 1, LANES), jnp.float32),
+            jax.ShapeDtypeStruct((8, LANES), jnp.float32),
         ],
         scratch_shapes=[pltpu.VMEM((chips * LANES // GROUP * 2 * BANDS, GROUP), jnp.bfloat16)],
         compiler_params=params(chips),
@@ -354,12 +384,13 @@
 
 
 def exposure_kernel(planes, *refs):
-    places_ref, absorption_ref, geometry_ref, out_hbm, done_ref, table, out_ref, sems = refs[1 + planes :]
+    places_ref, absorption_ref, geometry_ref, out_hbm, done_ref, table, out_ref, sems = refs[QUAD + planes :]
     done_ref[...] = jnp.zeros_like(done_ref)
     tiles, recv_tile, paths = geometry_ref.shape
     rows = out_ref.shape[0]
-    for (first, last), blocks in zip(CHUNKS, (blocks_of_first(refs[0]), blocks_of_second(refs[1 : 1 + planes]))):
-        stack_groups(blocks, 0, (last - first) * HOURS, table, first * HOURS, rows)
+    (first_a, last_a), (first_b, last_b) = CHUNKS
+    stack_steps(refs[:QUAD], 0, (last_a - first_a) * HOURS, table, first_a * HOURS, rows)
+    stack_groups(blocks_of_second(refs[QUAD : QUAD + planes]), 0, (last_b - first_b) * HOURS, table, first_b * HOURS, rows)
     places = places_ref[...]
     copies = []
     for t in range(tiles):
@@ -380,7 +411,7 @@
 def make_exposure(moved, chips, places, absorption, geometry):
     tiles, recv_tile, paths = geometry.shape
     shape = (BANDS * HOURS, tiles * recv_tile)
-    operands = [moved[0], *moved[1], places, absorption, geometry]
+    operands = [*moved[0], *moved[1], places, absorption, geometry]
     return pl.pallas_call(
         functools.partial(exposure_kernel, chips // QUAD),
         in_specs=[VMEM] * len(operands),
@@ -452,7 +483,9 @@
         blocks_a[0], tile_slots, dwellings, addr_sends[0].T, addr_building[0].T, chips
     )
     moved = exchange(blocks_a, block_b, chips, places)
-    levels, pay = make_levels(moved[0], chips, places, absorption, geometry, dwell, addr)
+    levels, pay, ready = make_levels(moved[0], chips, places, absorption, geometry, dwell, addr)
+    planes = chips // QUAD
+    moved[1].append(along_plane(last_blocks(ready, moved[1][0], chips), planes - 1, planes))
     arrived = lax.all_to_all(pay, AXES, split_axis=0, concat_axis=0, tiled=True)
     exposure_t, done = make_exposure(moved, chips, places, absorption, geometry)
     buildings = make_buildings(done, arrived, building, chips)

time: 46.1 us -> 46 us (level)
  starting transfers between devices: 22 us -> 21.5 us
    all_to_all x2 -> x1, starting transfers between devices: 9.38 us -> 5.17 us  [among_cells(): lax.all_to_all(array, 'cell', split_axis=0, concat_axis=0, tiled=True)]
    ppermute x6 -> x9, starting transfers between devices: 8.8 us -> 12.1 us  [the longest x6 8.62 us: along_plane(): return lax.ppermute(block, ('plane', 'band'), pairs)]
    ppermute x6 -> x9, waiting for transfers between devices: 7.04 us -> 8.08 us  [the longest x6 6.78 us: along_plane(): return lax.ppermute(block, ('plane', 'band'), pairs)]
    pallas_call x1, Pallas kernels: 5.32 us -> 6.31 us  [make_exposure(): pl.pallas_call(functools.partial(exposure_kernel, chips // QUAD), in_spec...]
    all_to_all x2 -> x1, waiting for transfers between devices: 0.95 us -> 0.01 us  [among_cells(): lax.all_to_all(array, 'cell', split_axis=0, concat_axis=0, tiled=True)]
    pallas_call x1, Pallas kernels: 1.45 us -> 0.75 us  [regroup(): pl.pallas_call(functools.partial(regroup_kernel, planes), in_specs=[VMEM]...]
    all_to_all x1, waiting for transfers between devices: 0.49 us -> 0.01 us  [local(): arrived = lax.all_to_all(pay, AXES, split_axis=0, concat_axis=0, tiled=True)]
    unnamed x20 -> x18, local copies, waits for them, and re-layouts: 2.36 us -> 2.37 us
  transfers between devices with their start and end apart: 11 -> 13, of which waited for: 6 -> 4; matrix products, arithmetic and copies ran while one was open for 0% -> 0% of each run, Pallas kernels for 18% -> 21%
where the time goes in v4:
time: 46 us; the launch traced here: 45.2 us
  starting transfers between devices  21.5 us (47%)
  Pallas kernels  12.5 us (27%)
  waiting for transfers between devices  8.09 us (18%)
  local copies, waits for them, and re-layouts  2.37 us (5%)
  between operations  0.75 us (2%)
    ppermute x6, starting transfers between devices, along_plane(): return lax.ppermute(block, ('plane', 'band'), pairs)  8.62 us
    ppermute x6, waiting for transfers between devices, along_plane(): return lax.ppermute(block, ('plane', 'band'), pairs)  6.78 us
    pallas_call x1, Pallas kernels, make_exposure(): pl.pallas_call(functools.partial(exposure_kernel, chips // QUAD), in_spec...  6.31 us
    all_to_all x1, starting transfers between devices, among_cells(): lax.all_to_all(array, 'cell', split_axis=0, concat_axis=0, tiled=True)  5.17 us
    all_to_all x1, starting transfers between devices, local(): arrived = lax.all_to_all(pay, AXES, split_axis=0, concat_axis=0, tiled=True)  3.59 us
    ppermute x3, starting transfers between devices, to_cells(): lax.ppermute(blocks[i], 'cell', [(q, q ^ i) for q in range(QUAD)])  3.49 us
    unnamed x18, local copies, waits for them, and re-layouts  2.37 us
    pallas_call x1, Pallas kernels, make_levels(): pl.pallas_call(functools.partial(level_kernel, devices), in_specs=[VMEM]...  2.27 us
  transfers between devices with their start and end apart: 13, of which 4 were waited for; matrix products, arithmetic and copies ran while one was open for 0% of the time, Pallas kernels for 21%

profile of v4, /device:TPU:0, one launch (start us, length us, event | category | flops | bytes accessed | tf_op | source)
XLA Modules:
  0.0 45.2 jit_solution(10295126941721308138)
XLA Ops:
  0.7 0.5 %collective-permute-start = (bf16[192,512]{1,0:T(8,128)(2,1)}, bf16[192,512]{1,0:T(8,128)(2,1)S(1)}, u32[]{:S(2)}, u32[]{:S(2)}) collective-permute-start(bf16[192,512]{1,0:T(8,128)(2,1)} %bitcast.13), channel_id=1, source_target_pairs={{0,1},{1,0},{2,3},{3,2},{4,5},{5,4},{6,7},{7,6},{8,9},{9,8},{10,11... | collective-permute-start | bytes 589832 | tf_op jit(solution)/shard_map/ppermute | solution.py:479
  1.2 0.1 collective-permute-start.1
  1.3 1.0 %copy-done.2 = bf16[512,192]{0,1:T(8,128)(2,1)S(1)} copy-done((bf16[512,192]{0,1:T(8,128)(2,1)S(1)}, bf16[512,192]{0,1:T(8,128)(2,1)}, u32[]{:S(2)}) %copy-start.2) | copy-done | bytes 196632
  2.2 0.7 %copy-done.3 = s32[1,32,64]{2,1,0:T(8,128)S(1)} copy-done((s32[1,32,64]{2,1,0:T(8,128)S(1)}, s32[1,32,64]{2,1,0:T(8,128)}, u32[]{:S(2)}) %copy-start.3) | copy-done | bytes 8216
  2.9 0.7 %copy-done.8 = s32[24]{0:T(128)S(1)} copy-done((s32[24]{0:T(128)S(1)}, s32[24]{0:T(128)}, u32[]{:S(2)}) %copy-start.8) | copy-done | bytes 120
  3.6 0.9 %own_rows.1.own_ref = bf16[4,2,208,128]{3,2,1,0:T(8,128)(2,1)S(1)} custom-call(s32[1,24]{1,0:T(1,128)S(1)} %bitcast.20, bf16[192,512]{1,0:T(8,128)(2,1)S(1)} %bitcast.14, s32[32,64]{1,0:T(8,128)S(1)} %bitcast.16), custom_call_target="tpu_custom_call" | custom-call | tf_op jit(solution)/shard_map/own_rows/pallas_call | solution.py:165
  4.5 0.0 collective-permute-done.1.list_ref
  4.5 0.0 collective-permute-done.emission_ref
  4.5 1.3 %send_rows.1 = (bf16[4,64,128]{2,1,0:T(8,128)(2,1)S(1)}, bf16[4,64,128]{2,1,0:T(8,128)(2,1)S(1)}, bf16[4,64,128]{2,1,0:T(8,128)(2,1)S(1)}, bf16[4,64,128]{2,1,0:T(8,128)(2,1)S(1)}, bf16[4,4,144,128]{3,2,1,0:T(8,128)(2,1)}) custom-call(s32[1,24]{1,0:T(1,128)S(1)} %bitcast.21, bf16[192,512]{1,0:T(8,128)(2,1)S(1)} %collective-permute-done.emission_ref, ...), custom_call_target="tpu_custom_call" | custom-call | tf_op jit(solution)/shard_map/send_rows/pallas_call | solution.py:174
  5.8 5.2 %all-to-all-start = ((bf16[4,4,144,128]{3,2,1,0:T(8,128)(2,1)}), bf16[4,4,144,128]{3,2,1,0:T(8,128)(2,1)S(1)}, u32[]{:S(2)}, u32[]{:S(2)}) async-start(bf16[4,4,144,128]{3,2,1,0:T(8,128)(2,1)} %get-tuple-element.25), calls=%async_computation | async-start | bytes 1179648 | tf_op jit(solution)/shard_map/all_to_all | solution.py:242
  11.0 2.6 %collective-permute-start.2 = (bf16[4,64,128]{2,1,0:T(8,128)(2,1)S(1)}, bf16[4,64,128]{2,1,0:T(8,128)(2,1)S(1)}, u32[]{:S(2)}, u32[]{:S(2)}) collective-permute-start(bf16[4,64,128]{2,1,0:T(8,128)(2,1)S(1)} %get-tuple-element.26), channel_id=1, source_target_pairs={{0,16},{8,24},{16,0},{24,8},{1,25},{9,17},{17,9},{25,1},{2,18},{10... | collective-permute-start | bytes 196616 | tf_op jit(solution)/shard_map/ppermute | solution.py:238
  13.6 1.4 %collective-permute-start.3 = (bf16[4,64,128]{2,1,0:T(8,128)(2,1)S(1)}, bf16[4,64,128]{2,1,0:T(8,128)(2,1)S(1)}, u32[]{:S(2)}, u32[]{:S(2)}) collective-permute-start(bf16[4,64,128]{2,1,0:T(8,128)(2,1)S(1)} %get-tuple-element.27), channel_id=1, source_target_pairs={{0,24},{8,16},{16,8},{24,0},{1,9},{9,1},{17,25},{25,17},{2,26},{10... | collective-permute-start | bytes 196616 | tf_op jit(solution)/shard_map/ppermute | solution.py:238
  14.9 0.2 collective-permute-start.4
  15.2 0.1 index_rows.1
  15.3 1.6 %collective-permute-done.2.refs_3_ = bf16[4,64,128]{2,1,0:T(8,128)(2,1)S(1)} collective-permute-done((bf16[4,64,128]{2,1,0:T(8,128)(2,1)S(1)}, bf16[4,64,128]{2,1,0:T(8,128)(2,1)S(1)}, u32[]{:S(2)}, u32[]{:S(2)}) %collective-permute-start.2) | collective-permute-done | bytes 65568 | tf_op jit(solution)/shard_map/ppermute | solution.py:238
  16.9 3.4 %collective-permute-done.3.refs_4_ = bf16[4,64,128]{2,1,0:T(8,128)(2,1)S(1)} collective-permute-done((bf16[4,64,128]{2,1,0:T(8,128)(2,1)S(1)}, bf16[4,64,128]{2,1,0:T(8,128)(2,1)S(1)}, u32[]{:S(2)}, u32[]{:S(2)}) %collective-permute-start.3) | collective-permute-done | bytes 65568 | tf_op jit(solution)/shard_map/ppermute | solution.py:238
  20.3 0.0 collective-permute-done.4.refs_5_
  20.3 0.0 all-to-all-done.refs_1_.b_ref.refs_4_
  20.3 0.8 %regroup.1 = (bf16[4,64,128]{2,1,0:T(8,128)(2,1)S(1)}, bf16[4,64,128]{2,1,0:T(8,128)(2,1)S(1)}, bf16[4,64,128]{2,1,0:T(8,128)(2,1)S(1)}, bf16[4,64,128]{2,1,0:T(...) custom-call(s32[8,512]{1,0:T(8,128)S(1)} %get-tuple-element.24.refs_0_.refs_4_.refs_8_, ...), custom_call_target="tpu_custom_call" | custom-call | tf_op jit(solution)/shard_map/regroup/pallas_call | solution.py:220
  21.1 1.6 %collective-permute-start.5 = (bf16[4,64,128]{2,1,0:T(8,128)(2,1)S(1)}, bf16[4,64,128]{2,1,0:T(8,128)(2,1)S(1)}, u32[]{:S(2)}, u32[]{:S(2)}) collective-permute-start(bf16[4,64,128]{2,1,0:T(8,128)(2,1)S(1)} %get-tuple-element.30), channel_id=1, source_target_pairs={{0,2},{2,0},{4,6},{6,4},{1,3},{3,1},{5,7},{7,5},{8,10},{10,8},{12,... | collective-permute-start | bytes 196616 | tf_op jit(solution)/shard_map/ppermute | solution.py:247
  22.7 1.5 %collective-permute-start.6 = (bf16[4,64,128]{2,1,0:T(8,128)(2,1)S(1)}, bf16[4,64,128]{2,1,0:T(8,128)(2,1)S(1)}, u32[]{:S(2)}, u32[]{:S(2)}) collective-permute-start(bf16[4,64,128]{2,1,0:T(8,128)(2,1)S(1)} %get-tuple-element.31), channel_id=1, source_target_pairs={{0,4},{2,6},{4,0},{6,2},{1,5},{3,7},{5,1},{7,3},{8,12},{10,14},{12... | collective-permute-start | bytes 196616 | tf_op jit(solution)/shard_map/ppermute | solution.py:247
  24.2 0.4 collective-permute-start.7
  24.6 2.5 %collective-permute-start.8 = (bf16[4,144,128]{2,1,0:T(8,128)(2,1)}, bf16[4,144,128]{2,1,0:T(8,128)(2,1)S(1)}, u32[]{:S(2)}, u32[]{:S(2)}) collective-permute-start(bf16[4,144,128]{2,1,0:T(8,128)(2,1)} %get-tuple-element.36), channel_id=1, source_target_pairs={{0,16},{8,24},{16,0},{24,8},{1,25},{9,17},{17,9},{25,1},{2,18},{10... | collective-permute-start | bytes 442376 | tf_op jit(solution)/shard_map/ppermute | solution.py:238
  27.1 1.0 %collective-permute-start.9 = (bf16[4,144,128]{2,1,0:T(8,128)(2,1)}, bf16[4,144,128]{2,1,0:T(8,128)(2,1)S(1)}, u32[]{:S(2)}, u32[]{:S(2)}) collective-permute-start(bf16[4,144,128]{2,1,0:T(8,128)(2,1)} %get-tuple-element.37), channel_id=1, source_target_pairs={{0,24},{8,16},{16,8},{24,0},{1,9},{9,1},{17,25},{25,17},{2,26},{10... | collective-permute-start | bytes 442376 | tf_op jit(solution)/shard_map/ppermute | solution.py:238
  28.1 0.0 collective-permute-done.5.refs_1_
  28.1 1.3 %collective-permute-done.7.refs_3_ = bf16[4,64,128]{2,1,0:T(8,128)(2,1)S(1)} collective-permute-done((bf16[4,64,128]{2,1,0:T(8,128)(2,1)S(1)}, bf16[4,64,128]{2,1,0:T(8,128)(2,1)S(1)}, u32[]{:S(2)}, u32[]{:S(2)}) %collective-permute-start.7) | collective-permute-done | bytes 65568 | tf_op jit(solution)/shard_map/ppermute | solution.py:247
  29.4 2.3 %levels.1 = (f32[16,128]{1,0:T(8,128)}, f32[32,1,128]{2,1,0:T(1,128)}, f32[8,128]{1,0:T(8,128)S(1)}) custom-call(bf16[4,64,128]{2,1,0:T(8,128)(2,1)S(1)} %get-tuple-element.29.refs_0_, bf16[4,64,128]{2,1,0:T(8,128)(2,1)S(1)} %collective-permute-done.5.refs_1_, bf16[4,64,128]{2,1,0:T(8,128)(2,1)S(1)} %collective-permute-done.6.refs_2_, ...), custom_call_target="tpu_custom_call" | custom-call | tf_op jit(solution)/shard_map/levels/pallas_call | solution.py:371
  31.7 1.0 %collective-permute-start.10 = (bf16[4,144,128]{2,1,0:T(8,128)(2,1)S(1)}, bf16[4,144,128]{2,1,0:T(8,128)(2,1)}, u32[]{:S(2)}, u32[]{:S(2)}) collective-permute-start(bf16[4,144,128]{2,1,0:T(8,128)(2,1)S(1)} %last_blocks.1), channel_id=1, source_target_pairs={{0,8},{8,0},{16,24},{24,16},{1,17},{9,25},{17,1},{25,9},{2,10},{10... | collective-permute-start | bytes 442376 | tf_op jit(solution)/shard_map/ppermute | solution.py:238
  32.6 3.6 %all-to-all-start.1 = ((f32[32,1,128]{2,1,0:T(1,128)}), f32[32,1,128]{2,1,0:T(1,128)S(1)}, u32[]{:S(2)}, u32[]{:S(2)}) async-start(f32[32,1,128]{2,1,0:T(1,128)} %get-tuple-element.40), calls=%async_computation.1 | async-start | bytes 32768 | tf_op jit(solution)/shard_map/all_to_all | solution.py:489
  36.2 1.7 %collective-permute-done.10.refs_7_ = bf16[4,144,128]{2,1,0:T(8,128)(2,1)} collective-permute-done((bf16[4,144,128]{2,1,0:T(8,128)(2,1)S(1)}, bf16[4,144,128]{2,1,0:T(8,128)(2,1)}, u32[]{:S(2)}, u32[]{:S(2)}) %collective-permute-start.10) | collective-permute-done | bytes 147488 | tf_op jit(solution)/shard_map/ppermute | solution.py:238
  38.0 6.3 %exposure.1 = (f32[192,2048]{1,0:T(8,128)}, f32[8,128]{1,0:T(8,128)S(1)}) custom-call(bf16[4,64,128]{2,1,0:T(8,128)(2,1)S(1)} %get-tuple-element.29.refs_0_, bf16[4,64,128]{2,1,0:T(8,128)(2,1)S(1)} %collective-permute-done.5.refs_1_, bf16[4,64,128]{2,1,0:T(8,128)(2,1)S(1)} %collective-permute-done.6.refs_2_, ...), custom_call_target="tpu_custom_call" | custom-call | tf_op jit(solution)/shard_map/exposure/pallas_call | solution.py:415
  44.3 0.9 %buildings.1 = f32[16,128]{1,0:T(8,128)} custom-call(f32[8,128]{1,0:T(8,128)S(1)} %get-tuple-element.39.after_ref, f32[32,1,128]{2,1,0:T(1,128)S(1)} %all-to-all-done.1.arrived_ref, s32[1,512]{1,0:T(1,128)S(1)} %get-tuple-element.41.building_ref), custom_call_target="tpu_custom_call" | custom-call | tf_op jit(solution)/shard_map/buildings/pallas_call | solution.py:454
  (20 shorter events, 0.0 us)
Async XLA Ops:
  0.6 28.7 %copy-start.1 = (bf16[8,8,512]{2,1,0:T(8,128)(2,1)S(1)}, bf16[8,8,512]{2,1,0:T(8,128)(2,1)}, u32[]{:S(2)}) copy-start(bf16[8,8,512]{2,1,0:T(8,128)(2,1)} %refs_9_.1) | copy-start | bytes 196612
  0.6 28.7 %copy-start = (bf16[8,256,512]{2,1,0:T(8,128)(2,1)S(1)}, bf16[8,256,512]{2,1,0:T(8,128)(2,1)}, u32[]{:S(2)}) copy-start(bf16[8,256,512]{2,1,0:T(8,128)(2,1)} %refs_10_.1) | copy-start | bytes 6291460
  0.7 3.8 %collective-permute-start = (bf16[192,512]{1,0:T(8,128)(2,1)}, bf16[192,512]{1,0:T(8,128)(2,1)S(1)}, u32[]{:S(2)}, u32[]{:S(2)}) collective-permute-start(bf16[192,512]{1,0:T(8,128)(2,1)} %bitcast.13), channel_id=1, source_target_pairs={{0,1},{1,0},{2,3},{3,2},{4,5},{5,4},{6,7},{7,6},{8,9},{9,8},{10,11... | collective-permute-start | bytes 589832 | tf_op jit(solution)/shard_map/ppermute | solution.py:479
  1.2 3.3 %collective-permute-start.1 = (s32[32,64]{1,0:T(8,128)}, s32[32,64]{1,0:T(8,128)S(1)}, u32[]{:S(2)}, u32[]{:S(2)}) collective-permute-start(s32[32,64]{1,0:T(8,128)} %bitcast.15), channel_id=1, source_target_pairs={{0,1},{1,0},{2,3},{3,2},{4,5},{5,4},{6,7},{7,6},{8,9},{9,8},{10,11... | collective-permute-start | bytes 24584 | tf_op jit(solution)/shard_map/ppermute | solution.py:480
  1.2 1.0 %copy-start.2 = (bf16[512,192]{0,1:T(8,128)(2,1)S(1)}, bf16[512,192]{0,1:T(8,128)(2,1)}, u32[]{:S(2)}) copy-start(bf16[512,192]{0,1:T(8,128)(2,1)} %param.9) | copy-start | bytes 589828
  2.2 0.7 %copy-start.3 = (s32[1,32,64]{2,1,0:T(8,128)S(1)}, s32[1,32,64]{2,1,0:T(8,128)}, u32[]{:S(2)}) copy-start(s32[1,32,64]{2,1,0:T(8,128)} %param.10) | copy-start | bytes 24580
  2.9 0.7 %copy-start.8 = (s32[24]{0:T(128)S(1)}, s32[24]{0:T(128)}, u32[]{:S(2)}) copy-start(s32[24]{0:T(128)} %param.14) | copy-start | bytes 292
  3.6 11.6 %copy-start.4 = (s32[8,512]{1,0:T(8,128)S(1)}, s32[8,512]{1,0:T(8,128)}, u32[]{:S(2)}) copy-start(s32[8,512]{1,0:T(8,128)} %slots_ref.1) | copy-start | bytes 49156
  3.6 11.6 %copy-start.5 = (s32[2048]{0:T(1024)S(1)}, s32[2048]{0:T(1024)}, u32[]{:S(2)}) copy-start(s32[2048]{0:T(1024)} %param.15) | copy-start | bytes 24580
  3.6 11.6 %copy-start.6 = (s32[1,32,16]{1,2,0:T(8,128)S(1)}, s32[1,32,16]{1,2,0:T(8,128)}, u32[]{:S(2)}) copy-start(s32[1,32,16]{1,2,0:T(8,128)} %param.16) | copy-start | bytes 6148
  3.6 11.6 %copy-start.7 = (s32[1,32,16]{1,2,0:T(8,128)S(1)}, s32[1,32,16]{1,2,0:T(8,128)}, u32[]{:S(2)}) copy-start(s32[1,32,16]{1,2,0:T(8,128)} %param.17) | copy-start | bytes 6148
  5.8 14.5 %all-to-all-start = ((bf16[4,4,144,128]{3,2,1,0:T(8,128)(2,1)}), bf16[4,4,144,128]{3,2,1,0:T(8,128)(2,1)S(1)}, u32[]{:S(2)}, u32[]{:S(2)}) async-start(bf16[4,4,144,128]{3,2,1,0:T(8,128)(2,1)} %get-tuple-element.25), calls=%async_computation | async-start | bytes 1179648 | tf_op jit(solution)/shard_map/all_to_all | solution.py:242
  11.0 5.9 %collective-permute-start.2 = (bf16[4,64,128]{2,1,0:T(8,128)(2,1)S(1)}, bf16[4,64,128]{2,1,0:T(8,128)(2,1)S(1)}, u32[]{:S(2)}, u32[]{:S(2)}) collective-permute-start(bf16[4,64,128]{2,1,0:T(8,128)(2,1)S(1)} %get-tuple-element.26), channel_id=1, source_target_pairs={{0,16},{8,24},{16,0},{24,8},{1,25},{9,17},{17,9},{25,1},{2,18},{10... | collective-permute-start | bytes 196616 | tf_op jit(solution)/shard_map/ppermute | solution.py:238
  13.6 6.8 %collective-permute-start.3 = (bf16[4,64,128]{2,1,0:T(8,128)(2,1)S(1)}, bf16[4,64,128]{2,1,0:T(8,128)(2,1)S(1)}, u32[]{:S(2)}, u32[]{:S(2)}) collective-permute-start(bf16[4,64,128]{2,1,0:T(8,128)(2,1)S(1)} %get-tuple-element.27), channel_id=1, source_target_pairs={{0,24},{8,16},{16,8},{24,0},{1,9},{9,1},{17,25},{25,17},{2,26},{10... | collective-permute-start | bytes 196616 | tf_op jit(solution)/shard_map/ppermute | solution.py:238
  14.9 5.4 %collective-permute-start.4 = (bf16[4,64,128]{2,1,0:T(8,128)(2,1)S(1)}, bf16[4,64,128]{2,1,0:T(8,128)(2,1)S(1)}, u32[]{:S(2)}, u32[]{:S(2)}) collective-permute-start(bf16[4,64,128]{2,1,0:T(8,128)(2,1)S(1)} %get-tuple-element.28), channel_id=1, source_target_pairs={{0,8},{8,0},{16,24},{24,16},{1,17},{9,25},{17,1},{25,9},{2,10},{10... | collective-permute-start | bytes 196616 | tf_op jit(solution)/shard_map/ppermute | solution.py:238
  21.1 7.0 %collective-permute-start.5 = (bf16[4,64,128]{2,1,0:T(8,128)(2,1)S(1)}, bf16[4,64,128]{2,1,0:T(8,128)(2,1)S(1)}, u32[]{:S(2)}, u32[]{:S(2)}) collective-permute-start(bf16[4,64,128]{2,1,0:T(8,128)(2,1)S(1)} %get-tuple-element.30), channel_id=1, source_target_pairs={{0,2},{2,0},{4,6},{6,4},{1,3},{3,1},{5,7},{7,5},{8,10},{10,8},{12,... | collective-permute-start | bytes 196616 | tf_op jit(solution)/shard_map/ppermute | solution.py:247
  22.7 5.3 %collective-permute-start.6 = (bf16[4,64,128]{2,1,0:T(8,128)(2,1)S(1)}, bf16[4,64,128]{2,1,0:T(8,128)(2,1)S(1)}, u32[]{:S(2)}, u32[]{:S(2)}) collective-permute-start(bf16[4,64,128]{2,1,0:T(8,128)(2,1)S(1)} %get-tuple-element.31), channel_id=1, source_target_pairs={{0,4},{2,6},{4,0},{6,2},{1,5},{3,7},{5,1},{7,3},{8,12},{10,14},{12... | collective-permute-start | bytes 196616 | tf_op jit(solution)/shard_map/ppermute | solution.py:247
  24.2 5.2 %collective-permute-start.7 = (bf16[4,64,128]{2,1,0:T(8,128)(2,1)S(1)}, bf16[4,64,128]{2,1,0:T(8,128)(2,1)S(1)}, u32[]{:S(2)}, u32[]{:S(2)}) collective-permute-start(bf16[4,64,128]{2,1,0:T(8,128)(2,1)S(1)} %get-tuple-element.32), channel_id=1, source_target_pairs={{0,6},{2,4},{4,2},{6,0},{1,7},{3,5},{5,3},{7,1},{8,14},{10,12},{12... | collective-permute-start | bytes 196616 | tf_op jit(solution)/shard_map/ppermute | solution.py:247
  24.6 11.6 %collective-permute-start.8 = (bf16[4,144,128]{2,1,0:T(8,128)(2,1)}, bf16[4,144,128]{2,1,0:T(8,128)(2,1)S(1)}, u32[]{:S(2)}, u32[]{:S(2)}) collective-permute-start(bf16[4,144,128]{2,1,0:T(8,128)(2,1)} %get-tuple-element.36), channel_id=1, source_target_pairs={{0,16},{8,24},{16,0},{24,8},{1,25},{9,17},{17,9},{25,1},{2,18},{10... | collective-permute-start | bytes 442376 | tf_op jit(solution)/shard_map/ppermute | solution.py:238
  27.1 9.1 %collective-permute-start.9 = (bf16[4,144,128]{2,1,0:T(8,128)(2,1)}, bf16[4,144,128]{2,1,0:T(8,128)(2,1)S(1)}, u32[]{:S(2)}, u32[]{:S(2)}) collective-permute-start(bf16[4,144,128]{2,1,0:T(8,128)(2,1)} %get-tuple-element.37), channel_id=1, source_target_pairs={{0,24},{8,16},{16,8},{24,0},{1,9},{9,1},{17,25},{25,17},{2,26},{10... | collective-permute-start | bytes 442376 | tf_op jit(solution)/shard_map/ppermute | solution.py:238
  31.7 6.3 %collective-permute-start.10 = (bf16[4,144,128]{2,1,0:T(8,128)(2,1)S(1)}, bf16[4,144,128]{2,1,0:T(8,128)(2,1)}, u32[]{:S(2)}, u32[]{:S(2)}) collective-permute-start(bf16[4,144,128]{2,1,0:T(8,128)(2,1)S(1)} %last_blocks.1), channel_id=1, source_target_pairs={{0,8},{8,0},{16,24},{24,16},{1,17},{9,25},{17,1},{25,9},{2,10},{10... | collective-permute-start | bytes 442376 | tf_op jit(solution)/shard_map/ppermute | solution.py:238
  32.6 11.6 %all-to-all-start.1 = ((f32[32,1,128]{2,1,0:T(1,128)}), f32[32,1,128]{2,1,0:T(1,128)S(1)}, u32[]{:S(2)}, u32[]{:S(2)}) async-start(f32[32,1,128]{2,1,0:T(1,128)} %get-tuple-element.40), calls=%async_computation.1 | async-start | bytes 32768 | tf_op jit(solution)/shard_map/all_to_all | solution.py:489

commit v5 on v4

--- a/solution.py
+++ b/solution.py
@@ -271,9 +271,9 @@
     return [near.at[q, 0] for q in range(QUAD)] + [ref.at[q] for ref in far for q in range(QUAD)]
 
 
-def stack_groups(blocks, start, count, table_ref, first, rows):
+def stack_groups(blocks, start, count, table_ref, first, rows, skip=0):
     per_group = GROUP // LANES
-    for c, block in enumerate(blocks):
+    for c, block in enumerate(blocks[skip:], skip):
         g, j = divmod(c, per_group)
         table_ref[pl.ds(g * rows + first, count), j * LANES : (j + 1) * LANES] = block[start : start + count, :]
 
@@ -384,13 +384,19 @@
 
 
 def exposure_kernel(planes, *refs):
-    places_ref, absorption_ref, geometry_ref, out_hbm, done_ref, table, out_ref, sems = refs[QUAD + planes :]
+    places_ref, absorption_ref, geometry_ref, out_hbm, done_ref, table, out_ref, sems, last_ref, last_sem = refs[QUAD + planes :]
+    fetch = pltpu.make_async_copy(refs[QUAD + planes - 1], last_ref, last_sem)
+    fetch.start()
     done_ref[...] = jnp.zeros_like(done_ref)
     tiles, recv_tile, paths = geometry_ref.shape
     rows = out_ref.shape[0]
     (first_a, last_a), (first_b, last_b) = CHUNKS
     stack_steps(refs[:QUAD], 0, (last_a - first_a) * HOURS, table, first_a * HOURS, rows)
-    stack_groups(blocks_of_second(refs[QUAD : QUAD + planes]), 0, (last_b - first_b) * HOURS, table, first_b * HOURS, rows)
+    blocks = blocks_of_second([*refs[QUAD : QUAD + planes - 1], last_ref])
+    count = (last_b - first_b) * HOURS
+    stack_groups(blocks[:-QUAD], 0, count, table, first_b * HOURS, rows)
+    fetch.wait()
+    stack_groups(blocks, 0, count, table, first_b * HOURS, rows, skip=len(blocks) - QUAD)
     places = places_ref[...]
     copies = []
     for t in range(tiles):
@@ -414,13 +420,15 @@
     operands = [*moved[0], *moved[1], places, absorption, geometry]
     return pl.pallas_call(
         functools.partial(exposure_kernel, chips // QUAD),
-        in_specs=[VMEM] * len(operands),
+        in_specs=[VMEM] * (len(operands) - 4) + [HBM] + [VMEM] * 3,
         out_specs=[HBM, VMEM],
         out_shape=[jax.ShapeDtypeStruct(shape, jnp.float32), jax.ShapeDtypeStruct((8, LANES), jnp.float32)],
         scratch_shapes=[
             pltpu.VMEM((chips * LANES // GROUP * shape[0], GROUP), jnp.bfloat16),
             pltpu.VMEM(shape, jnp.float32),
             pltpu.SemaphoreType.DMA((tiles,)),
+            pltpu.VMEM(moved[1][-1].shape, jnp.bfloat16),
+            pltpu.SemaphoreType.DMA,
         ],
         compiler_params=params(chips),
         name="exposure",

time: 46 us -> 46 us (level)
  no operation moved by 1% of the time
where the time goes in v5:
time: 46 us; the launch traced here: 45.2 us
  starting transfers between devices  21.5 us (47%)
  Pallas kernels  12.6 us (27%)
  waiting for transfers between devices  8.09 us (18%)
  local copies, waits for them, and re-layouts  2.37 us (5%)
  between operations  0.75 us (2%)
    ppermute x6, starting transfers between devices, along_plane(): return lax.ppermute(block, ('plane', 'band'), pairs)  8.62 us
    ppermute x6, waiting for transfers between devices, along_plane(): return lax.ppermute(block, ('plane', 'band'), pairs)  6.78 us
    pallas_call x1, Pallas kernels, make_exposure(): pl.pallas_call(functools.partial(exposure_kernel, chips // QUAD), in_spec...  6.34 us
    all_to_all x1, starting transfers between devices, among_cells(): lax.all_to_all(array, 'cell', split_axis=0, concat_axis=0, tiled=True)  5.17 us
    all_to_all x1, starting transfers between devices, local(): arrived = lax.all_to_all(pay, AXES, split_axis=0, concat_axis=0, tiled=True)  3.59 us
    ppermute x3, starting transfers between devices, to_cells(): lax.ppermute(blocks[i], 'cell', [(q, q ^ i) for q in range(QUAD)])  3.49 us
    unnamed x18, local copies, waits for them, and re-layouts  2.37 us
    pallas_call x1, Pallas kernels, make_levels(): pl.pallas_call(functools.partial(level_kernel, devices), in_specs=[VMEM]...  2.27 us
  transfers between devices with their start and end apart: 13, of which 4 were waited for; matrix products, arithmetic and copies ran while one was open for 0% of the time, Pallas kernels for 21%

profile of v5, /device:TPU:0, one launch (start us, length us, event | category | flops | bytes accessed | tf_op | source)
XLA Modules:
  0.0 45.2 jit_solution(13795224474010490148)
XLA Ops:
  0.7 0.5 %collective-permute-start = (bf16[192,512]{1,0:T(8,128)(2,1)}, bf16[192,512]{1,0:T(8,128)(2,1)S(1)}, u32[]{:S(2)}, u32[]{:S(2)}) collective-permute-start(bf16[192,512]{1,0:T(8,128)(2,1)} %bitcast.13), channel_id=1, source_target_pairs={{0,1},{1,0},{2,3},{3,2},{4,5},{5,4},{6,7},{7,6},{8,9},{9,8},{10,11... | collective-permute-start | bytes 589832 | tf_op jit(solution)/shard_map/ppermute | solution.py:487
  1.2 0.1 collective-permute-start.1
  1.3 1.0 %copy-done.2 = bf16[512,192]{0,1:T(8,128)(2,1)S(1)} copy-done((bf16[512,192]{0,1:T(8,128)(2,1)S(1)}, bf16[512,192]{0,1:T(8,128)(2,1)}, u32[]{:S(2)}) %copy-start.2) | copy-done | bytes 196632
  2.2 0.7 %copy-done.3 = s32[1,32,64]{2,1,0:T(8,128)S(1)} copy-done((s32[1,32,64]{2,1,0:T(8,128)S(1)}, s32[1,32,64]{2,1,0:T(8,128)}, u32[]{:S(2)}) %copy-start.3) | copy-done | bytes 8216
  2.9 0.7 %copy-done.8 = s32[24]{0:T(128)S(1)} copy-done((s32[24]{0:T(128)S(1)}, s32[24]{0:T(128)}, u32[]{:S(2)}) %copy-start.8) | copy-done | bytes 120
  3.6 0.9 %own_rows.1.own_ref = bf16[4,2,208,128]{3,2,1,0:T(8,128)(2,1)S(1)} custom-call(s32[1,24]{1,0:T(1,128)S(1)} %bitcast.20, bf16[192,512]{1,0:T(8,128)(2,1)S(1)} %bitcast.14, s32[32,64]{1,0:T(8,128)S(1)} %bitcast.16), custom_call_target="tpu_custom_call" | custom-call | tf_op jit(solution)/shard_map/own_rows/pallas_call | solution.py:165
  4.5 0.0 collective-permute-done.1.list_ref
  4.5 0.0 collective-permute-done.emission_ref
  4.5 1.3 %send_rows.1 = (bf16[4,64,128]{2,1,0:T(8,128)(2,1)S(1)}, bf16[4,64,128]{2,1,0:T(8,128)(2,1)S(1)}, bf16[4,64,128]{2,1,0:T(8,128)(2,1)S(1)}, bf16[4,64,128]{2,1,0:T(8,128)(2,1)S(1)}, bf16[4,4,144,128]{3,2,1,0:T(8,128)(2,1)}) custom-call(s32[1,24]{1,0:T(1,128)S(1)} %bitcast.21, bf16[192,512]{1,0:T(8,128)(2,1)S(1)} %collective-permute-done.emission_ref, ...), custom_call_target="tpu_custom_call" | custom-call | tf_op jit(solution)/shard_map/send_rows/pallas_call | solution.py:174
  5.8 5.2 %all-to-all-start = ((bf16[4,4,144,128]{3,2,1,0:T(8,128)(2,1)}), bf16[4,4,144,128]{3,2,1,0:T(8,128)(2,1)S(1)}, u32[]{:S(2)}, u32[]{:S(2)}) async-start(bf16[4,4,144,128]{3,2,1,0:T(8,128)(2,1)} %get-tuple-element.25), calls=%async_computation | async-start | bytes 1179648 | tf_op jit(solution)/shard_map/all_to_all | solution.py:242
  11.0 2.6 %collective-permute-start.2 = (bf16[4,64,128]{2,1,0:T(8,128)(2,1)S(1)}, bf16[4,64,128]{2,1,0:T(8,128)(2,1)S(1)}, u32[]{:S(2)}, u32[]{:S(2)}) collective-permute-start(bf16[4,64,128]{2,1,0:T(8,128)(2,1)S(1)} %get-tuple-element.26), channel_id=1, source_target_pairs={{0,16},{8,24},{16,0},{24,8},{1,25},{9,17},{17,9},{25,1},{2,18},{10... | collective-permute-start | bytes 196616 | tf_op jit(solution)/shard_map/ppermute | solution.py:238
  13.6 1.4 %collective-permute-start.3 = (bf16[4,64,128]{2,1,0:T(8,128)(2,1)S(1)}, bf16[4,64,128]{2,1,0:T(8,128)(2,1)S(1)}, u32[]{:S(2)}, u32[]{:S(2)}) collective-permute-start(bf16[4,64,128]{2,1,0:T(8,128)(2,1)S(1)} %get-tuple-element.27), channel_id=1, source_target_pairs={{0,24},{8,16},{16,8},{24,0},{1,9},{9,1},{17,25},{25,17},{2,26},{10... | collective-permute-start | bytes 196616 | tf_op jit(solution)/shard_map/ppermute | solution.py:238
  14.9 0.2 collective-permute-start.4
  15.2 0.1 index_rows.1
  15.3 1.6 %collective-permute-done.2.refs_3_ = bf16[4,64,128]{2,1,0:T(8,128)(2,1)S(1)} collective-permute-done((bf16[4,64,128]{2,1,0:T(8,128)(2,1)S(1)}, bf16[4,64,128]{2,1,0:T(8,128)(2,1)S(1)}, u32[]{:S(2)}, u32[]{:S(2)}) %collective-permute-start.2) | collective-permute-done | bytes 65568 | tf_op jit(solution)/shard_map/ppermute | solution.py:238
  16.9 3.4 %collective-permute-done.3.refs_4_ = bf16[4,64,128]{2,1,0:T(8,128)(2,1)S(1)} collective-permute-done((bf16[4,64,128]{2,1,0:T(8,128)(2,1)S(1)}, bf16[4,64,128]{2,1,0:T(8,128)(2,1)S(1)}, u32[]{:S(2)}, u32[]{:S(2)}) %collective-permute-start.3) | collective-permute-done | bytes 65568 | tf_op jit(solution)/shard_map/ppermute | solution.py:238
  20.3 0.0 collective-permute-done.4.refs_5_
  20.3 0.0 all-to-all-done.refs_1_.b_ref.refs_4_
  20.3 0.8 %regroup.1 = (bf16[4,64,128]{2,1,0:T(8,128)(2,1)S(1)}, bf16[4,64,128]{2,1,0:T(8,128)(2,1)S(1)}, bf16[4,64,128]{2,1,0:T(8,128)(2,1)S(1)}, bf16[4,64,128]{2,1,0:T(...) custom-call(s32[8,512]{1,0:T(8,128)S(1)} %get-tuple-element.24.refs_0_.refs_4_.refs_8_, ...), custom_call_target="tpu_custom_call" | custom-call | tf_op jit(solution)/shard_map/regroup/pallas_call | solution.py:220
  21.1 1.6 %collective-permute-start.5 = (bf16[4,64,128]{2,1,0:T(8,128)(2,1)S(1)}, bf16[4,64,128]{2,1,0:T(8,128)(2,1)S(1)}, u32[]{:S(2)}, u32[]{:S(2)}) collective-permute-start(bf16[4,64,128]{2,1,0:T(8,128)(2,1)S(1)} %get-tuple-element.30), channel_id=1, source_target_pairs={{0,2},{2,0},{4,6},{6,4},{1,3},{3,1},{5,7},{7,5},{8,10},{10,8},{12,... | collective-permute-start | bytes 196616 | tf_op jit(solution)/shard_map/ppermute | solution.py:247
  22.7 1.5 %collective-permute-start.6 = (bf16[4,64,128]{2,1,0:T(8,128)(2,1)S(1)}, bf16[4,64,128]{2,1,0:T(8,128)(2,1)S(1)}, u32[]{:S(2)}, u32[]{:S(2)}) collective-permute-start(bf16[4,64,128]{2,1,0:T(8,128)(2,1)S(1)} %get-tuple-element.31), channel_id=1, source_target_pairs={{0,4},{2,6},{4,0},{6,2},{1,5},{3,7},{5,1},{7,3},{8,12},{10,14},{12... | collective-permute-start | bytes 196616 | tf_op jit(solution)/shard_map/ppermute | solution.py:247
  24.2 0.4 collective-permute-start.7
  24.6 2.5 %collective-permute-start.8 = (bf16[4,144,128]{2,1,0:T(8,128)(2,1)}, bf16[4,144,128]{2,1,0:T(8,128)(2,1)S(1)}, u32[]{:S(2)}, u32[]{:S(2)}) collective-permute-start(bf16[4,144,128]{2,1,0:T(8,128)(2,1)} %get-tuple-element.36), channel_id=1, source_target_pairs={{0,16},{8,24},{16,0},{24,8},{1,25},{9,17},{17,9},{25,1},{2,18},{10... | collective-permute-start | bytes 442376 | tf_op jit(solution)/shard_map/ppermute | solution.py:238
  27.1 1.0 %collective-permute-start.9 = (bf16[4,144,128]{2,1,0:T(8,128)(2,1)}, bf16[4,144,128]{2,1,0:T(8,128)(2,1)S(1)}, u32[]{:S(2)}, u32[]{:S(2)}) collective-permute-start(bf16[4,144,128]{2,1,0:T(8,128)(2,1)} %get-tuple-element.37), channel_id=1, source_target_pairs={{0,24},{8,16},{16,8},{24,0},{1,9},{9,1},{17,25},{25,17},{2,26},{10... | collective-permute-start | bytes 442376 | tf_op jit(solution)/shard_map/ppermute | solution.py:238
  28.1 0.0 collective-permute-done.5.refs_1_
  28.1 1.3 %collective-permute-done.7.refs_3_ = bf16[4,64,128]{2,1,0:T(8,128)(2,1)S(1)} collective-permute-done((bf16[4,64,128]{2,1,0:T(8,128)(2,1)S(1)}, bf16[4,64,128]{2,1,0:T(8,128)(2,1)S(1)}, u32[]{:S(2)}, u32[]{:S(2)}) %collective-permute-start.7) | collective-permute-done | bytes 65568 | tf_op jit(solution)/shard_map/ppermute | solution.py:247
  29.4 2.3 %levels.1 = (f32[16,128]{1,0:T(8,128)}, f32[32,1,128]{2,1,0:T(1,128)}, f32[8,128]{1,0:T(8,128)S(1)}) custom-call(bf16[4,64,128]{2,1,0:T(8,128)(2,1)S(1)} %get-tuple-element.29.refs_0_, bf16[4,64,128]{2,1,0:T(8,128)(2,1)S(1)} %collective-permute-done.5.refs_1_, bf16[4,64,128]{2,1,0:T(8,128)(2,1)S(1)} %collective-permute-done.6.refs_2_, ...), custom_call_target="tpu_custom_call" | custom-call | tf_op jit(solution)/shard_map/levels/pallas_call | solution.py:371
  31.7 1.0 %collective-permute-start.10 = (bf16[4,144,128]{2,1,0:T(8,128)(2,1)S(1)}, bf16[4,144,128]{2,1,0:T(8,128)(2,1)}, u32[]{:S(2)}, u32[]{:S(2)}) collective-permute-start(bf16[4,144,128]{2,1,0:T(8,128)(2,1)S(1)} %last_blocks.1), channel_id=1, source_target_pairs={{0,8},{8,0},{16,24},{24,16},{1,17},{9,25},{17,1},{25,9},{2,10},{10... | collective-permute-start | bytes 442376 | tf_op jit(solution)/shard_map/ppermute | solution.py:238
  32.6 3.6 %all-to-all-start.1 = ((f32[32,1,128]{2,1,0:T(1,128)}), f32[32,1,128]{2,1,0:T(1,128)S(1)}, u32[]{:S(2)}, u32[]{:S(2)}) async-start(f32[32,1,128]{2,1,0:T(1,128)} %get-tuple-element.40), calls=%async_computation.1 | async-start | bytes 32768 | tf_op jit(solution)/shard_map/all_to_all | solution.py:497
  36.2 1.7 %collective-permute-done.10.refs_7_ = bf16[4,144,128]{2,1,0:T(8,128)(2,1)} collective-permute-done((bf16[4,144,128]{2,1,0:T(8,128)(2,1)S(1)}, bf16[4,144,128]{2,1,0:T(8,128)(2,1)}, u32[]{:S(2)}, u32[]{:S(2)}) %collective-permute-start.10) | collective-permute-done | bytes 147488 | tf_op jit(solution)/shard_map/ppermute | solution.py:238
  38.0 6.3 %exposure.1 = (f32[192,2048]{1,0:T(8,128)}, f32[8,128]{1,0:T(8,128)S(1)}) custom-call(bf16[4,64,128]{2,1,0:T(8,128)(2,1)S(1)} %get-tuple-element.29.refs_0_, bf16[4,64,128]{2,1,0:T(8,128)(2,1)S(1)} %collective-permute-done.5.refs_1_, bf16[4,64,128]{2,1,0:T(8,128)(2,1)S(1)} %collective-permute-done.6.refs_2_, ...), custom_call_target="tpu_custom_call" | custom-call | tf_op jit(solution)/shard_map/exposure/pallas_call | solution.py:421
  44.3 0.9 %buildings.1 = f32[16,128]{1,0:T(8,128)} custom-call(f32[8,128]{1,0:T(8,128)S(1)} %get-tuple-element.39.after_ref, f32[32,1,128]{2,1,0:T(1,128)S(1)} %all-to-all-done.1.arrived_ref, s32[1,512]{1,0:T(1,128)S(1)} %get-tuple-element.41.building_ref), custom_call_target="tpu_custom_call" | custom-call | tf_op jit(solution)/shard_map/buildings/pallas_call | solution.py:462
  (20 shorter events, 0.0 us)
Async XLA Ops:
  0.6 28.7 %copy-start.1 = (bf16[8,8,512]{2,1,0:T(8,128)(2,1)S(1)}, bf16[8,8,512]{2,1,0:T(8,128)(2,1)}, u32[]{:S(2)}) copy-start(bf16[8,8,512]{2,1,0:T(8,128)(2,1)} %refs_9_.1) | copy-start | bytes 196612
  0.6 28.7 %copy-start = (bf16[8,256,512]{2,1,0:T(8,128)(2,1)S(1)}, bf16[8,256,512]{2,1,0:T(8,128)(2,1)}, u32[]{:S(2)}) copy-start(bf16[8,256,512]{2,1,0:T(8,128)(2,1)} %refs_10_.1) | copy-start | bytes 6291460
  0.7 3.8 %collective-permute-start = (bf16[192,512]{1,0:T(8,128)(2,1)}, bf16[192,512]{1,0:T(8,128)(2,1)S(1)}, u32[]{:S(2)}, u32[]{:S(2)}) collective-permute-start(bf16[192,512]{1,0:T(8,128)(2,1)} %bitcast.13), channel_id=1, source_target_pairs={{0,1},{1,0},{2,3},{3,2},{4,5},{5,4},{6,7},{7,6},{8,9},{9,8},{10,11... | collective-permute-start | bytes 589832 | tf_op jit(solution)/shard_map/ppermute | solution.py:487
  1.2 3.3 %collective-permute-start.1 = (s32[32,64]{1,0:T(8,128)}, s32[32,64]{1,0:T(8,128)S(1)}, u32[]{:S(2)}, u32[]{:S(2)}) collective-permute-start(s32[32,64]{1,0:T(8,128)} %bitcast.15), channel_id=1, source_target_pairs={{0,1},{1,0},{2,3},{3,2},{4,5},{5,4},{6,7},{7,6},{8,9},{9,8},{10,11... | collective-permute-start | bytes 24584 | tf_op jit(solution)/shard_map/ppermute | solution.py:488
  1.2 1.0 %copy-start.2 = (bf16[512,192]{0,1:T(8,128)(2,1)S(1)}, bf16[512,192]{0,1:T(8,128)(2,1)}, u32[]{:S(2)}) copy-start(bf16[512,192]{0,1:T(8,128)(2,1)} %param.9) | copy-start | bytes 589828
  2.2 0.7 %copy-start.3 = (s32[1,32,64]{2,1,0:T(8,128)S(1)}, s32[1,32,64]{2,1,0:T(8,128)}, u32[]{:S(2)}) copy-start(s32[1,32,64]{2,1,0:T(8,128)} %param.10) | copy-start | bytes 24580
  2.9 0.7 %copy-start.8 = (s32[24]{0:T(128)S(1)}, s32[24]{0:T(128)}, u32[]{:S(2)}) copy-start(s32[24]{0:T(128)} %param.14) | copy-start | bytes 292
  3.6 11.6 %copy-start.4 = (s32[8,512]{1,0:T(8,128)S(1)}, s32[8,512]{1,0:T(8,128)}, u32[]{:S(2)}) copy-start(s32[8,512]{1,0:T(8,128)} %slots_ref.1) | copy-start | bytes 49156
  3.6 11.6 %copy-start.5 = (s32[2048]{0:T(1024)S(1)}, s32[2048]{0:T(1024)}, u32[]{:S(2)}) copy-start(s32[2048]{0:T(1024)} %param.15) | copy-start | bytes 24580
  3.6 11.6 %copy-start.6 = (s32[1,32,16]{1,2,0:T(8,128)S(1)}, s32[1,32,16]{1,2,0:T(8,128)}, u32[]{:S(2)}) copy-start(s32[1,32,16]{1,2,0:T(8,128)} %param.16) | copy-start | bytes 6148
  3.6 11.6 %copy-start.7 = (s32[1,32,16]{1,2,0:T(8,128)S(1)}, s32[1,32,16]{1,2,0:T(8,128)}, u32[]{:S(2)}) copy-start(s32[1,32,16]{1,2,0:T(8,128)} %param.17) | copy-start | bytes 6148
  5.8 14.5 %all-to-all-start = ((bf16[4,4,144,128]{3,2,1,0:T(8,128)(2,1)}), bf16[4,4,144,128]{3,2,1,0:T(8,128)(2,1)S(1)}, u32[]{:S(2)}, u32[]{:S(2)}) async-start(bf16[4,4,144,128]{3,2,1,0:T(8,128)(2,1)} %get-tuple-element.25), calls=%async_computation | async-start | bytes 1179648 | tf_op jit(solution)/shard_map/all_to_all | solution.py:242
  11.0 5.9 %collective-permute-start.2 = (bf16[4,64,128]{2,1,0:T(8,128)(2,1)S(1)}, bf16[4,64,128]{2,1,0:T(8,128)(2,1)S(1)}, u32[]{:S(2)}, u32[]{:S(2)}) collective-permute-start(bf16[4,64,128]{2,1,0:T(8,128)(2,1)S(1)} %get-tuple-element.26), channel_id=1, source_target_pairs={{0,16},{8,24},{16,0},{24,8},{1,25},{9,17},{17,9},{25,1},{2,18},{10... | collective-permute-start | bytes 196616 | tf_op jit(solution)/shard_map/ppermute | solution.py:238
  13.6 6.8 %collective-permute-start.3 = (bf16[4,64,128]{2,1,0:T(8,128)(2,1)S(1)}, bf16[4,64,128]{2,1,0:T(8,128)(2,1)S(1)}, u32[]{:S(2)}, u32[]{:S(2)}) collective-permute-start(bf16[4,64,128]{2,1,0:T(8,128)(2,1)S(1)} %get-tuple-element.27), channel_id=1, source_target_pairs={{0,24},{8,16},{16,8},{24,0},{1,9},{9,1},{17,25},{25,17},{2,26},{10... | collective-permute-start | bytes 196616 | tf_op jit(solution)/shard_map/ppermute | solution.py:238
  14.9 5.4 %collective-permute-start.4 = (bf16[4,64,128]{2,1,0:T(8,128)(2,1)S(1)}, bf16[4,64,128]{2,1,0:T(8,128)(2,1)S(1)}, u32[]{:S(2)}, u32[]{:S(2)}) collective-permute-start(bf16[4,64,128]{2,1,0:T(8,128)(2,1)S(1)} %get-tuple-element.28), channel_id=1, source_target_pairs={{0,8},{8,0},{16,24},{24,16},{1,17},{9,25},{17,1},{25,9},{2,10},{10... | collective-permute-start | bytes 196616 | tf_op jit(solution)/shard_map/ppermute | solution.py:238
  21.1 7.0 %collective-permute-start.5 = (bf16[4,64,128]{2,1,0:T(8,128)(2,1)S(1)}, bf16[4,64,128]{2,1,0:T(8,128)(2,1)S(1)}, u32[]{:S(2)}, u32[]{:S(2)}) collective-permute-start(bf16[4,64,128]{2,1,0:T(8,128)(2,1)S(1)} %get-tuple-element.30), channel_id=1, source_target_pairs={{0,2},{2,0},{4,6},{6,4},{1,3},{3,1},{5,7},{7,5},{8,10},{10,8},{12,... | collective-permute-start | bytes 196616 | tf_op jit(solution)/shard_map/ppermute | solution.py:247
  22.7 5.3 %collective-permute-start.6 = (bf16[4,64,128]{2,1,0:T(8,128)(2,1)S(1)}, bf16[4,64,128]{2,1,0:T(8,128)(2,1)S(1)}, u32[]{:S(2)}, u32[]{:S(2)}) collective-permute-start(bf16[4,64,128]{2,1,0:T(8,128)(2,1)S(1)} %get-tuple-element.31), channel_id=1, source_target_pairs={{0,4},{2,6},{4,0},{6,2},{1,5},{3,7},{5,1},{7,3},{8,12},{10,14},{12... | collective-permute-start | bytes 196616 | tf_op jit(solution)/shard_map/ppermute | solution.py:247
  24.2 5.2 %collective-permute-start.7 = (bf16[4,64,128]{2,1,0:T(8,128)(2,1)S(1)}, bf16[4,64,128]{2,1,0:T(8,128)(2,1)S(1)}, u32[]{:S(2)}, u32[]{:S(2)}) collective-permute-start(bf16[4,64,128]{2,1,0:T(8,128)(2,1)S(1)} %get-tuple-element.32), channel_id=1, source_target_pairs={{0,6},{2,4},{4,2},{6,0},{1,7},{3,5},{5,3},{7,1},{8,14},{10,12},{12... | collective-permute-start | bytes 196616 | tf_op jit(solution)/shard_map/ppermute | solution.py:247
  24.6 11.6 %collective-permute-start.8 = (bf16[4,144,128]{2,1,0:T(8,128)(2,1)}, bf16[4,144,128]{2,1,0:T(8,128)(2,1)S(1)}, u32[]{:S(2)}, u32[]{:S(2)}) collective-permute-start(bf16[4,144,128]{2,1,0:T(8,128)(2,1)} %get-tuple-element.36), channel_id=1, source_target_pairs={{0,16},{8,24},{16,0},{24,8},{1,25},{9,17},{17,9},{25,1},{2,18},{10... | collective-permute-start | bytes 442376 | tf_op jit(solution)/shard_map/ppermute | solution.py:238
  27.1 9.1 %collective-permute-start.9 = (bf16[4,144,128]{2,1,0:T(8,128)(2,1)}, bf16[4,144,128]{2,1,0:T(8,128)(2,1)S(1)}, u32[]{:S(2)}, u32[]{:S(2)}) collective-permute-start(bf16[4,144,128]{2,1,0:T(8,128)(2,1)} %get-tuple-element.37), channel_id=1, source_target_pairs={{0,24},{8,16},{16,8},{24,0},{1,9},{9,1},{17,25},{25,17},{2,26},{10... | collective-permute-start | bytes 442376 | tf_op jit(solution)/shard_map/ppermute | solution.py:238
  31.7 6.3 %collective-permute-start.10 = (bf16[4,144,128]{2,1,0:T(8,128)(2,1)S(1)}, bf16[4,144,128]{2,1,0:T(8,128)(2,1)}, u32[]{:S(2)}, u32[]{:S(2)}) collective-permute-start(bf16[4,144,128]{2,1,0:T(8,128)(2,1)S(1)} %last_blocks.1), channel_id=1, source_target_pairs={{0,8},{8,0},{16,24},{24,16},{1,17},{9,25},{17,1},{25,9},{2,10},{10... | collective-permute-start | bytes 442376 | tf_op jit(solution)/shard_map/ppermute | solution.py:238
  32.6 11.7 %all-to-all-start.1 = ((f32[32,1,128]{2,1,0:T(1,128)}), f32[32,1,128]{2,1,0:T(1,128)S(1)}, u32[]{:S(2)}, u32[]{:S(2)}) async-start(f32[32,1,128]{2,1,0:T(1,128)} %get-tuple-element.40), calls=%async_computation.1 | async-start | bytes 32768 | tf_op jit(solution)/shard_map/all_to_all | solution.py:497
